TPU v7x, 128 devices: a whole 4x4x4 slice. The times are simulated.
128 devices in a mesh: gx: 4 (over z_hi, core), gy: 4 (over y), gz: 8 (over x, z_lo).
Axes of the slice: x: 4, y: 4, z: 4 (z_hi: 2, z_lo: 2; z = z_hi * 2 + z_lo), core: 2. Of those that a mesh axis runs over, the one named last changes fastest.
Arguments:
- cells: float32 [512, 5, 32, 1024], P(('gx', 'gy', 'gz')), may hold values from -4 to 16, as said below
- moves: int32 [128, 3, 2], replicated, may hold values from 0 to 3, as said below
- neighbours: int32 [64, 4], replicated, may hold values from 0 to 63, as said below
Outputs:
- updated: float32 [512, 5, 32, 1024], P(('gx', 'gy', 'gz'))
Inputs may be any that keep to these rules, and one draw needn't show every extreme that they name: `cells`: density is 0.25 or more and the pressure (5/3 - 1)(E - |m|^2 / (2 rho)) is 0.25 or more in every cell. `moves`: the 2 slots of one device in one round are distinct. Neighbour relations are mutual (the -x neighbour of a patch's +x neighbour is that patch, likewise for y); no patch neighbours itself; counted with sides, the patches of one device have at most 2 neighbour links to any one other device, and some pair of devices has exactly 2 in every draw.
All inputs are finite; a program needn't handle non-finite values.
Results may differ from a plain program's by a relative error of at most 0.0003.
Values sent between devices are 32-bit elements; how exact they have to be, the bound alone decides.
No kernel may reach another device: no remote copies, remote signals or barrier semaphores. Data moves between devices by JAX's collectives and lax.ppermute only.
A program may use at most 128 MiB of HBM per device.

v0:
```python
import functools

import jax
import jax.numpy as jnp
from jax import lax
from jax.experimental import pallas as pl
from jax.experimental.pallas import tpu as pltpu
from jax.sharding import PartitionSpec as P

GAMMA = 5.0 / 3.0
DT_DX = 0.02
EDGE = 32
GHOST = 3
SLOTS = 4
CHUNKS = 4
FIELDS = 5
PLANE = 16
LINKS = 16
ITEM_ROWS = 120
MIB = 1024 * 1024

F32 = jnp.float32
ANY = pl.BlockSpec(memory_space=pl.ANY)
SMEM = pl.BlockSpec(memory_space=pltpu.SMEM)
VMEM = pl.BlockSpec(memory_space=pltpu.VMEM)
CHUNK_SHAPE = (2, FIELDS, 64, 128)


def start_copy(plan, slot, rounds, chunk, cells, received, target, sem):
    taken = jnp.bool_(False)
    for r in reversed(range(rounds)):
        for j in range(2):
            hit = jnp.logical_and(plan[2 * r + j] == slot, jnp.logical_not(taken))

            @pl.when(hit)
            def _(r=r, j=j):
                pltpu.make_async_copy(received[r].at[j], target, sem).start()

            taken = jnp.logical_or(taken, hit)

    @pl.when(jnp.logical_not(taken))
    def _():
        pltpu.make_async_copy(cells.at[slot, :, chunk], target, sem).start()


def wait_copy(chunk, cells, target, sem):
    pltpu.make_async_copy(cells.at[0, :, chunk], target, sem).wait()


def pack_first_kernel(plan, cells, *refs):
    outs, sems = refs[:CHUNKS], refs[CHUNKS]
    copies = []
    for c in range(CHUNKS):
        for j in range(2):
            copies.append(
                pltpu.make_async_copy(cells.at[plan[j], :, c], outs[c].at[j], sems.at[c, j])
            )
    for copy in copies:
        copy.start()
    for copy in copies:
        copy.wait()


def pack_first(plan, cells):
    return pl.pallas_call(
        pack_first_kernel,
        out_shape=[jax.ShapeDtypeStruct(CHUNK_SHAPE, F32)] * CHUNKS,
        in_specs=[SMEM, ANY],
        out_specs=[VMEM] * CHUNKS,
        scratch_shapes=[pltpu.SemaphoreType.DMA((CHUNKS, 2))],
        compiler_params=pltpu.CompilerParams(vmem_limit_bytes=2 * MIB),
        name="pack_first",
    )(plan, cells)


def pack_kernel(r, chunk, plan, cells, *refs):
    received, out, sems = refs[:r], refs[r + 1], refs[r + 2]
    for j in range(2):
        start_copy(plan, plan[2 * r + j], r, chunk, cells, received, out.at[j], sems.at[j])
    for j in range(2):
        wait_copy(chunk, cells, out.at[j], sems.at[j])


def pack(r, chunk, plan, cells, received, after):
    return pl.pallas_call(
        functools.partial(pack_kernel, r, chunk),
        out_shape=jax.ShapeDtypeStruct(CHUNK_SHAPE, F32),
        in_specs=[SMEM, ANY] + [ANY] * (r + 1),
        out_specs=VMEM,
        scratch_shapes=[pltpu.SemaphoreType.DMA((2,))],
        compiler_params=pltpu.CompilerParams(vmem_limit_bytes=2 * MIB),
        name="pack",
    )(plan, cells, *received, after)


def swapped(block, axis):
    count = lax.axis_size(axis)
    return lax.ppermute(block, axis, [(i, i ^ (count // 2)) for i in range(count)])


def migrate(plan, cells):
    first = pack_first(plan, cells)
    got = [[swapped(block, "gx") for block in first], [None] * CHUNKS, [None] * CHUNKS]
    last = first[0]
    order = [(1, 0), (1, 1), (2, 0), (1, 2), (2, 1), (1, 3), (2, 2), (2, 3)]
    for r, c in order:
        last = pack(r, c, plan, cells, [got[i][c] for i in range(r)], last)
        got[r][c] = swapped(last, ("gx", "gy", "gz")[r])
    return got


def load_patches(plan, cells, received, patches, sems, wait):
    for k in range(SLOTS):
        for c in range(CHUNKS):
            if wait:
                wait_copy(c, cells, patches.at[k, :, c], sems.at[k, c])
            else:
                chunk_got = [received[r * CHUNKS + c] for r in range(3)]
                start_copy(plan, k, 3, c, cells, chunk_got, patches.at[k, :, c], sems.at[k, c])


def primitives(u):
    inv = 1.0 / u[0]
    v = [u[i] * inv for i in (1, 2, 3)]
    kinetic = u[1] * v[0] + u[2] * v[1] + u[3] * v[2]
    return [u[0]] + v + [(GAMMA - 1.0) * (u[4] - 0.5 * kinetic)]


def block_transpose(b):
    lane = lax.broadcasted_iota(jnp.int32, (8, 128), 1)
    low = lane < 64
    even = (lane & 32) == 0

    def rolled(x, shift):
        return pltpu.roll(x, shift, 1)

    a0 = jnp.where(low, b[0], rolled(b[2], 64))
    a2 = jnp.where(low, rolled(b[0], 64), b[2])
    a1 = jnp.where(low, b[1], rolled(b[3], 64))
    a3 = jnp.where(low, rolled(b[1], 64), b[3])
    return [
        jnp.where(even, a0, rolled(a1, 32)),
        jnp.where(even, rolled(a0, 96), a1),
        jnp.where(even, a2, rolled(a3, 32)),
        jnp.where(even, rolled(a2, 96), a3),
    ]


def face_block(turned, side, f, layer, g):
    if side == 0:
        return turned[f, g, pl.ds(layer, 8, stride=EDGE), :]
    if side == 1:
        return turned[f, g, pl.ds(EDGE - GHOST + layer, 8, stride=EDGE), :]
    if side == 2:
        return turned[f, 0, pl.ds(layer * EDGE + 8 * g, 8), :]
    return turned[f, 3, pl.ds((8 - GHOST + layer) * EDGE + 8 * g, 8), :]


def faces_kernel(plan, place, links, cells, *refs):
    received = refs[: 3 * CHUNKS]
    turned, send, own_items, z_first, z_last = refs[3 * CHUNKS : 3 * CHUNKS + 5]
    patches, prim, items, sems, item_sems = refs[3 * CHUNKS + 5 :]
    load_patches(plan, cells, received, patches, sems, False)
    load_patches(plan, cells, received, patches, sems, True)

    def turn(g, carry):
        for half in range(2):
            rows = pl.ds(pl.multiple_of((2 * g + half) * 8, 8), 8)
            for k in range(SLOTS):
                for c in range(CHUNKS):
                    w = primitives([patches[k, f, c, rows, :] for f in range(FIELDS)])
                    for f in range(FIELDS):
                        prim[f, pl.ds((k * CHUNKS + c) * 8, 8), :] = w[f]
            for f in range(FIELDS):
                turned[f, g, pl.ds(half * 128, 128), :] = jnp.transpose(prim[f])
        return carry

    lax.fori_loop(0, 4, turn, 0)

    for side in range(4):
        for f in range(FIELDS):
            for layer in range(GHOST):
                blocks = block_transpose([face_block(turned, side, f, layer, g) for g in range(4)])
                for k in range(SLOTS):
                    items[k * 4 + side, pl.ds((f * GHOST + layer) * 8, 8), :] = blocks[k]

    me = place[0]
    owners = [links[me * LINKS + i] // SLOTS for i in range(LINKS)]
    for i in range(LINKS):
        rank = jnp.int32(0)
        for j in range(i):
            rank = rank + (owners[j] == owners[i]).astype(jnp.int32)
        rank = jnp.minimum(rank, 1)

        @pl.when(owners[i] != me)
        def _(i=i, rank=rank):
            pltpu.make_async_copy(items.at[i], send.at[owners[i], rank], item_sems.at[i]).start()

        @pl.when(owners[i] == me)
        def _(i=i):
            pltpu.make_async_copy(items.at[i], own_items.at[i], item_sems.at[i]).start()

    for k in range(SLOTS):
        for f in range(FIELDS):
            for layer in range(GHOST):
                z_first[k, f, layer] = patches[k, f, 0, pl.ds(layer, 8, stride=8), :]
                z_last[k, f, layer] = patches[k, f, CHUNKS - 1, pl.ds(5 + layer, 8, stride=8), :]

    for i in range(LINKS):
        pltpu.make_async_copy(items.at[i], own_items.at[i], item_sems.at[i]).wait()


def faces(plan, place, links, cells, received):
    z_shape = jax.ShapeDtypeStruct((SLOTS, FIELDS, GHOST, 8, 128), F32)
    return pl.pallas_call(
        faces_kernel,
        out_shape=[
            jax.ShapeDtypeStruct((FIELDS, 4, 256, 128), F32),
            jax.ShapeDtypeStruct((PLANE, 2, ITEM_ROWS, 128), F32),
            jax.ShapeDtypeStruct((LINKS, ITEM_ROWS, 128), F32),
            z_shape,
            z_shape,
        ],
        in_specs=[SMEM, SMEM, SMEM, ANY] + [ANY] * (3 * CHUNKS),
        out_specs=[VMEM, ANY, ANY, VMEM, VMEM],
        scratch_shapes=[
            pltpu.VMEM((SLOTS, FIELDS, CHUNKS, 64, 128), F32),
            pltpu.VMEM((FIELDS, 128, 128), F32),
            pltpu.VMEM((LINKS, ITEM_ROWS, 128), F32),
            pltpu.SemaphoreType.DMA((SLOTS, CHUNKS)),
            pltpu.SemaphoreType.DMA((LINKS,)),
        ],
        compiler_params=pltpu.CompilerParams(vmem_limit_bytes=12 * MIB),
        name="faces",
    )(plan, place, links, cells, *received)


def clamped(x, y):
    return jnp.minimum(jnp.maximum(x, jnp.minimum(y, 0.0)), jnp.maximum(y, 0.0))


def euler_terms(w, normal):
    density, velocity, pressure = w[0], w[1:4], w[4]
    speed = velocity[normal]
    momentum = [density * v for v in velocity]
    kinetic = momentum[0] * velocity[0] + momentum[1] * velocity[1] + momentum[2] * velocity[2]
    energy = 1.5 * pressure + 0.5 * kinetic
    flux = [momentum[normal]]
    for i in range(3):
        term = momentum[i] * speed
        flux.append(term + pressure if i == normal else term)
    flux.append((energy + pressure) * speed)
    stiff = GAMMA * pressure
    signal = jnp.abs(speed) + stiff * lax.rsqrt(stiff * density)
    return [density] + momentum + [energy], flux, signal


def sweep(get, put, normal):
    w, d, a = {}, {}, {}
    b, prev_flux, left = {}, None, None
    for i in range(-3, EDGE + GHOST):
        w[i] = get(i)
        if i == -3:
            continue
        d[i - 1] = [hi - lo for hi, lo in zip(w[i], w[i - 1])]
        if i < 0:
            continue
        m = i - 2
        a[m] = [
            clamped(0.5 * mid - (1.0 / 12.0) * (up - down), mid)
            for down, mid, up in zip(d[m - 1], d[m], d[m + 1])
        ]
        b[m + 1] = [mid - part for mid, part in zip(d[m], a[m])]
        if m < -1:
            continue
        lower = [v - clamped(y, 2.0 * x) for v, x, y in zip(w[m], a[m], b[m])]
        upper = [v + clamped(x, 2.0 * y) for v, x, y in zip(w[m], a[m], b[m])]
        if left is not None:
            right = euler_terms(lower, normal)
            fastest = jnp.maximum(left[2], right[2])
            flux = [
                gl + gr - fastest * (ur - ul)
                for gl, gr, ul, ur in zip(left[1], right[1], left[0], right[0])
            ]
            if prev_flux is not None:
                put(m - 1, [new - old for new, old in zip(flux, prev_flux)])
            prev_flux = flux
        left = euler_terms(upper, normal)


def update_kernel(plan, place, links, cells, *refs):
    received = refs[: 3 * CHUNKS]
    turned, arrived, own_items, z_below, z_above, out = refs[3 * CHUNKS : 3 * CHUNKS + 6]
    patches, items, ghosts, change, z_change, sems, item_sems = refs[3 * CHUNKS + 6 :]
    load_patches(plan, cells, received, patches, sems, False)

    me = place[0]
    for k in range(SLOTS):
        for side in range(4):
            i = k * 4 + side
            entry = links[me * LINKS + i]
            owner = entry // SLOTS
            source = (entry % SLOTS) * 4 + (side ^ 1)
            rank = jnp.int32(0)
            for j in range(LINKS - 1):
                same = jnp.logical_and(links[owner * LINKS + j] // SLOTS == me, j < source)
                rank = rank + same.astype(jnp.int32)
            rank = jnp.minimum(rank, 1)

            @pl.when(owner != me)
            def _(i=i, owner=owner, rank=rank):
                pltpu.make_async_copy(arrived.at[owner, rank], items.at[i], item_sems.at[i]).start()

            @pl.when(owner == me)
            def _(i=i, source=source):
                pltpu.make_async_copy(own_items.at[source], items.at[i], item_sems.at[i]).start()

    load_patches(plan, cells, received, patches, sems, True)

    def z_sweep(k, carry):
        def get(i):
            if i < 0:
                u = [z_below[k, f, i + GHOST] for f in range(FIELDS)]
            elif i >= EDGE:
                u = [z_above[k, f, i - EDGE] for f in range(FIELDS)]
            else:
                u = [patches[k, f, i // 8, pl.ds(i % 8, 8, stride=8), :] for f in range(FIELDS)]
            return primitives(u)

        def put(i, values):
            for f in range(FIELDS):
                z_change[k, f, i // 8, pl.ds(i % 8, 8, stride=8), :] = values[f]

        sweep(get, put, 2)
        return carry

    lax.fori_loop(0, SLOTS, z_sweep, 0)

    for i in range(LINKS):
        pltpu.make_async_copy(own_items.at[i], items.at[i], item_sems.at[i]).wait()
    for side in range(4):
        for n in range(FIELDS * GHOST):
            blocks = block_transpose([items[k * 4 + side, pl.ds(n * 8, 8), :] for k in range(SLOTS)])
            for g in range(4):
                ghosts[side, n, g] = blocks[g]

    def y_sweep(g, carry):
        def rows(i):
            return pl.ds(pl.multiple_of((i % 8) * EDGE + 8 * g, 8), 8)

        def get(i):
            if i < 0:
                return [ghosts[2, f * GHOST + i + GHOST, g] for f in range(FIELDS)]
            if i >= EDGE:
                return [ghosts[3, f * GHOST + i - EDGE, g] for f in range(FIELDS)]
            return [turned[f, i // 8, rows(i), :] for f in range(FIELDS)]

        def put(i, values):
            for f in range(FIELDS):
                change[f, i // 8, rows(i), :] = values[f]

        sweep(get, put, 1)
        return carry

    lax.fori_loop(0, 4, y_sweep, 0)

    def x_sweep(g, carry):
        def get(i):
            if i < 0:
                return [ghosts[0, f * GHOST + i + GHOST, g] for f in range(FIELDS)]
            if i >= EDGE:
                return [ghosts[1, f * GHOST + i - EDGE, g] for f in range(FIELDS)]
            return [turned[f, g, pl.ds(i, 8, stride=EDGE), :] for f in range(FIELDS)]

        def put(i, values):
            for f in range(FIELDS):
                rows = pl.ds(i, 8, stride=EDGE)
                change[f, g, rows, :] = change[f, g, rows, :] + values[f]

        sweep(get, put, 0)
        return carry

    lax.fori_loop(0, 4, x_sweep, 0)

    def finish(g, carry):
        for f in range(FIELDS):
            for half in range(2):
                rows = pl.ds(pl.multiple_of((2 * g + half) * 8, 8), 8)
                back = jnp.transpose(change[f, g, pl.ds(half * 128, 128), :])
                for k in range(SLOTS):
                    for c in range(CHUNKS):
                        n = (k * CHUNKS + c) * 8
                        total = back[n : n + 8] + z_change[k, f, c, rows, :]
                        out[k, f, c, rows, :] = patches[k, f, c, rows, :] - (0.5 * DT_DX) * total
        return carry

    lax.fori_loop(0, 4, finish, 0)


def update(plan, place, links, cells, received, turned, arrived, own_items, z_below, z_above):
    patch_shape = (SLOTS, FIELDS, CHUNKS, 64, 128)
    return pl.pallas_call(
        update_kernel,
        out_shape=jax.ShapeDtypeStruct(patch_shape, F32),
        in_specs=[SMEM, SMEM, SMEM, ANY] + [ANY] * (3 * CHUNKS) + [VMEM, ANY, ANY, VMEM, VMEM],
        out_specs=VMEM,
        scratch_shapes=[
            pltpu.VMEM(patch_shape, F32),
            pltpu.VMEM((LINKS, ITEM_ROWS, 128), F32),
            pltpu.VMEM((4, FIELDS * GHOST, 4, 8, 128), F32),
            pltpu.VMEM((FIELDS, 4, 256, 128), F32),
            pltpu.VMEM(patch_shape, F32),
            pltpu.SemaphoreType.DMA((SLOTS, CHUNKS)),
            pltpu.SemaphoreType.DMA((LINKS,)),
        ],
        compiler_params=pltpu.CompilerParams(vmem_limit_bytes=20 * MIB),
        name="update",
    )(plan, place, links, cells, *received, turned, arrived, own_items, z_below, z_above)


def local(cells, moves, neighbours):
    tiled = cells.reshape(SLOTS, FIELDS, CHUNKS, 8, 8, 128).transpose(0, 1, 2, 4, 3, 5)
    tiled = tiled.reshape(SLOTS, FIELDS, CHUNKS, 64, 128)
    plan = moves[lax.axis_index(("gx", "gy", "gz"))].reshape(-1)
    place = lax.axis_index(("gx", "gy")).reshape(1)
    links = neighbours.reshape(-1)

    got = migrate(plan, tiled)
    received = [block for row in got for block in row]
    turned, send, own_items, z_first, z_last = faces(plan, place, links, tiled, received)

    layers = lax.axis_size("gz")
    up = [(i, (i + 1) % layers) for i in range(layers)]
    down = [(j, i) for i, j in up]
    z_below = lax.ppermute(z_last, "gz", up)
    z_above = lax.ppermute(z_first, "gz", down)
    arrived = lax.all_to_all(send, ("gx", "gy"), 0, 0, tiled=True)
    result = update(
        plan, place, links, tiled, received, turned, arrived, own_items, z_below, z_above
    )
    result = result.reshape(SLOTS, FIELDS, CHUNKS, 8, 8, 128).transpose(0, 1, 2, 4, 3, 5)
    return result.reshape(cells.shape)


def solution(mesh):
    return jax.shard_map(
        local,
        mesh=mesh,
        in_specs=(P(("gx", "gy", "gz"), None, None, None), P(), P()),
        out_specs=P(("gx", "gy", "gz"), None, None, None),
        check_vma=False,
    )
```

profile of v0, /device:TPU:0, one launch (start us, length us, event | category | flops | bytes accessed | tf_op | source)
XLA Modules:
  0.0 165.9 jit_solution(12870596540928696283)
XLA Ops:
  1.0 1.7 %copy-done.1 = f32[4,5,32,1024]{3,2,1,0:T(8,128)S(1)} copy-done((f32[4,5,32,1024]{3,2,1,0:T(8,128)S(1)}, f32[4,5,32,1024]{3,2,1,0:T(8,128)}, u32[]{:S(2)}) %copy-start.1) | copy-done | bytes 2621464
  2.7 1.0 pack_first.1
  3.7 4.0 %collective-permute-start = (f32[2,5,64,128]{3,2,1,0:T(8,128)S(1)}, f32[2,5,64,128]{3,2,1,0:T(8,128)S(1)}, u32[]{:S(2)}, u32[]{:S(2)}) collective-permute-start(f32[2,5,64,128]{3,2,1,0:T(8,128)S(1)} %get-tuple-element.14.refs_1_), channel_id=1, source_target_pairs={{0,64},{32,96},{64,0},{96,32},{1,65},{33,97},{65,1},{97,33},{2,66}... | collective-permute-start | bytes 983048 | tf_op jit(solution)/shard_map/ppermute | solution.py:98
  7.8 8.4 %collective-permute-done.refs_0_ = f32[2,5,64,128]{3,2,1,0:T(8,128)S(1)} collective-permute-done((f32[2,5,64,128]{3,2,1,0:T(8,128)S(1)}, f32[2,5,64,128]{3,2,1,0:T(8,128)S(1)}, u32[]{:S(2)}, u32[]{:S(2)}) %collective-permute-start) | collective-permute-done | bytes 327712 | tf_op jit(solution)/shard_map/ppermute | solution.py:98
  16.3 0.9 pack.8.refs_1_
  17.2 3.3 %collective-permute-start.4 = (f32[2,5,64,128]{3,2,1,0:T(8,128)S(1)}, f32[2,5,64,128]{3,2,1,0:T(8,128)S(1)}, u32[]{:S(2)}, u32[]{:S(2)}) collective-permute-start(f32[2,5,64,128]{3,2,1,0:T(8,128)S(1)} %pack.8.refs_1_), channel_id=1, source_target_pairs={{0,16},{8,24},{16,0},{24,8},{1,17},{9,25},{17,1},{25,9},{2,18},{10... | collective-permute-start | bytes 983048 | tf_op jit(solution)/shard_map/ppermute | solution.py:98
  20.4 3.6 %collective-permute-start.2 = (f32[2,5,64,128]{3,2,1,0:T(8,128)S(1)}, f32[2,5,64,128]{3,2,1,0:T(8,128)S(1)}, u32[]{:S(2)}, u32[]{:S(2)}) collective-permute-start(f32[2,5,64,128]{3,2,1,0:T(8,128)S(1)} %get-tuple-element.16), channel_id=1, source_target_pairs={{0,64},{32,96},{64,0},{96,32},{1,65},{33,97},{65,1},{97,33},{2,66}... | collective-permute-start | bytes 983048 | tf_op jit(solution)/shard_map/ppermute | solution.py:98
  24.0 0.9 pack.9.refs_2_
  24.9 2.6 %collective-permute-start.5 = (f32[2,5,64,128]{3,2,1,0:T(8,128)S(1)}, f32[2,5,64,128]{3,2,1,0:T(8,128)S(1)}, u32[]{:S(2)}, u32[]{:S(2)}) collective-permute-start(f32[2,5,64,128]{3,2,1,0:T(8,128)S(1)} %pack.9.refs_2_), channel_id=1, source_target_pairs={{0,16},{8,24},{16,0},{24,8},{1,17},{9,25},{17,1},{25,9},{2,18},{10... | collective-permute-start | bytes 983048 | tf_op jit(solution)/shard_map/ppermute | solution.py:98
  27.4 3.6 %collective-permute-start.3 = (f32[2,5,64,128]{3,2,1,0:T(8,128)S(1)}, f32[2,5,64,128]{3,2,1,0:T(8,128)S(1)}, u32[]{:S(2)}, u32[]{:S(2)}) collective-permute-start(f32[2,5,64,128]{3,2,1,0:T(8,128)S(1)} %get-tuple-element.17), channel_id=1, source_target_pairs={{0,64},{32,96},{64,0},{96,32},{1,65},{33,97},{65,1},{97,33},{2,66}... | collective-permute-start | bytes 983048 | tf_op jit(solution)/shard_map/ppermute | solution.py:98
  31.0 1.6 pack.10.refs_1_
  32.7 0.9 pack.11.refs_2_
  33.5 0.9 collective-permute-start.6
  34.5 1.6 pack.12.refs_1_
  37.6 3.1 %collective-permute-start.7 = (f32[2,5,64,128]{3,2,1,0:T(8,128)S(1)}, f32[2,5,64,128]{3,2,1,0:T(8,128)S(1)}, u32[]{:S(2)}, u32[]{:S(2)}) collective-permute-start(f32[2,5,64,128]{3,2,1,0:T(8,128)S(1)} %pack.13.refs_2_), channel_id=1, source_target_pairs={{0,16},{8,24},{16,0},{24,8},{1,17},{9,25},{17,1},{25,9},{2,18},{10... | collective-permute-start | bytes 983048 | tf_op jit(solution)/shard_map/ppermute | solution.py:98
  40.7 3.0 %collective-permute-start.9 = (f32[2,5,64,128]{3,2,1,0:T(8,128)}, f32[2,5,64,128]{3,2,1,0:T(8,128)}, u32[]{:S(2)}, u32[]{:S(2)}) collective-permute-start(f32[2,5,64,128]{3,2,1,0:T(8,128)} %pack.12.refs_1_), channel_id=1, source_target_pairs={{0,4},{1,5},{2,6},{3,7},{4,0},{5,1},{6,2},{7,3},{8,12},{9,13},{10,... | collective-permute-start | bytes 983048 | tf_op jit(solution)/shard_map/ppermute | solution.py:98
  44.2 1.6 pack.14.refs_2_
  46.6 2.6 %collective-permute-done.7.refs_1_.refs_7_ = f32[2,5,64,128]{3,2,1,0:T(8,128)S(1)} collective-permute-done((f32[2,5,64,128]{3,2,1,0:T(8,128)S(1)}, f32[2,5,64,128]{3,2,1,0:T(8,128)S(1)}, u32[]{:S(2)}, u32[]{:S(2)}) %collective-permute-start.7) | collective-permute-done | bytes 327712 | tf_op jit(solution)/shard_map/ppermute | solution.py:98
  49.2 1.6 pack.15
  50.9 3.4 %collective-permute-start.11 = (f32[2,5,64,128]{3,2,1,0:T(8,128)}, f32[2,5,64,128]{3,2,1,0:T(8,128)}, u32[]{:S(2)}, u32[]{:S(2)}) collective-permute-start(f32[2,5,64,128]{3,2,1,0:T(8,128)} %pack.15), channel_id=1, source_target_pairs={{0,4},{1,5},{2,6},{3,7},{4,0},{5,1},{6,2},{7,3},{8,12},{9,13},{10,... | collective-permute-start | bytes 983048 | tf_op jit(solution)/shard_map/ppermute | solution.py:98
  54.7 5.5 %collective-permute-done.8.refs_8_ = f32[2,5,64,128]{3,2,1,0:T(8,128)} collective-permute-done((f32[2,5,64,128]{3,2,1,0:T(8,128)}, f32[2,5,64,128]{3,2,1,0:T(8,128)}, u32[]{:S(2)}, u32[]{:S(2)}) %collective-permute-start.8) | collective-permute-done | bytes 327712 | tf_op jit(solution)/shard_map/ppermute | solution.py:98
  60.2 7.0 %collective-permute-done.11.refs_11_ = f32[2,5,64,128]{3,2,1,0:T(8,128)} collective-permute-done((f32[2,5,64,128]{3,2,1,0:T(8,128)}, f32[2,5,64,128]{3,2,1,0:T(8,128)}, u32[]{:S(2)}, u32[]{:S(2)}) %collective-permute-start.11) | collective-permute-done | bytes 327712 | tf_op jit(solution)/shard_map/ppermute | solution.py:98
  67.2 4.9 %collective-permute-done.10.refs_10_ = f32[2,5,64,128]{3,2,1,0:T(8,128)} collective-permute-done((f32[2,5,64,128]{3,2,1,0:T(8,128)}, f32[2,5,64,128]{3,2,1,0:T(8,128)}, u32[]{:S(2)}, u32[]{:S(2)}) %collective-permute-start.10) | collective-permute-done | bytes 327712 | tf_op jit(solution)/shard_map/ppermute | solution.py:98
  72.1 1.0 copy-done.4
  73.1 1.0 copy-done.7
  74.1 1.0 copy-done.10
  75.0 1.0 copy-done.13
  76.0 1.0 copy-done.16
  77.0 1.0 copy-done.19
  77.9 8.8 %faces.1 = (f32[5,4,256,128]{3,2,1,0:T(8,128)S(1)}, f32[16,2,120,128]{3,2,1,0:T(8,128)S(1)}, f32[16,120,128]{2,1,0:T(8,128)S(1)}, f32[4,5,3,8,128]{4,3,2,1,0:T(8,128)S(1)}, f32[4,5,3,8,128]{4,3,2,1,0:T(8,128)S(1)}) custom-call(s32[6]{0:T(128)S(1)} %reshape_squeeze.3.plan, s32[1]{0:T(128)} %bitcast.place, s32[256]{0:T(256)S(1)} %reshape.19.links, ...), custom_call_target="tpu_custom_call" | custom-call | tf_op jit(solution)/shard_map/faces/pallas_call | solution.py:215
  86.8 1.5 copy-done.21
  88.3 1.3 copy-done.23
  89.5 1.0 copy-done.24
  91.9 4.7 %all-to-all-start = ((f32[16,2,120,128]{3,2,1,0:T(8,128)}), f32[16,2,120,128]{3,2,1,0:T(8,128)}, u32[]{:S(2)}, u32[]{:S(2)}) async-start(f32[16,2,120,128]{3,2,1,0:T(8,128)} %copy-done.23), calls=%async_computation | async-start | bytes 3932160 | tf_op jit(solution)/shard_map/all_to_all | solution.py:437
  96.7 1.1 collective-permute-start.12
  97.8 3.1 %collective-permute-start.13 = (f32[4,5,3,8,128]{4,3,2,1,0:T(8,128)}, f32[4,5,3,8,128]{4,3,2,1,0:T(8,128)S(1)}, u32[]{:S(2)}, u32[]{:S(2)}) collective-permute-start(f32[4,5,3,8,128]{4,3,2,1,0:T(8,128)} %copy-done.28), channel_id=1, source_target_pairs={{1,0},{2,1},{3,2},{4,3},{5,4},{6,5},{7,6},{0,7},{9,8},{10,9},{11,1... | collective-permute-start | bytes 737288 | tf_op jit(solution)/shard_map/ppermute | solution.py:436
  100.9 28.5 %collective-permute-done.12.refs_15_ = f32[4,5,3,8,128]{4,3,2,1,0:T(8,128)S(1)} collective-permute-done((f32[4,5,3,8,128]{4,3,2,1,0:T(8,128)}, f32[4,5,3,8,128]{4,3,2,1,0:T(8,128)S(1)}, u32[]{:S(2)}, u32[]{:S(2)}) %collective-permute-start.12) | collective-permute-done | bytes 245792 | tf_op jit(solution)/shard_map/ppermute | solution.py:435
  129.3 1.4 collective-permute-done.13.refs_16_
  131.4 1.0 copy-done.5
  132.4 1.0 copy-done.8
  133.3 1.0 copy-done.11
  134.3 1.0 copy-done.14
  135.3 1.0 copy-done.17
  136.3 1.0 copy-done.20
  137.2 1.7 %copy-done.22 = f32[5,4,256,128]{3,2,1,0:T(8,128)S(1)} copy-done((f32[5,4,256,128]{3,2,1,0:T(8,128)S(1)}, f32[5,4,256,128]{3,2,1,0:T(8,128)}, u32[]{:S(2)}) %copy-start.22) | copy-done | bytes 2621464
  139.0 1.2 copy-done.25
  140.2 0.9 copy-done.27
  141.1 24.6 %update.1 = f32[4,5,4,64,128]{4,3,2,1,0:T(8,128)} custom-call(s32[6]{0:T(128)S(1)} %reshape_squeeze.3.plan, s32[1]{0:T(128)} %bitcast.place, s32[256]{0:T(256)S(1)} %reshape.19.links, f32[4,5,4,64,128]{4,3,2,1,0:T(8,128)S(1)} %bitcast.21, f32[2,5,64,128]{3,2,1,0:T(8,128)S(1)} %collective-permute-done.refs_0_, ...), custom_call_target="tpu_custom_call" | custom-call | tf_op jit(solution)/shard_map/update/pallas_call | solution.py:402
  (59 shorter events, 6.4 us)
Async XLA Ops:
  0.0 0.7 copy-start
  1.0 1.8 %copy-start.1 = (f32[4,5,32,1024]{3,2,1,0:T(8,128)S(1)}, f32[4,5,32,1024]{3,2,1,0:T(8,128)}, u32[]{:S(2)}) copy-start(f32[4,5,32,1024]{3,2,1,0:T(8,128)} %param.3) | copy-start | bytes 7864324
  3.7 12.6 %collective-permute-start = (f32[2,5,64,128]{3,2,1,0:T(8,128)S(1)}, f32[2,5,64,128]{3,2,1,0:T(8,128)S(1)}, u32[]{:S(2)}, u32[]{:S(2)}) collective-permute-start(f32[2,5,64,128]{3,2,1,0:T(8,128)S(1)} %get-tuple-element.14.refs_1_), channel_id=1, source_target_pairs={{0,64},{32,96},{64,0},{96,32},{1,65},{33,97},{65,1},{97,33},{2,66}... | collective-permute-start | bytes 983048 | tf_op jit(solution)/shard_map/ppermute | solution.py:98
  7.7 16.2 %collective-permute-start.1 = (f32[2,5,64,128]{3,2,1,0:T(8,128)S(1)}, f32[2,5,64,128]{3,2,1,0:T(8,128)S(1)}, u32[]{:S(2)}, u32[]{:S(2)}) collective-permute-start(f32[2,5,64,128]{3,2,1,0:T(8,128)S(1)} %get-tuple-element.15), channel_id=1, source_target_pairs={{0,64},{32,96},{64,0},{96,32},{1,65},{33,97},{65,1},{97,33},{2,66}... | collective-permute-start | bytes 983048 | tf_op jit(solution)/shard_map/ppermute | solution.py:98
  17.2 13.9 %collective-permute-start.4 = (f32[2,5,64,128]{3,2,1,0:T(8,128)S(1)}, f32[2,5,64,128]{3,2,1,0:T(8,128)S(1)}, u32[]{:S(2)}, u32[]{:S(2)}) collective-permute-start(f32[2,5,64,128]{3,2,1,0:T(8,128)S(1)} %pack.8.refs_1_), channel_id=1, source_target_pairs={{0,16},{8,24},{16,0},{24,8},{1,17},{9,25},{17,1},{25,9},{2,18},{10... | collective-permute-start | bytes 983048 | tf_op jit(solution)/shard_map/ppermute | solution.py:98
  20.4 12.2 %collective-permute-start.2 = (f32[2,5,64,128]{3,2,1,0:T(8,128)S(1)}, f32[2,5,64,128]{3,2,1,0:T(8,128)S(1)}, u32[]{:S(2)}, u32[]{:S(2)}) collective-permute-start(f32[2,5,64,128]{3,2,1,0:T(8,128)S(1)} %get-tuple-element.16), channel_id=1, source_target_pairs={{0,64},{32,96},{64,0},{96,32},{1,65},{33,97},{65,1},{97,33},{2,66}... | collective-permute-start | bytes 983048 | tf_op jit(solution)/shard_map/ppermute | solution.py:98
  24.9 9.6 %collective-permute-start.5 = (f32[2,5,64,128]{3,2,1,0:T(8,128)S(1)}, f32[2,5,64,128]{3,2,1,0:T(8,128)S(1)}, u32[]{:S(2)}, u32[]{:S(2)}) collective-permute-start(f32[2,5,64,128]{3,2,1,0:T(8,128)S(1)} %pack.9.refs_2_), channel_id=1, source_target_pairs={{0,16},{8,24},{16,0},{24,8},{1,17},{9,25},{17,1},{25,9},{2,18},{10... | collective-permute-start | bytes 983048 | tf_op jit(solution)/shard_map/ppermute | solution.py:98
  27.4 9.3 %collective-permute-start.3 = (f32[2,5,64,128]{3,2,1,0:T(8,128)S(1)}, f32[2,5,64,128]{3,2,1,0:T(8,128)S(1)}, u32[]{:S(2)}, u32[]{:S(2)}) collective-permute-start(f32[2,5,64,128]{3,2,1,0:T(8,128)S(1)} %get-tuple-element.17), channel_id=1, source_target_pairs={{0,64},{32,96},{64,0},{96,32},{1,65},{33,97},{65,1},{97,33},{2,66}... | collective-permute-start | bytes 983048 | tf_op jit(solution)/shard_map/ppermute | solution.py:98
  31.0 2.5 %copy-start.9 = (f32[2,5,64,128]{3,2,1,0:T(8,128)}, f32[2,5,64,128]{3,2,1,0:T(8,128)S(1)}, u32[]{:S(2)}) copy-start(f32[2,5,64,128]{3,2,1,0:T(8,128)S(1)} %collective-permute-done.4.refs_1_.refs_4_) | copy-start | bytes 983044
  32.6 11.6 %copy-start.3 = (f32[2,5,64,128]{3,2,1,0:T(8,128)}, f32[2,5,64,128]{3,2,1,0:T(8,128)S(1)}, u32[]{:S(2)}) copy-start(f32[2,5,64,128]{3,2,1,0:T(8,128)S(1)} %collective-permute-done.2.refs_0_.refs_2_) | copy-start | bytes 983044
  33.5 10.7 %collective-permute-start.6 = (f32[2,5,64,128]{3,2,1,0:T(8,128)S(1)}, f32[2,5,64,128]{3,2,1,0:T(8,128)S(1)}, u32[]{:S(2)}, u32[]{:S(2)}) collective-permute-start(f32[2,5,64,128]{3,2,1,0:T(8,128)S(1)} %pack.11.refs_2_), channel_id=1, source_target_pairs={{0,16},{8,24},{16,0},{24,8},{1,17},{9,25},{17,1},{25,9},{2,18},{10... | collective-permute-start | bytes 983048 | tf_op jit(solution)/shard_map/ppermute | solution.py:98
  34.5 3.1 %copy-start.12 = (f32[2,5,64,128]{3,2,1,0:T(8,128)}, f32[2,5,64,128]{3,2,1,0:T(8,128)S(1)}, u32[]{:S(2)}) copy-start(f32[2,5,64,128]{3,2,1,0:T(8,128)S(1)} %collective-permute-done.5.refs_1_.refs_5_) | copy-start | bytes 983044
  36.7 12.5 %copy-start.6 = (f32[2,5,64,128]{3,2,1,0:T(8,128)}, f32[2,5,64,128]{3,2,1,0:T(8,128)S(1)}, u32[]{:S(2)}) copy-start(f32[2,5,64,128]{3,2,1,0:T(8,128)S(1)} %collective-permute-done.3.refs_0_.refs_3_) | copy-start | bytes 983044
  37.6 11.6 %collective-permute-start.7 = (f32[2,5,64,128]{3,2,1,0:T(8,128)S(1)}, f32[2,5,64,128]{3,2,1,0:T(8,128)S(1)}, u32[]{:S(2)}, u32[]{:S(2)}) collective-permute-start(f32[2,5,64,128]{3,2,1,0:T(8,128)S(1)} %pack.13.refs_2_), channel_id=1, source_target_pairs={{0,16},{8,24},{16,0},{24,8},{1,17},{9,25},{17,1},{25,9},{2,18},{10... | collective-permute-start | bytes 983048 | tf_op jit(solution)/shard_map/ppermute | solution.py:98
  40.7 14.0 %collective-permute-start.9 = (f32[2,5,64,128]{3,2,1,0:T(8,128)}, f32[2,5,64,128]{3,2,1,0:T(8,128)}, u32[]{:S(2)}, u32[]{:S(2)}) collective-permute-start(f32[2,5,64,128]{3,2,1,0:T(8,128)} %pack.12.refs_1_), channel_id=1, source_target_pairs={{0,4},{1,5},{2,6},{3,7},{4,0},{5,1},{6,2},{7,3},{8,12},{9,13},{10,... | collective-permute-start | bytes 983048 | tf_op jit(solution)/shard_map/ppermute | solution.py:98
  43.7 16.5 %collective-permute-start.8 = (f32[2,5,64,128]{3,2,1,0:T(8,128)}, f32[2,5,64,128]{3,2,1,0:T(8,128)}, u32[]{:S(2)}, u32[]{:S(2)}) collective-permute-start(f32[2,5,64,128]{3,2,1,0:T(8,128)} %pack.10.refs_1_), channel_id=1, source_target_pairs={{0,4},{1,5},{2,6},{3,7},{4,0},{5,1},{6,2},{7,3},{8,12},{9,13},{10,... | collective-permute-start | bytes 983048 | tf_op jit(solution)/shard_map/ppermute | solution.py:98
  45.8 0.7 copy-start.15
  46.6 7.9 %copy-start.30 = (s32[64,4]{0,1:T(4,128)S(1)}, s32[64,4]{0,1:T(4,128)}, u32[]{:S(2)}) copy-start(s32[64,4]{0,1:T(4,128)} %param.5) | copy-start | bytes 3076
  46.6 25.5 %copy-start.2 = (f32[4,5,32,1024]{3,2,1,0:T(8,128)S(1)}, f32[4,5,32,1024]{3,2,1,0:T(8,128)}, u32[]{:S(2)}) copy-start(f32[4,5,32,1024]{3,2,1,0:T(8,128)} %param.3) | copy-start | bytes 7864324
  49.2 1.6 copy-start.18
  50.9 16.3 %collective-permute-start.11 = (f32[2,5,64,128]{3,2,1,0:T(8,128)}, f32[2,5,64,128]{3,2,1,0:T(8,128)}, u32[]{:S(2)}, u32[]{:S(2)}) collective-permute-start(f32[2,5,64,128]{3,2,1,0:T(8,128)} %pack.15), channel_id=1, source_target_pairs={{0,4},{1,5},{2,6},{3,7},{4,0},{5,1},{6,2},{7,3},{8,12},{9,13},{10,... | collective-permute-start | bytes 983048 | tf_op jit(solution)/shard_map/ppermute | solution.py:98
  54.3 17.8 %collective-permute-start.10 = (f32[2,5,64,128]{3,2,1,0:T(8,128)}, f32[2,5,64,128]{3,2,1,0:T(8,128)}, u32[]{:S(2)}, u32[]{:S(2)}) collective-permute-start(f32[2,5,64,128]{3,2,1,0:T(8,128)} %pack.14.refs_2_), channel_id=1, source_target_pairs={{0,4},{1,5},{2,6},{3,7},{4,0},{5,1},{6,2},{7,3},{8,12},{9,13},{10,... | collective-permute-start | bytes 983048 | tf_op jit(solution)/shard_map/ppermute | solution.py:98
  72.1 1.0 copy-start.4
  73.1 1.0 copy-start.7
  74.1 1.0 copy-start.10
  75.0 1.0 copy-start.13
  76.0 1.0 copy-start.16
  77.0 1.0 copy-start.19
  86.8 1.5 copy-start.21
  88.3 1.3 copy-start.23
  89.5 1.0 copy-start.24
  90.5 0.7 copy-start.28
  91.2 0.7 copy-start.29
  91.9 39.5 %all-to-all-start = ((f32[16,2,120,128]{3,2,1,0:T(8,128)}), f32[16,2,120,128]{3,2,1,0:T(8,128)}, u32[]{:S(2)}, u32[]{:S(2)}) async-start(f32[16,2,120,128]{3,2,1,0:T(8,128)} %copy-done.23), calls=%async_computation | async-start | bytes 3932160 | tf_op jit(solution)/shard_map/all_to_all | solution.py:437
  96.7 32.7 %collective-permute-start.12 = (f32[4,5,3,8,128]{4,3,2,1,0:T(8,128)}, f32[4,5,3,8,128]{4,3,2,1,0:T(8,128)S(1)}, u32[]{:S(2)}, u32[]{:S(2)}) collective-permute-start(f32[4,5,3,8,128]{4,3,2,1,0:T(8,128)} %copy-done.29), channel_id=1, source_target_pairs={{0,1},{1,2},{2,3},{3,4},{4,5},{5,6},{6,7},{7,0},{8,9},{9,10},{10,1... | collective-permute-start | bytes 737288 | tf_op jit(solution)/shard_map/ppermute | solution.py:435
  97.8 32.9 %collective-permute-start.13 = (f32[4,5,3,8,128]{4,3,2,1,0:T(8,128)}, f32[4,5,3,8,128]{4,3,2,1,0:T(8,128)S(1)}, u32[]{:S(2)}, u32[]{:S(2)}) collective-permute-start(f32[4,5,3,8,128]{4,3,2,1,0:T(8,128)} %copy-done.28), channel_id=1, source_target_pairs={{1,0},{2,1},{3,2},{4,3},{5,4},{6,5},{7,6},{0,7},{9,8},{10,9},{11,1... | collective-permute-start | bytes 737288 | tf_op jit(solution)/shard_map/ppermute | solution.py:436
  130.7 0.7 copy-start.26
  131.4 1.0 copy-start.5
  132.4 1.0 copy-start.8
  133.3 1.0 copy-start.11
  134.3 1.0 copy-start.14
  135.3 1.0 copy-start.17
  136.3 1.0 copy-start.20
  137.2 1.7 %copy-start.22 = (f32[5,4,256,128]{3,2,1,0:T(8,128)S(1)}, f32[5,4,256,128]{3,2,1,0:T(8,128)}, u32[]{:S(2)}) copy-start(f32[5,4,256,128]{3,2,1,0:T(8,128)} %copy-done.21) | copy-start | bytes 7864324
  139.0 1.2 copy-start.25
  140.2 0.9 copy-start.27
where the time goes:
time: 167 us; the launch traced here: 166 us
  waiting for transfers between devices  59 us (35%)
  Pallas kernels  44.3 us (27%)
  starting transfers between devices  37.2 us (22%)
  local copies, waits for them, and re-layouts  25.1 us (15%)
    ppermute x12, waiting for transfers between devices, swapped(): lax.ppermute(block, axis, [(i, i ^ count // 2) for i in range(count)])  29.1 us
    ppermute x1, waiting for transfers between devices, local(): z_below = lax.ppermute(z_last, 'gz', up)  28.5 us
    ppermute x12, starting transfers between devices, swapped(): lax.ppermute(block, axis, [(i, i ^ count // 2) for i in range(count)])  28.3 us
    unnamed x63, local copies, waits for them, and re-layouts  24.7 us
    pallas_call x1, Pallas kernels, update(): pl.pallas_call(update_kernel, out_shape=jax.ShapeDtypeStruct(patch_shape,...  24.6 us
    pallas_call x8, Pallas kernels, pack(): pl.pallas_call(functools.partial(pack_kernel, r, chunk), out_shape=jax.Sh...  9.88 us
    pallas_call x1, Pallas kernels, faces(): pl.pallas_call(faces_kernel, out_shape=[jax.ShapeDtypeStruct((FIELDS, 4,...  8.83 us
    all_to_all x1, starting transfers between devices, local(): arrived = lax.all_to_all(send, ('gx', 'gy'), 0, 0, tiled=True)  4.72 us
  transfers between devices with their start and end apart: 15, of which 8 were waited for; matrix products, arithmetic and copies ran while one was open for 0% of the time, Pallas kernels for 6%

commit v1 on v0

v1 whole, which is shorter than its diff:
```python
import functools

import jax
import jax.numpy as jnp
from jax import lax
from jax.experimental import pallas as pl
from jax.experimental.pallas import tpu as pltpu
from jax.sharding import PartitionSpec as P

GAMMA = 5.0 / 3.0
DT_DX = 0.02
EDGE = 32
GHOST = 3
SLOTS = 4
LAYERS = 4
FIELDS = 5
PLANE = 16
LINKS = 16
GROUPS = ((0, 1, 2), (3, 4))
ITEM_ROWS = FIELDS * GHOST * 8
PATCH_SHAPE = (FIELDS, SLOTS, LAYERS, 64, 128)
TURNED_SHAPE = (FIELDS, 4, 256, 128)
MIB = 1024 * 1024

F32 = jnp.float32
ANY = pl.BlockSpec(memory_space=pl.ANY)
HBM = pl.BlockSpec(memory_space=pltpu.HBM)
SMEM = pl.BlockSpec(memory_space=pltpu.SMEM)
VMEM = pl.BlockSpec(memory_space=pltpu.VMEM)
LONG = pl.CostEstimate(flops=10**12, bytes_accessed=10**10, transcendentals=10**10)
CHUNK_SHAPE = (2, LAYERS, 64, 128)


def held(x):
    return pltpu.with_memory_space_constraint(x, pltpu.HBM)


def start_copy(plan, slot, rounds, field, cells, received, target, sem, part=slice(None)):
    taken = jnp.bool_(False)
    for r in reversed(range(rounds)):
        for j in range(2):
            hit = jnp.logical_and(plan[2 * r + j] == slot, jnp.logical_not(taken))

            @pl.when(hit)
            def _(r=r, j=j):
                pltpu.make_async_copy(received[r].at[j, part], target, sem).start()

            taken = jnp.logical_or(taken, hit)

    @pl.when(jnp.logical_not(taken))
    def _():
        pltpu.make_async_copy(cells.at[slot, field, part], target, sem).start()


def pack_kernel(sends, taken, plan, cells, *refs):
    received, refs = refs[:taken], refs[-len(sends) - 1 :]
    outs, sems = refs[:-1], refs[-1]
    at = 0
    for n, (r, f) in enumerate(sends):
        got = received[at : at + r]
        at += r
        for j in range(2):
            start_copy(plan, plan[2 * r + j], r, f, cells, got, outs[n].at[j], sems.at[n, j])
    for n, (r, f) in enumerate(sends):
        for j in range(2):
            pltpu.make_async_copy(cells.at[0, f], outs[n].at[j], sems.at[n, j]).wait()


def pack(sends, plan, cells, received, after):
    return pl.pallas_call(
        functools.partial(pack_kernel, sends, len(received)),
        out_shape=[jax.ShapeDtypeStruct(CHUNK_SHAPE, F32)] * len(sends),
        in_specs=[SMEM, HBM] + [ANY] * (len(received) + len(after)),
        out_specs=[VMEM] * len(sends),
        scratch_shapes=[pltpu.SemaphoreType.DMA((len(sends), 2))],
        compiler_params=pltpu.CompilerParams(vmem_limit_bytes=4 * MIB),
        name="pack",
    )(plan, held(cells), *received, *after)


def swapped(block, axis):
    count = lax.axis_size(axis)
    return lax.ppermute(block, axis, [(i, i ^ (count // 2)) for i in range(count)])


WAVES = (
    ([(0, 0), (0, 1), (0, 2), (0, 3), (0, 4)], []),
    ([(1, 0)], []),
    ([(1, 1)], []),
    ([(1, 2), (2, 0)], []),
    ([(1, 3), (2, 1)], []),
    ([(1, 4), (2, 2)], [(2, 0)]),
    ([(2, 3)], [(2, 1)]),
    ([(2, 4)], [(2, 2)]),
)


def migrate(plan, cells):
    got, last = {}, []
    for sends, awaited in WAVES:
        received = [got[i, f] for r, f in sends for i in range(r)]
        after = list(last[-1:]) + [got[at] for at in awaited]
        last = pack(sends, plan, cells, received, after)
        for (r, f), block in zip(sends, last):
            got[r, f] = swapped(block, ("gx", "gy", "gz")[r])
    return got, last[-1]


def primitives(u):
    inv = 1.0 / u[0]
    v = [u[i] * inv for i in (1, 2, 3)]
    kinetic = u[1] * v[0] + u[2] * v[1] + u[3] * v[2]
    return [u[0]] + v + [(GAMMA - 1.0) * (u[4] - 0.5 * kinetic)]


def block_transpose(b):
    lane = lax.broadcasted_iota(jnp.int32, (8, 128), 1)
    low = lane < 64
    even = (lane & 32) == 0

    def rolled(x, shift):
        return pltpu.roll(x, shift, 1)

    a0 = jnp.where(low, b[0], rolled(b[2], 64))
    a2 = jnp.where(low, rolled(b[0], 64), b[2])
    a1 = jnp.where(low, b[1], rolled(b[3], 64))
    a3 = jnp.where(low, rolled(b[1], 64), b[3])
    return [
        jnp.where(even, a0, rolled(a1, 32)),
        jnp.where(even, rolled(a0, 96), a1),
        jnp.where(even, a2, rolled(a3, 32)),
        jnp.where(even, rolled(a2, 96), a3),
    ]


def face_block(turned, side, f, layer, g):
    if side == 0:
        return turned[f, g, pl.ds(layer, 8, stride=EDGE), :]
    if side == 1:
        return turned[f, g, pl.ds(EDGE - GHOST + layer, 8, stride=EDGE), :]
    if side == 2:
        return turned[f, 0, pl.ds(layer * EDGE + 8 * g, 8), :]
    return turned[f, 3, pl.ds((8 - GHOST + layer) * EDGE + 8 * g, 8), :]


def faces_kernel(fields, plan, place, links, cells, *refs):
    count, first, last = len(fields), fields[0], fields[0] > 0
    received = refs[: 3 * count]
    refs = refs[3 * count + 1 + 4 * last :]
    patches_out, turned_out, send, own_items = refs[:4]
    patches, turned, items, sems, item_sems, out_sems = refs[-6:]
    for n, f in enumerate(fields):
        got = received[3 * n : 3 * n + 3]
        for k in range(SLOTS):
            start_copy(plan, k, 3, f, cells, got, patches.at[n, k], sems.at[n, k])
    mine = pl.ds(first, count)
    outs = [
        pltpu.make_async_copy(patches, patches_out.at[mine], out_sems.at[0]),
        pltpu.make_async_copy(turned, turned_out.at[mine], out_sems.at[1]),
    ]
    for n, f in enumerate(fields):
        for k in range(SLOTS):
            pltpu.make_async_copy(cells.at[k, f], patches.at[n, k], sems.at[n, k]).wait()

        def turn(g, carry, n=n):
            for half in range(2):
                rows = pl.ds(pl.multiple_of((2 * g + half) * 8, 8), 8)
                tiles = [patches[n, k, c, rows, :] for k in range(SLOTS) for c in range(LAYERS)]
                turned[n, g, pl.ds(half * 128, 128), :] = jnp.transpose(
                    jnp.concatenate(tiles, axis=0)
                )
            return carry

        lax.fori_loop(0, 4, turn, 0)
    for copy in outs:
        copy.start()

    me = place[0]
    owners = [links[me * LINKS + i] // SLOTS for i in range(LINKS)]
    rows = pl.ds(first * GHOST * 8, count * GHOST * 8)
    for side in range(4):
        for n in range(count):
            for layer in range(GHOST):
                blocks = block_transpose([face_block(turned, side, n, layer, g) for g in range(4)])
                for k in range(SLOTS):
                    items[k * 4 + side, pl.ds((n * GHOST + layer) * 8, 8), :] = blocks[k]
        for i in range(side, LINKS, 4):
            rank = jnp.int32(0)
            for j in range(i):
                rank = rank + (owners[j] == owners[i]).astype(jnp.int32)
            rank = jnp.minimum(rank, 1)

            @pl.when(owners[i] != me)
            def _(i=i, rank=rank):
                target = send.at[owners[i], rank, rows]
                pltpu.make_async_copy(items.at[i], target, item_sems.at[i]).start()

            @pl.when(owners[i] == me)
            def _(i=i):
                target = own_items.at[i, rows]
                pltpu.make_async_copy(items.at[i], target, item_sems.at[i]).start()

    for i in range(LINKS):
        pltpu.make_async_copy(items.at[i], own_items.at[i, rows], item_sems.at[i]).wait()
    for copy in outs:
        copy.wait()


def faces(fields, plan, place, links, cells, received, after, carried):
    count, first = len(fields), fields[0]
    scratch = [
        pltpu.VMEM((count,) + PATCH_SHAPE[1:], F32),
        pltpu.VMEM((count,) + TURNED_SHAPE[1:], F32),
        pltpu.VMEM((LINKS, count * GHOST * 8, 128), F32),
        pltpu.SemaphoreType.DMA((count, SLOTS)),
        pltpu.SemaphoreType.DMA((LINKS,)),
        pltpu.SemaphoreType.DMA((2,)),
    ]
    inputs = [held(cells)] + list(received) + [after] + [held(x) for x in carried]
    return pl.pallas_call(
        functools.partial(faces_kernel, fields),
        out_shape=[
            pltpu.HBM(PATCH_SHAPE, F32),
            pltpu.HBM(TURNED_SHAPE, F32),
            pltpu.HBM((PLANE, 2, ITEM_ROWS, 128), F32),
            pltpu.HBM((LINKS, ITEM_ROWS, 128), F32),
        ],
        in_specs=[SMEM] * 3 + [HBM] + [ANY] * (3 * count + 1) + [HBM] * len(carried),
        out_specs=[HBM] * 4,
        scratch_shapes=scratch,
        input_output_aliases={3 * count + 5 + i: i for i in range(len(carried))},
        compiler_params=pltpu.CompilerParams(vmem_limit_bytes=16 * MIB),
        name="faces",
    )(plan, place, links, *inputs)


def ends_kernel(plan, cells, patches, *refs):
    late = GROUPS[1]
    received = refs[: 3 * len(late)]
    z_first, z_last, ends, sems = refs[3 * len(late) :]
    loads = []
    for e in range(2):
        source = patches.at[pl.ds(0, late[0]), :, e * (LAYERS - 1)]
        load = pltpu.make_async_copy(source, ends.at[e, pl.ds(0, late[0])], sems.at[e, 0, 0])
        load.start()
        loads.append(load)
    places = [(n, k, e) for n in range(len(late)) for k in range(SLOTS) for e in range(2)]
    for n, k, e in places:
        f, got, layer = late[n], received[3 * n : 3 * n + 3], e * (LAYERS - 1)
        start_copy(plan, k, 3, f, cells, got, ends.at[e, f, k], sems.at[e, n + 1, k], layer)
    for load in loads:
        load.wait()
    for n, k, e in places:
        f = late[n]
        pltpu.make_async_copy(cells.at[k, f, 0], ends.at[e, f, k], sems.at[e, n + 1, k]).wait()
    for f in range(FIELDS):
        for k in range(SLOTS):
            for layer in range(GHOST):
                z_first[k, f, layer] = ends[0, f, k, pl.ds(layer, 8, stride=8), :]
                z_last[k, f, layer] = ends[1, f, k, pl.ds(5 + layer, 8, stride=8), :]


def z_ends(plan, cells, patches, received):
    z_shape = jax.ShapeDtypeStruct((SLOTS, FIELDS, GHOST, 8, 128), F32)
    return pl.pallas_call(
        ends_kernel,
        out_shape=[z_shape, z_shape],
        in_specs=[SMEM, HBM, HBM] + [ANY] * len(received),
        out_specs=[VMEM, VMEM],
        scratch_shapes=[
            pltpu.VMEM((2, FIELDS, SLOTS, 64, 128), F32),
            pltpu.SemaphoreType.DMA((2, 1 + len(GROUPS[1]), SLOTS)),
        ],
        compiler_params=pltpu.CompilerParams(vmem_limit_bytes=6 * MIB),
        name="z_ends",
    )(plan, held(cells), held(patches), *received)


def clamped(x, y):
    return jnp.minimum(jnp.maximum(x, jnp.minimum(y, 0.0)), jnp.maximum(y, 0.0))


def euler_terms(w, normal):
    density, velocity, pressure = w[0], w[1:4], w[4]
    speed = velocity[normal]
    momentum = [density * v for v in velocity]
    kinetic = momentum[0] * velocity[0] + momentum[1] * velocity[1] + momentum[2] * velocity[2]
    energy = 1.5 * pressure + 0.5 * kinetic
    flux = [momentum[normal]]
    for i in range(3):
        term = momentum[i] * speed
        flux.append(term + pressure if i == normal else term)
    flux.append((energy + pressure) * speed)
    stiff = GAMMA * pressure
    signal = jnp.abs(speed) + stiff * lax.rsqrt(stiff * density)
    return [density] + momentum + [energy], flux, signal


def sweep(get, put, normal, first, last):
    w, d, a, b = {}, {}, {}, {}
    prev, left = None, None
    start = first - 2
    for i in range(start, last + 4):
        w[i] = get(i)
        if i == start:
            continue
        d[i - 1] = [hi - lo for hi, lo in zip(w[i], w[i - 1])]
        m = i - 2
        if m <= start:
            continue
        a[m] = [
            clamped(0.5 * mid - (1.0 / 12.0) * (up - down), mid)
            for down, mid, up in zip(d[m - 1], d[m], d[m + 1])
        ]
        b[m + 1] = [mid - part for mid, part in zip(d[m], a[m])]
        if m < first:
            continue
        if m > first:
            lower = [v - clamped(y, 2.0 * x) for v, x, y in zip(w[m], a[m], b[m])]
            right = euler_terms(lower, normal)
            fastest = jnp.maximum(left[2], right[2])
            flux = [
                gl + gr - fastest * (ur - ul)
                for gl, gr, ul, ur in zip(left[1], right[1], left[0], right[0])
            ]
            if prev is not None:
                put(m - 1, [new - old for new, old in zip(flux, prev)])
            elif m > 0:
                put(m - 1, flux)
            prev = flux
        if m <= last:
            upper = [v + clamped(x, 2.0 * y) for v, x, y in zip(w[m], a[m], b[m])]
            left = euler_terms(upper, normal)
    if last + 1 < EDGE:
        put(last + 1, [-v for v in prev])


def y_rows(i, g):
    return pl.ds(pl.multiple_of((i % 8) * EDGE + 8 * g, 8), 8)


def own_layer(turned, direction, i, g):
    rows = pl.ds(i, 8, stride=EDGE) if direction == 0 else y_rows(i, g)
    return primitives([turned[f, g if direction == 0 else i // 8, rows, :] for f in range(FIELDS)])


def add_change(change, direction, i, g, values):
    rows = pl.ds(i, 8, stride=EDGE) if direction == 0 else y_rows(i, g)
    for f in range(FIELDS):
        at = (f, g if direction == 0 else i // 8, rows)
        change[at] = change[at] + values[f]


def inner_kernel(turned_in, after, change, turned, sem):
    load = pltpu.make_async_copy(turned_in, turned, sem)
    load.start()
    load.wait()

    def y_sweep(g, carry):
        def put(i, values):
            for f in range(FIELDS):
                change[f, i // 8, y_rows(i, g), :] = values[f]

        for i in (0, 1, EDGE - 2, EDGE - 1):
            put(i, [jnp.zeros((8, 128), F32)] * FIELDS)
        sweep(lambda i: own_layer(turned, 1, i, g), put, 1, 2, EDGE - 4)
        return carry

    lax.fori_loop(0, 4, y_sweep, 0)

    def x_sweep(g, carry):
        def put(i, values):
            add_change(change, 0, i, g, values)

        sweep(lambda i: own_layer(turned, 0, i, g), put, 0, 2, EDGE - 4)
        return carry

    lax.fori_loop(0, 4, x_sweep, 0)


def inner(turned, after):
    return pl.pallas_call(
        inner_kernel,
        out_shape=jax.ShapeDtypeStruct(TURNED_SHAPE, F32),
        in_specs=[HBM, ANY],
        out_specs=VMEM,
        scratch_shapes=[pltpu.VMEM(TURNED_SHAPE, F32), pltpu.SemaphoreType.DMA],
        compiler_params=pltpu.CompilerParams(vmem_limit_bytes=12 * MIB),
        cost_estimate=LONG,
        name="inner",
    )(held(turned), after)


def z_kernel(patches_in, z_below, z_above, partial, patches, sems):
    for k in range(SLOTS):
        pltpu.make_async_copy(patches_in.at[:, k], patches.at[:, k], sems.at[k]).start()

    def z_sweep(k, carry):
        pltpu.make_async_copy(patches_in.at[:, k], patches.at[:, k], sems.at[k]).wait()

        def get(i):
            if i < 0:
                u = [z_below[k, f, i + GHOST] for f in range(FIELDS)]
            elif i >= EDGE:
                u = [z_above[k, f, i - EDGE] for f in range(FIELDS)]
            else:
                rows = pl.ds(i % 8, 8, stride=8)
                u = [patches[f, k, i // 8, rows, :] for f in range(FIELDS)]
            return primitives(u)

        def put(i, values):
            rows = pl.ds(i % 8, 8, stride=8)
            for f in range(FIELDS):
                partial[f, k, i // 8, rows, :] = (
                    patches[f, k, i // 8, rows, :] - (0.5 * DT_DX) * values[f]
                )

        sweep(get, put, 2, -1, EDGE - 1)
        return carry

    lax.fori_loop(0, SLOTS, z_sweep, 0)


def z_update(patches, z_below, z_above):
    return pl.pallas_call(
        z_kernel,
        out_shape=jax.ShapeDtypeStruct(PATCH_SHAPE, F32),
        in_specs=[HBM, VMEM, VMEM],
        out_specs=VMEM,
        scratch_shapes=[pltpu.VMEM(PATCH_SHAPE, F32), pltpu.SemaphoreType.DMA((SLOTS,))],
        compiler_params=pltpu.CompilerParams(vmem_limit_bytes=12 * MIB),
        cost_estimate=LONG,
        name="z_update",
    )(held(patches), z_below, z_above)


def outer_kernel(place, links, turned_in, arrived, own_items, inside, partial_in, out, *scratch):
    turned, items, ghosts, change, partial, result, item_sems, sems, out_sems = scratch
    me = place[0]
    loads = [
        pltpu.make_async_copy(turned_in, turned, sems.at[0]),
        pltpu.make_async_copy(inside, change, sems.at[1]),
        pltpu.make_async_copy(partial_in, partial, sems.at[2]),
    ]
    for i in range(LINKS):
        entry = links[me * LINKS + i]
        owner = entry // SLOTS
        source = (entry % SLOTS) * 4 + (i % 4 ^ 1)
        rank = jnp.int32(0)
        for j in range(LINKS - 1):
            same = jnp.logical_and(links[owner * LINKS + j] // SLOTS == me, j < source)
            rank = rank + same.astype(jnp.int32)
        rank = jnp.minimum(rank, 1)

        @pl.when(owner != me)
        def _(i=i, owner=owner, rank=rank):
            pltpu.make_async_copy(arrived.at[owner, rank], items.at[i], item_sems.at[i]).start()

        @pl.when(owner == me)
        def _(i=i, source=source):
            pltpu.make_async_copy(own_items.at[source], items.at[i], item_sems.at[i]).start()

    for load in loads:
        load.start()
    for i in range(LINKS):
        pltpu.make_async_copy(own_items.at[i], items.at[i], item_sems.at[i]).wait()
    for side in range(4):
        for n in range(FIELDS * GHOST):
            blocks = [items[k * 4 + side, pl.ds(n * 8, 8), :] for k in range(SLOTS)]
            for g, block in enumerate(block_transpose(blocks)):
                ghosts[side, n, g] = block
    loads[0].wait()
    loads[1].wait()

    def border(g, carry):
        for direction in (1, 0):
            low, high = (0, 1) if direction == 0 else (2, 3)

            def get(i):
                if i < 0:
                    u = [ghosts[low, f * GHOST + i + GHOST, g] for f in range(FIELDS)]
                elif i >= EDGE:
                    u = [ghosts[high, f * GHOST + i - EDGE, g] for f in range(FIELDS)]
                else:
                    return own_layer(turned, direction, i, g)
                return primitives(u)

            def put(i, values):
                add_change(change, direction, i, g, values)

            sweep(get, put, direction, -1, 1)
            sweep(get, put, direction, EDGE - 3, EDGE - 1)
        return carry

    lax.fori_loop(0, 4, border, 0)
    loads[2].wait()

    for f in range(FIELDS):

        def finish(g, carry, f=f):
            for half in range(2):
                rows = pl.ds(pl.multiple_of((2 * g + half) * 8, 8), 8)
                back = jnp.transpose(change[f, g, pl.ds(half * 128, 128), :])
                for k in range(SLOTS):
                    for c in range(LAYERS):
                        n = (k * LAYERS + c) * 8
                        result[f, k, c, rows, :] = (
                            partial[f, k, c, rows, :] - (0.5 * DT_DX) * back[n : n + 8]
                        )
            return carry

        lax.fori_loop(0, 4, finish, 0)
        pltpu.make_async_copy(result.at[f], out.at[:, f], out_sems.at[f]).start()
    for f in range(FIELDS):
        pltpu.make_async_copy(result.at[f], out.at[:, f], out_sems.at[f]).wait()


def outer(place, links, turned, arrived, own_items, inside, partial):
    return pl.pallas_call(
        outer_kernel,
        out_shape=jax.ShapeDtypeStruct((SLOTS, FIELDS, LAYERS, 64, 128), F32),
        in_specs=[SMEM, SMEM] + [HBM] * 3 + [ANY] * 2,
        out_specs=HBM,
        scratch_shapes=[
            pltpu.VMEM(TURNED_SHAPE, F32),
            pltpu.VMEM((LINKS, ITEM_ROWS, 128), F32),
            pltpu.VMEM((4, FIELDS * GHOST, 4, 8, 128), F32),
            pltpu.VMEM(TURNED_SHAPE, F32),
            pltpu.VMEM(PATCH_SHAPE, F32),
            pltpu.VMEM(PATCH_SHAPE, F32),
            pltpu.SemaphoreType.DMA((LINKS,)),
            pltpu.SemaphoreType.DMA((3,)),
            pltpu.SemaphoreType.DMA((FIELDS,)),
        ],
        compiler_params=pltpu.CompilerParams(vmem_limit_bytes=24 * MIB),
        name="outer",
    )(place, links, held(turned), held(arrived), held(own_items), inside, partial)


def local(cells, moves, neighbours):
    tiled = cells.reshape(SLOTS, FIELDS, LAYERS, 8, 8, 128).transpose(0, 1, 2, 4, 3, 5)
    tiled = tiled.reshape(SLOTS, FIELDS, LAYERS, 64, 128)
    plan = moves[lax.axis_index(("gx", "gy", "gz"))].reshape(-1)
    place = lax.axis_index(("gx", "gy")).reshape(1)
    links = neighbours.reshape(-1)

    got, after = migrate(plan, tiled)
    made = ()
    for fields in GROUPS:
        received = [got[r, f] for f in fields for r in range(3)]
        made = faces(fields, plan, place, links, tiled, received, after, made)
        if not fields[0]:
            late = [got[r, f] for f in GROUPS[1] for r in range(3)]
            z_first, z_last = z_ends(plan, tiled, made[0], late)
            after = z_last
    patches, turned, send, own_items = made

    arrived = lax.all_to_all(send, ("gx", "gy"), 0, 0, tiled=True)
    layers = lax.axis_size("gz")
    up = [(i, (i + 1) % layers) for i in range(layers)]
    down = [(j, i) for i, j in up]
    z_below = lax.ppermute(z_last, "gz", up)
    z_above = lax.ppermute(z_first, "gz", down)
    partial = z_update(patches, z_below, z_above)
    inside = inner(turned, partial)
    result = outer(place, links, turned, arrived, own_items, inside, partial)
    result = result.reshape(SLOTS, FIELDS, LAYERS, 8, 8, 128).transpose(0, 1, 2, 4, 3, 5)
    return result.reshape(cells.shape)


def solution(mesh):
    return jax.shard_map(
        local,
        mesh=mesh,
        in_specs=(P(("gx", "gy", "gz"), None, None, None), P(), P()),
        out_specs=P(("gx", "gy", "gz"), None, None, None),
        check_vma=False,
    )
```

time: 167 us -> 128 us (0.77)
  waiting for transfers between devices: 59 us -> 19.5 us
  local copies, waits for them, and re-layouts: 25.1 us -> 6.32 us
  Pallas kernels: 44.3 us -> 59.2 us
  starting transfers between devices: 37.2 us -> 41.8 us
    ppermute x1, waiting for transfers between devices: 28.5 us -> 0.01 us  [local(): z_below = lax.ppermute(z_last, 'gz', up)]
    ppermute x12 -> x15, waiting for transfers between devices: 29.1 us -> 8.81 us  [swapped(): lax.ppermute(block, axis, [(i, i ^ count // 2) for i in range(count)])]
    unnamed x63 -> x17, local copies, waits for them, and re-layouts: 24.7 us -> 5.92 us
    pallas_call x11 -> x14, Pallas kernels: 44.3 us -> 59.2 us  [the longest x8 13.6 us: pack(): pl.pallas_call(functools.partial(pack_kernel, sends, len(received)), out_...]
    all_to_all x1, waiting for transfers between devices: 0.01 us -> 10.7 us  [local(): arrived = lax.all_to_all(send, ('gx', 'gy'), 0, 0, tiled=True)]
    ppermute x12 -> x15, starting transfers between devices: 28.3 us -> 33.7 us  [swapped(): lax.ppermute(block, axis, [(i, i ^ count // 2) for i in range(count)])]
  transfers between devices with their start and end apart: 15 -> 18, of which waited for: 8 -> 4; matrix products, arithmetic and copies ran while one was open for 0% -> 0% of each run, Pallas kernels for 6% -> 33%
where the time goes in v1:
time: 128 us; the launch traced here: 127 us
  Pallas kernels  59.2 us (46%)
  starting transfers between devices  41.8 us (33%)
  waiting for transfers between devices  19.5 us (15%)
  local copies, waits for them, and re-layouts  6.32 us (5%)
    ppermute x15, starting transfers between devices, swapped(): lax.ppermute(block, axis, [(i, i ^ count // 2) for i in range(count)])  33.7 us
    pallas_call x8, Pallas kernels, pack(): pl.pallas_call(functools.partial(pack_kernel, sends, len(received)), out_...  13.6 us
    pallas_call x1, Pallas kernels, outer(): pl.pallas_call(outer_kernel, out_shape=jax.ShapeDtypeStruct((SLOTS, FIELD...  13.1 us
    pallas_call x2, Pallas kernels, faces(): pl.pallas_call(functools.partial(faces_kernel, fields), out_shape=[pltpu....  12.7 us
    pallas_call x1, Pallas kernels, inner(): pl.pallas_call(inner_kernel, out_shape=jax.ShapeDtypeStruct(TURNED_SHAPE,...  11.6 us
    all_to_all x1, waiting for transfers between devices, local(): arrived = lax.all_to_all(send, ('gx', 'gy'), 0, 0, tiled=True)  10.7 us
    ppermute x15, waiting for transfers between devices, swapped(): lax.ppermute(block, axis, [(i, i ^ count // 2) for i in range(count)])  8.81 us
    unnamed x17, local copies, waits for them, and re-layouts  5.92 us
  transfers between devices with their start and end apart: 18, of which 4 were waited for; matrix products, arithmetic and copies ran while one was open for 0% of the time, Pallas kernels for 33%

profile of v1, /device:TPU:0, one launch (start us, length us, event | category | flops | bytes accessed | tf_op | source)
XLA Modules:
  0.0 127.2 jit_solution(10375863937452804272)
XLA Ops:
  0.0 0.7 copy-done
  0.7 0.2 dynamic-slice_reduce_fusion
  0.9 0.1 reshape_squeeze.3.plan
  1.0 2.0 %pack.8 = (f32[2,4,64,128]{3,2,1,0:T(8,128)S(1)}, f32[2,4,64,128]{3,2,1,0:T(8,128)S(1)}, f32[2,4,64,128]{3,2,1,0:T(8,128)S(1)}, f32[2,4,64,128]{3,2,1,0:T(8,128)S(1)}, f32[2,4,64,128]{3,2,1,0:T(8,128)S(1)}) custom-call(s32[6]{0:T(128)S(1)} %reshape_squeeze.3.plan, f32[4,5,4,64,128]{4,3,2,1,0:T(8,128)} %bitcast.11), custom_call_target="tpu_custom_call" | custom-call | tf_op jit(solution)/shard_map/pack/pallas_call | solution.py:70
  3.0 4.0 %collective-permute-start.2 = (f32[2,4,64,128]{3,2,1,0:T(8,128)S(1)}, f32[2,4,64,128]{3,2,1,0:T(8,128)S(1)}, u32[]{:S(2)}, u32[]{:S(2)}) collective-permute-start(f32[2,4,64,128]{3,2,1,0:T(8,128)S(1)} %get-tuple-element.28), channel_id=1, source_target_pairs={{0,64},{32,96},{64,0},{96,32},{1,65},{33,97},{65,1},{97,33},{2,66}... | collective-permute-start | bytes 786440 | tf_op jit(solution)/shard_map/ppermute | solution.py:83
  7.0 0.1 collective-permute-start.1
  7.1 3.4 %collective-permute-start.4 = (f32[2,4,64,128]{3,2,1,0:T(8,128)S(1)}, f32[2,4,64,128]{3,2,1,0:T(8,128)S(1)}, u32[]{:S(2)}, u32[]{:S(2)}) collective-permute-start(f32[2,4,64,128]{3,2,1,0:T(8,128)S(1)} %get-tuple-element.30), channel_id=1, source_target_pairs={{0,64},{32,96},{64,0},{96,32},{1,65},{33,97},{65,1},{97,33},{2,66}... | collective-permute-start | bytes 786440 | tf_op jit(solution)/shard_map/ppermute | solution.py:83
  10.6 3.6 %collective-permute-done.2.refs_0_.refs_1_ = f32[2,4,64,128]{3,2,1,0:T(8,128)S(1)} collective-permute-done((f32[2,4,64,128]{3,2,1,0:T(8,128)S(1)}, f32[2,4,64,128]{3,2,1,0:T(8,128)S(1)}, u32[]{:S(2)}, u32[]{:S(2)}) %collective-permute-start.2) | collective-permute-done | bytes 262176 | tf_op jit(solution)/shard_map/ppermute | solution.py:83
  14.2 1.7 %pack.9.refs_1_ = f32[2,4,64,128]{3,2,1,0:T(8,128)S(1)} custom-call(s32[6]{0:T(128)S(1)} %reshape_squeeze.3.plan, f32[4,5,4,64,128]{4,3,2,1,0:T(8,128)} %bitcast.12, f32[2,4,64,128]{3,2,1,0:T(8,128)S(1)} %collective-permute-done.2.refs_0_.refs_1_, f32[2,4,64,128]{3,2,1,0:T(8,128)S(1)} %get-tuple-element.29.refs_1_), custom_call_target="tpu_custom_call" | custom-call | tf_op jit(solution)/shard_map/pack/pallas_call | solution.py:70
  15.8 3.1 %collective-permute-start.5 = (f32[2,4,64,128]{3,2,1,0:T(8,128)S(1)}, f32[2,4,64,128]{3,2,1,0:T(8,128)S(1)}, u32[]{:S(2)}, u32[]{:S(2)}) collective-permute-start(f32[2,4,64,128]{3,2,1,0:T(8,128)S(1)} %pack.9.refs_1_), channel_id=1, source_target_pairs={{0,16},{8,24},{16,0},{24,8},{1,17},{9,25},{17,1},{25,9},{2,18},{10... | collective-permute-start | bytes 786440 | tf_op jit(solution)/shard_map/ppermute | solution.py:83
  18.9 3.7 %collective-permute-start = (f32[2,4,64,128]{3,2,1,0:T(8,128)S(1)}, f32[2,4,64,128]{3,2,1,0:T(8,128)S(1)}, u32[]{:S(2)}, u32[]{:S(2)}) collective-permute-start(f32[2,4,64,128]{3,2,1,0:T(8,128)S(1)} %get-tuple-element.26), channel_id=1, source_target_pairs={{0,64},{32,96},{64,0},{96,32},{1,65},{33,97},{65,1},{97,33},{2,66}... | collective-permute-start | bytes 786440 | tf_op jit(solution)/shard_map/ppermute | solution.py:83
  22.7 1.7 %pack.10.refs_3_ = f32[2,4,64,128]{3,2,1,0:T(8,128)S(1)} custom-call(s32[6]{0:T(128)S(1)} %reshape_squeeze.3.plan, f32[4,5,4,64,128]{4,3,2,1,0:T(8,128)} %bitcast.13, f32[2,4,64,128]{3,2,1,0:T(8,128)S(1)} %collective-permute-done.1.refs_0_.refs_1_.refs_3_, f32[2,4,64,128]{3,2,1,0:T(8,128)S(1)} %pack.9.refs_1_), custom_call_target="tpu_custom_call" | custom-call | tf_op jit(solution)/shard_map/pack/pallas_call | solution.py:70
  24.4 0.2 collective-permute-start.3
  24.6 3.7 %collective-permute-start.7 = (f32[2,4,64,128]{3,2,1,0:T(8,128)S(1)}, f32[2,4,64,128]{3,2,1,0:T(8,128)S(1)}, u32[]{:S(2)}, u32[]{:S(2)}) collective-permute-start(f32[2,4,64,128]{3,2,1,0:T(8,128)S(1)} %get-tuple-element.29.refs_1_), channel_id=1, source_target_pairs={{0,64},{32,96},{64,0},{96,32},{1,65},{33,97},{65,1},{97,33},{2,66}... | collective-permute-start | bytes 786440 | tf_op jit(solution)/shard_map/ppermute | solution.py:83
  28.3 1.8 %pack.11 = (f32[2,4,64,128]{3,2,1,0:T(8,128)S(1)}, f32[2,4,64,128]{3,2,1,0:T(8,128)S(1)}) custom-call(s32[6]{0:T(128)S(1)} %reshape_squeeze.3.plan, f32[4,5,4,64,128]{4,3,2,1,0:T(8,128)} %bitcast.14, f32[2,4,64,128]{3,2,1,0:T(8,128)S(1)} %collective-permute-done.4.refs_0_.refs_1_.refs_6_, f32[2,4,64,128]{3,2,1,0:T(8,128)S(1)} %collective-permute-done.2.refs_0_.refs_1_, ...), custom_call_target="tpu_custom_call" | custom-call | tf_op jit(solution)/shard_map/pack/pallas_call | solution.py:70
  30.1 0.6 collective-permute-start.8
  30.7 2.7 %collective-permute-start.9 = (f32[2,4,64,128]{3,2,1,0:T(8,128)S(1)}, f32[2,4,64,128]{3,2,1,0:T(8,128)S(1)}, u32[]{:S(2)}, u32[]{:S(2)}) collective-permute-start(f32[2,4,64,128]{3,2,1,0:T(8,128)S(1)} %get-tuple-element.31.refs_3_), channel_id=1, source_target_pairs={{0,4},{1,5},{2,6},{3,7},{4,0},{5,1},{6,2},{7,3},{8,12},{9,13},{10,... | collective-permute-start | bytes 786440 | tf_op jit(solution)/shard_map/ppermute | solution.py:83
  33.4 0.1 collective-permute-done.3.refs_2_.refs_4_
  33.5 1.8 %pack.12 = (f32[2,4,64,128]{3,2,1,0:T(8,128)S(1)}, f32[2,4,64,128]{3,2,1,0:T(8,128)S(1)}) custom-call(s32[6]{0:T(128)S(1)} %reshape_squeeze.3.plan, f32[4,5,4,64,128]{4,3,2,1,0:T(8,128)} %bitcast.15, f32[2,4,64,128]{3,2,1,0:T(8,128)S(1)} %collective-permute-done.refs_0_, f32[2,4,64,128]{3,2,1,0:T(8,128)S(1)} %collective-permute-done.1.refs_0_.refs_1_.refs_3_, ...), custom_call_target="tpu_custom_call" | custom-call | tf_op jit(solution)/shard_map/pack/pallas_call | solution.py:70
  35.3 2.7 %collective-permute-start.6 = (f32[2,4,64,128]{3,2,1,0:T(8,128)S(1)}, f32[2,4,64,128]{3,2,1,0:T(8,128)S(1)}, u32[]{:S(2)}, u32[]{:S(2)}) collective-permute-start(f32[2,4,64,128]{3,2,1,0:T(8,128)S(1)} %get-tuple-element.32), channel_id=1, source_target_pairs={{0,16},{8,24},{16,0},{24,8},{1,17},{9,25},{17,1},{25,9},{2,18},{10... | collective-permute-start | bytes 786440 | tf_op jit(solution)/shard_map/ppermute | solution.py:83
  38.0 1.1 collective-permute-start.10
  39.0 1.8 %pack.13 = (f32[2,4,64,128]{3,2,1,0:T(8,128)S(1)}, f32[2,4,64,128]{3,2,1,0:T(8,128)S(1)}) custom-call(s32[6]{0:T(128)S(1)} %reshape_squeeze.3.plan, f32[4,5,4,64,128]{4,3,2,1,0:T(8,128)} %bitcast.16, f32[2,4,64,128]{3,2,1,0:T(8,128)S(1)} %collective-permute-done.7.refs_0_.refs_3_, f32[2,4,64,128]{3,2,1,0:T(8,128)S(1)} %collective-permute-done.4.refs_0_.refs_1_.refs_6_, ...), custom_call_target="tpu_custom_call" | custom-call | tf_op jit(solution)/shard_map/pack/pallas_call | solution.py:70
  40.8 4.0 %collective-permute-start.12 = (f32[2,4,64,128]{3,2,1,0:T(8,128)S(1)}, f32[2,4,64,128]{3,2,1,0:T(8,128)S(1)}, u32[]{:S(2)}, u32[]{:S(2)}) collective-permute-start(f32[2,4,64,128]{3,2,1,0:T(8,128)S(1)} %get-tuple-element.36), channel_id=1, source_target_pairs={{0,16},{8,24},{16,0},{24,8},{1,17},{9,25},{17,1},{25,9},{2,18},{10... | collective-permute-start | bytes 786440 | tf_op jit(solution)/shard_map/ppermute | solution.py:83
  44.8 2.9 %collective-permute-start.13 = (f32[2,4,64,128]{3,2,1,0:T(8,128)S(1)}, f32[2,4,64,128]{3,2,1,0:T(8,128)S(1)}, u32[]{:S(2)}, u32[]{:S(2)}) collective-permute-start(f32[2,4,64,128]{3,2,1,0:T(8,128)S(1)} %get-tuple-element.35.refs_2_), channel_id=1, source_target_pairs={{0,4},{1,5},{2,6},{3,7},{4,0},{5,1},{6,2},{7,3},{8,12},{9,13},{10,... | collective-permute-start | bytes 786440 | tf_op jit(solution)/shard_map/ppermute | solution.py:83
  47.7 1.5 %pack.14.refs_2_ = f32[2,4,64,128]{3,2,1,0:T(8,128)S(1)} custom-call(s32[6]{0:T(128)S(1)} %reshape_squeeze.3.plan, f32[4,5,4,64,128]{4,3,2,1,0:T(8,128)} %bitcast.17, f32[2,4,64,128]{3,2,1,0:T(8,128)S(1)} %collective-permute-done.refs_0_, f32[2,4,64,128]{3,2,1,0:T(8,128)S(1)} %collective-permute-done.6.refs_1_, ...), custom_call_target="tpu_custom_call" | custom-call | tf_op jit(solution)/shard_map/pack/pallas_call | solution.py:70
  49.2 0.0 copy-start.7
  49.2 0.2 collective-permute-start.11
  49.4 5.1 %collective-permute-done.13.refs_3_.refs_8_ = f32[2,4,64,128]{3,2,1,0:T(8,128)S(1)} collective-permute-done((f32[2,4,64,128]{3,2,1,0:T(8,128)S(1)}, f32[2,4,64,128]{3,2,1,0:T(8,128)S(1)}, u32[]{:S(2)}, u32[]{:S(2)}) %collective-permute-start.13) | collective-permute-done | bytes 262176 | tf_op jit(solution)/shard_map/ppermute | solution.py:83
  54.5 1.5 %pack.15.refs_9_ = f32[2,4,64,128]{3,2,1,0:T(8,128)S(1)} custom-call(s32[6]{0:T(128)S(1)} %reshape_squeeze.3.plan, f32[4,5,4,64,128]{4,3,2,1,0:T(8,128)} %bitcast.18, f32[2,4,64,128]{3,2,1,0:T(8,128)S(1)} %collective-permute-done.7.refs_0_.refs_3_, f32[2,4,64,128]{3,2,1,0:T(8,128)S(1)} %collective-permute-done.12.refs_1_.refs_4_, ...), custom_call_target="tpu_custom_call" | custom-call | tf_op jit(solution)/shard_map/pack/pallas_call | solution.py:70
  56.0 1.1 collective-permute-start.14
  57.2 0.1 copy.8
  57.3 0.1 reshape.19.links
  57.4 0.0 copy-start.4
  57.4 0.9 copy-done.4
  58.3 0.9 copy-done.6
  59.3 7.6 %faces.2 = (f32[5,4,4,64,128]{4,3,2,1,0:T(8,128)}, f32[5,4,256,128]{3,2,1,0:T(8,128)}, f32[16,2,120,128]{3,2,1,0:T(8,128)}, f32[16,120,128]{2,1,0:T(8,128)}) custom-call(s32[6]{0:T(128)S(1)} %reshape_squeeze.3.plan, s32[1]{0:T(128)} %bitcast.place, s32[256]{0:T(256)S(1)} %reshape.19.links, f32[4,5,4,64,128]{4,3,2,1,0:T(8,128)} %bitcast.19, ...), custom_call_target="tpu_custom_call" | custom-call | tf_op jit(solution)/shard_map/faces/pallas_call | solution.py:220
  66.9 2.6 %z_ends.1 = (f32[4,5,3,8,128]{4,3,2,1,0:T(8,128)S(1)}, f32[4,5,3,8,128]{4,3,2,1,0:T(8,128)S(1)}) custom-call(s32[6]{0:T(128)S(1)} %reshape_squeeze.3.plan, f32[4,5,4,64,128]{4,3,2,1,0:T(8,128)} %bitcast.20, f32[5,4,4,64,128]{4,3,2,1,0:T(8,128)} %get-tuple-element.37.patches.refs_7_, f32[2,4,64,128]{3,2,1,0:T(8,128)S(1)} %collective-permute-done.refs_0_, ...), custom_call_target="tpu_custom_call" | custom-call | tf_op jit(solution)/shard_map/z_ends/pallas_call | solution.py:265
  69.5 2.9 %collective-permute-start.16 = (f32[4,5,3,8,128]{4,3,2,1,0:T(8,128)S(1)}, f32[4,5,3,8,128]{4,3,2,1,0:T(8,128)S(1)}, u32[]{:S(2)}, u32[]{:S(2)}) collective-permute-start(f32[4,5,3,8,128]{4,3,2,1,0:T(8,128)S(1)} %get-tuple-element.46), channel_id=1, source_target_pairs={{1,0},{2,1},{3,2},{4,3},{5,4},{6,5},{7,6},{0,7},{9,8},{10,9},{11,1... | collective-permute-start | bytes 737288 | tf_op jit(solution)/shard_map/ppermute | solution.py:563
  72.4 0.6 collective-permute-start.15
  73.0 5.2 %faces.3 = (f32[5,4,4,64,128]{4,3,2,1,0:T(8,128)}, f32[5,4,256,128]{3,2,1,0:T(8,128)}, f32[16,2,120,128]{3,2,1,0:T(8,128)}, f32[16,120,128]{2,1,0:T(8,128)}) custom-call(s32[6]{0:T(128)S(1)} %reshape_squeeze.3.plan, s32[1]{0:T(128)} %bitcast.place, ...), custom_call_target="tpu_custom_call", output_to_operand_aliasing={{0}: (11, {}), {1}: (12, {}), {2}: (13, {}), {3}: (14, {})} | custom-call | tf_op jit(solution)/shard_map/faces/pallas_call | solution.py:220
  78.2 4.7 %all-to-all-start = ((f32[16,2,120,128]{3,2,1,0:T(8,128)}), f32[16,2,120,128]{3,2,1,0:T(8,128)}, u32[]{:S(2)}, u32[]{:S(2)}) async-start(f32[16,2,120,128]{3,2,1,0:T(8,128)} %get-tuple-element.43), calls=%async_computation | async-start | bytes 3932160 | tf_op jit(solution)/shard_map/all_to_all | solution.py:558
  82.8 5.5 %z_update.1.after.partial_in = f32[5,4,4,64,128]{4,3,2,1,0:T(8,128)S(1)} custom-call(f32[5,4,4,64,128]{4,3,2,1,0:T(8,128)} %get-tuple-element.45.patches_in, f32[4,5,3,8,128]{4,3,2,1,0:T(8,128)S(1)} %collective-permute-done.15.z_below, f32[4,5,3,8,128]{4,3,2,1,0:T(8,128)S(1)} %collective-permute-done.16.z_above), custom_call_target="tpu_custom_call" | custom-call | flops 999999995904 | bytes 10000000000 | tf_op jit(solution)/shard_map/z_update/pallas_call | solution.py:425
  88.4 11.6 %inner.1.inside = f32[5,4,256,128]{3,2,1,0:T(8,128)S(1)} custom-call(f32[5,4,256,128]{3,2,1,0:T(8,128)} %get-tuple-element.42.turned_in, f32[5,4,4,64,128]{4,3,2,1,0:T(8,128)S(1)} %z_update.1.after.partial_in), custom_call_target="tpu_custom_call" | custom-call | flops 999999995904 | bytes 10000000000 | tf_op jit(solution)/shard_map/inner/pallas_call | solution.py:382
  100.0 0.0 copy-start.1
  100.0 1.5 %copy-done.1 = f32[5,4,256,128]{3,2,1,0:T(8,128)} copy-done((f32[5,4,256,128]{3,2,1,0:T(8,128)}, f32[5,4,256,128]{3,2,1,0:T(8,128)S(1)}, u32[]{:S(2)}) %copy-start.1) | copy-done | bytes 2621464
  101.5 10.7 %all-to-all-done.arrived = f32[16,2,120,128]{3,2,1,0:T(8,128)} async-done(((f32[16,2,120,128]{3,2,1,0:T(8,128)}), f32[16,2,120,128]{3,2,1,0:T(8,128)}, u32[]{:S(2)}, u32[]{:S(2)}) %all-to-all-start) | async-done | bytes 1966112 | tf_op jit(solution)/shard_map/all_to_all | solution.py:558
  112.2 1.7 %copy-done.2 = f32[5,4,256,128]{3,2,1,0:T(8,128)S(1)} copy-done((f32[5,4,256,128]{3,2,1,0:T(8,128)S(1)}, f32[5,4,256,128]{3,2,1,0:T(8,128)}, u32[]{:S(2)}) %copy-start.2) | copy-done | bytes 2621464
  113.9 13.1 %outer.1 = f32[4,5,4,64,128]{4,3,2,1,0:T(8,128)} custom-call(s32[1]{0:T(128)} %bitcast.place, s32[256]{0:T(256)S(1)} %reshape.19.links, f32[5,4,256,128]{3,2,1,0:T(8,128)} %get-tuple-element.42.turned_in, f32[16,2,120,128]{3,2,1,0:T(8,128)} %all-to-all-done.arrived, f32[16,120,128]{2,1,0:T(8,128)} %get-tuple-element.44.own_items, ...), custom_call_target="tpu_custom_call" | custom-call | tf_op jit(solution)/shard_map/outer/pallas_call | solution.py:519
  (22 shorter events, 0.1 us)
Async XLA Ops:
  0.0 0.7 copy-start
  3.0 11.2 %collective-permute-start.2 = (f32[2,4,64,128]{3,2,1,0:T(8,128)S(1)}, f32[2,4,64,128]{3,2,1,0:T(8,128)S(1)}, u32[]{:S(2)}, u32[]{:S(2)}) collective-permute-start(f32[2,4,64,128]{3,2,1,0:T(8,128)S(1)} %get-tuple-element.28), channel_id=1, source_target_pairs={{0,64},{32,96},{64,0},{96,32},{1,65},{33,97},{65,1},{97,33},{2,66}... | collective-permute-start | bytes 786440 | tf_op jit(solution)/shard_map/ppermute | solution.py:83
  7.0 15.6 %collective-permute-start.1 = (f32[2,4,64,128]{3,2,1,0:T(8,128)S(1)}, f32[2,4,64,128]{3,2,1,0:T(8,128)S(1)}, u32[]{:S(2)}, u32[]{:S(2)}) collective-permute-start(f32[2,4,64,128]{3,2,1,0:T(8,128)S(1)} %get-tuple-element.27), channel_id=1, source_target_pairs={{0,64},{32,96},{64,0},{96,32},{1,65},{33,97},{65,1},{97,33},{2,66}... | collective-permute-start | bytes 786440 | tf_op jit(solution)/shard_map/ppermute | solution.py:83
  7.1 21.2 %collective-permute-start.4 = (f32[2,4,64,128]{3,2,1,0:T(8,128)S(1)}, f32[2,4,64,128]{3,2,1,0:T(8,128)S(1)}, u32[]{:S(2)}, u32[]{:S(2)}) collective-permute-start(f32[2,4,64,128]{3,2,1,0:T(8,128)S(1)} %get-tuple-element.30), channel_id=1, source_target_pairs={{0,64},{32,96},{64,0},{96,32},{1,65},{33,97},{65,1},{97,33},{2,66}... | collective-permute-start | bytes 786440 | tf_op jit(solution)/shard_map/ppermute | solution.py:83
  15.8 12.5 %collective-permute-start.5 = (f32[2,4,64,128]{3,2,1,0:T(8,128)S(1)}, f32[2,4,64,128]{3,2,1,0:T(8,128)S(1)}, u32[]{:S(2)}, u32[]{:S(2)}) collective-permute-start(f32[2,4,64,128]{3,2,1,0:T(8,128)S(1)} %pack.9.refs_1_), channel_id=1, source_target_pairs={{0,16},{8,24},{16,0},{24,8},{1,17},{9,25},{17,1},{25,9},{2,18},{10... | collective-permute-start | bytes 786440 | tf_op jit(solution)/shard_map/ppermute | solution.py:83
  18.9 14.5 %collective-permute-start = (f32[2,4,64,128]{3,2,1,0:T(8,128)S(1)}, f32[2,4,64,128]{3,2,1,0:T(8,128)S(1)}, u32[]{:S(2)}, u32[]{:S(2)}) collective-permute-start(f32[2,4,64,128]{3,2,1,0:T(8,128)S(1)} %get-tuple-element.26), channel_id=1, source_target_pairs={{0,64},{32,96},{64,0},{96,32},{1,65},{33,97},{65,1},{97,33},{2,66}... | collective-permute-start | bytes 786440 | tf_op jit(solution)/shard_map/ppermute | solution.py:83
  24.4 9.1 %collective-permute-start.3 = (f32[2,4,64,128]{3,2,1,0:T(8,128)S(1)}, f32[2,4,64,128]{3,2,1,0:T(8,128)S(1)}, u32[]{:S(2)}, u32[]{:S(2)}) collective-permute-start(f32[2,4,64,128]{3,2,1,0:T(8,128)S(1)} %pack.10.refs_3_), channel_id=1, source_target_pairs={{0,16},{8,24},{16,0},{24,8},{1,17},{9,25},{17,1},{25,9},{2,18},{10... | collective-permute-start | bytes 786440 | tf_op jit(solution)/shard_map/ppermute | solution.py:83
  24.6 14.4 %collective-permute-start.7 = (f32[2,4,64,128]{3,2,1,0:T(8,128)S(1)}, f32[2,4,64,128]{3,2,1,0:T(8,128)S(1)}, u32[]{:S(2)}, u32[]{:S(2)}) collective-permute-start(f32[2,4,64,128]{3,2,1,0:T(8,128)S(1)} %get-tuple-element.29.refs_1_), channel_id=1, source_target_pairs={{0,64},{32,96},{64,0},{96,32},{1,65},{33,97},{65,1},{97,33},{2,66}... | collective-permute-start | bytes 786440 | tf_op jit(solution)/shard_map/ppermute | solution.py:83
  28.3 7.0 %copy-start.3 = (f32[2,4,64,128]{3,2,1,0:T(8,128)}, f32[2,4,64,128]{3,2,1,0:T(8,128)S(1)}, u32[]{:S(2)}) copy-start(f32[2,4,64,128]{3,2,1,0:T(8,128)S(1)} %collective-permute-done.5.refs_2_.refs_1_) | copy-start | bytes 786436
  30.1 9.0 %collective-permute-start.8 = (f32[2,4,64,128]{3,2,1,0:T(8,128)S(1)}, f32[2,4,64,128]{3,2,1,0:T(8,128)S(1)}, u32[]{:S(2)}, u32[]{:S(2)}) collective-permute-start(f32[2,4,64,128]{3,2,1,0:T(8,128)S(1)} %get-tuple-element.33), channel_id=1, source_target_pairs={{0,16},{8,24},{16,0},{24,8},{1,17},{9,25},{17,1},{25,9},{2,18},{10... | collective-permute-start | bytes 786440 | tf_op jit(solution)/shard_map/ppermute | solution.py:83
  30.7 8.4 %collective-permute-start.9 = (f32[2,4,64,128]{3,2,1,0:T(8,128)S(1)}, f32[2,4,64,128]{3,2,1,0:T(8,128)S(1)}, u32[]{:S(2)}, u32[]{:S(2)}) collective-permute-start(f32[2,4,64,128]{3,2,1,0:T(8,128)S(1)} %get-tuple-element.31.refs_3_), channel_id=1, source_target_pairs={{0,4},{1,5},{2,6},{3,7},{4,0},{5,1},{6,2},{7,3},{8,12},{9,13},{10,... | collective-permute-start | bytes 786440 | tf_op jit(solution)/shard_map/ppermute | solution.py:83
  33.5 7.3 %copy-start.5 = (f32[2,4,64,128]{3,2,1,0:T(8,128)}, f32[2,4,64,128]{3,2,1,0:T(8,128)S(1)}, u32[]{:S(2)}) copy-start(f32[2,4,64,128]{3,2,1,0:T(8,128)S(1)} %collective-permute-done.3.refs_2_.refs_4_) | copy-start | bytes 786436
  35.3 12.5 %collective-permute-start.6 = (f32[2,4,64,128]{3,2,1,0:T(8,128)S(1)}, f32[2,4,64,128]{3,2,1,0:T(8,128)S(1)}, u32[]{:S(2)}, u32[]{:S(2)}) collective-permute-start(f32[2,4,64,128]{3,2,1,0:T(8,128)S(1)} %get-tuple-element.32), channel_id=1, source_target_pairs={{0,16},{8,24},{16,0},{24,8},{1,17},{9,25},{17,1},{25,9},{2,18},{10... | collective-permute-start | bytes 786440 | tf_op jit(solution)/shard_map/ppermute | solution.py:83
  38.0 9.8 %collective-permute-start.10 = (f32[2,4,64,128]{3,2,1,0:T(8,128)S(1)}, f32[2,4,64,128]{3,2,1,0:T(8,128)S(1)}, u32[]{:S(2)}, u32[]{:S(2)}) collective-permute-start(f32[2,4,64,128]{3,2,1,0:T(8,128)S(1)} %get-tuple-element.34.refs_3_), channel_id=1, source_target_pairs={{0,4},{1,5},{2,6},{3,7},{4,0},{5,1},{6,2},{7,3},{8,12},{9,13},{10,... | collective-permute-start | bytes 786440 | tf_op jit(solution)/shard_map/ppermute | solution.py:83
  40.8 8.6 %collective-permute-start.12 = (f32[2,4,64,128]{3,2,1,0:T(8,128)S(1)}, f32[2,4,64,128]{3,2,1,0:T(8,128)S(1)}, u32[]{:S(2)}, u32[]{:S(2)}) collective-permute-start(f32[2,4,64,128]{3,2,1,0:T(8,128)S(1)} %get-tuple-element.36), channel_id=1, source_target_pairs={{0,16},{8,24},{16,0},{24,8},{1,17},{9,25},{17,1},{25,9},{2,18},{10... | collective-permute-start | bytes 786440 | tf_op jit(solution)/shard_map/ppermute | solution.py:83
  44.8 9.7 %collective-permute-start.13 = (f32[2,4,64,128]{3,2,1,0:T(8,128)S(1)}, f32[2,4,64,128]{3,2,1,0:T(8,128)S(1)}, u32[]{:S(2)}, u32[]{:S(2)}) collective-permute-start(f32[2,4,64,128]{3,2,1,0:T(8,128)S(1)} %get-tuple-element.35.refs_2_), channel_id=1, source_target_pairs={{0,4},{1,5},{2,6},{3,7},{4,0},{5,1},{6,2},{7,3},{8,12},{9,13},{10,... | collective-permute-start | bytes 786440 | tf_op jit(solution)/shard_map/ppermute | solution.py:83
  49.2 7.9 %copy-start.7 = (s32[64,4]{0,1:T(4,128)S(1)}, s32[64,4]{0,1:T(4,128)}, u32[]{:S(2)}) copy-start(s32[64,4]{0,1:T(4,128)} %param.5) | copy-start | bytes 3076
  49.2 17.6 %collective-permute-start.11 = (f32[2,4,64,128]{3,2,1,0:T(8,128)S(1)}, f32[2,4,64,128]{3,2,1,0:T(8,128)}, u32[]{:S(2)}, u32[]{:S(2)}) collective-permute-start(f32[2,4,64,128]{3,2,1,0:T(8,128)S(1)} %pack.14.refs_2_), channel_id=1, source_target_pairs={{0,4},{1,5},{2,6},{3,7},{4,0},{5,1},{6,2},{7,3},{8,12},{9,13},{10,... | collective-permute-start | bytes 786440 | tf_op jit(solution)/shard_map/ppermute | solution.py:83
  56.0 10.8 %collective-permute-start.14 = (f32[2,4,64,128]{3,2,1,0:T(8,128)S(1)}, f32[2,4,64,128]{3,2,1,0:T(8,128)}, u32[]{:S(2)}, u32[]{:S(2)}) collective-permute-start(f32[2,4,64,128]{3,2,1,0:T(8,128)S(1)} %pack.15.refs_9_), channel_id=1, source_target_pairs={{0,4},{1,5},{2,6},{3,7},{4,0},{5,1},{6,2},{7,3},{8,12},{9,13},{10,... | collective-permute-start | bytes 786440 | tf_op jit(solution)/shard_map/ppermute | solution.py:83
  57.4 1.0 copy-start.4
  58.3 0.9 copy-start.6
  69.5 13.3 %collective-permute-start.16 = (f32[4,5,3,8,128]{4,3,2,1,0:T(8,128)S(1)}, f32[4,5,3,8,128]{4,3,2,1,0:T(8,128)S(1)}, u32[]{:S(2)}, u32[]{:S(2)}) collective-permute-start(f32[4,5,3,8,128]{4,3,2,1,0:T(8,128)S(1)} %get-tuple-element.46), channel_id=1, source_target_pairs={{1,0},{2,1},{3,2},{4,3},{5,4},{6,5},{7,6},{0,7},{9,8},{10,9},{11,1... | collective-permute-start | bytes 737288 | tf_op jit(solution)/shard_map/ppermute | solution.py:563
  72.4 10.4 %collective-permute-start.15 = (f32[4,5,3,8,128]{4,3,2,1,0:T(8,128)S(1)}, f32[4,5,3,8,128]{4,3,2,1,0:T(8,128)S(1)}, u32[]{:S(2)}, u32[]{:S(2)}) collective-permute-start(f32[4,5,3,8,128]{4,3,2,1,0:T(8,128)S(1)} %get-tuple-element.38.refs_6_), channel_id=1, source_target_pairs={{0,1},{1,2},{2,3},{3,4},{4,5},{5,6},{6,7},{7,0},{8,9},{9,10},{10,1... | collective-permute-start | bytes 737288 | tf_op jit(solution)/shard_map/ppermute | solution.py:562
  78.2 34.0 %all-to-all-start = ((f32[16,2,120,128]{3,2,1,0:T(8,128)}), f32[16,2,120,128]{3,2,1,0:T(8,128)}, u32[]{:S(2)}, u32[]{:S(2)}) async-start(f32[16,2,120,128]{3,2,1,0:T(8,128)} %get-tuple-element.43), calls=%async_computation | async-start | bytes 3932160 | tf_op jit(solution)/shard_map/all_to_all | solution.py:558
  100.0 1.5 %copy-start.1 = (f32[5,4,256,128]{3,2,1,0:T(8,128)}, f32[5,4,256,128]{3,2,1,0:T(8,128)S(1)}, u32[]{:S(2)}) copy-start(f32[5,4,256,128]{3,2,1,0:T(8,128)S(1)} %inner.1.inside) | copy-start | bytes 7864324
  112.2 1.7 %copy-start.2 = (f32[5,4,256,128]{3,2,1,0:T(8,128)S(1)}, f32[5,4,256,128]{3,2,1,0:T(8,128)}, u32[]{:S(2)}) copy-start(f32[5,4,256,128]{3,2,1,0:T(8,128)} %copy-done.1) | copy-start | bytes 7864324

commit v2 on v1

v2 whole, which is shorter than its diff:
```python
import functools

import jax
import jax.numpy as jnp
from jax import lax
from jax.experimental import pallas as pl
from jax.experimental.pallas import tpu as pltpu
from jax.sharding import PartitionSpec as P

GAMMA = 5.0 / 3.0
DT_DX = 0.02
EDGE = 32
GHOST = 3
SLOTS = 4
LAYERS = 4
FIELDS = 5
PLANE = 16
LINKS = 16
GROUPS = ((0, 1, 2), (3, 4))
ITEM_ROWS = FIELDS * GHOST * 8
PATCH_SHAPE = (FIELDS, SLOTS, LAYERS, 64, 128)
PITCH = EDGE + 8
TURNED_SHAPE = (FIELDS, 4, 8 * PITCH, 128)
RIM = GHOST + 2
RIM_SHAPE = (2, 2, RIM, FIELDS, 4, 8, 128)
MIB = 1024 * 1024

F32 = jnp.float32
ANY = pl.BlockSpec(memory_space=pl.ANY)
HBM = pl.BlockSpec(memory_space=pltpu.HBM)
SMEM = pl.BlockSpec(memory_space=pltpu.SMEM)
VMEM = pl.BlockSpec(memory_space=pltpu.VMEM)
LONG = pl.CostEstimate(flops=10**12, bytes_accessed=10**10, transcendentals=10**10)
CHUNKS = (4, 4, 4, 4, 4)
STARTS = tuple(sum(CHUNKS[:c]) for c in range(len(CHUNKS)))


def held(x):
    return pltpu.with_memory_space_constraint(x, pltpu.HBM)


def start_copy(plan, slot, rounds, chunk, cells, received, target, sem, first=0, count=None):
    count = count or CHUNKS[chunk]
    taken = jnp.bool_(False)
    for r in reversed(range(rounds)):
        for j in range(2):
            hit = jnp.logical_and(plan[2 * r + j] == slot, jnp.logical_not(taken))

            @pl.when(hit)
            def _(r=r, j=j):
                source = received[r].at[j, pl.ds(first, count)]
                pltpu.make_async_copy(source, target, sem).start()

            taken = jnp.logical_or(taken, hit)

    @pl.when(jnp.logical_not(taken))
    def _():
        source = cells.at[slot, pl.ds(STARTS[chunk] + first, count)]
        pltpu.make_async_copy(source, target, sem).start()


def wait_copy(cells, count, target, sem):
    pltpu.make_async_copy(cells.at[0, pl.ds(0, count)], target, sem).wait()


def pack_kernel(sends, taken, plan, cells, *refs):
    received, refs = refs[:taken], refs[-len(sends) - 1 :]
    outs, sems = refs[:-1], refs[-1]
    at = 0
    for n, (r, c) in enumerate(sends):
        got = received[at : at + r]
        at += r
        for j in range(2):
            start_copy(plan, plan[2 * r + j], r, c, cells, got, outs[n].at[j], sems.at[n, j])
    for n, (r, c) in enumerate(sends):
        for j in range(2):
            wait_copy(cells, CHUNKS[c], outs[n].at[j], sems.at[n, j])


def pack(sends, plan, cells, received, after):
    return pl.pallas_call(
        functools.partial(pack_kernel, sends, len(received)),
        out_shape=[jax.ShapeDtypeStruct((2, CHUNKS[c], 64, 128), F32) for _, c in sends],
        in_specs=[SMEM, HBM] + [ANY] * (len(received) + len(after)),
        out_specs=[VMEM] * len(sends),
        scratch_shapes=[pltpu.SemaphoreType.DMA((len(sends), 2))],
        compiler_params=pltpu.CompilerParams(vmem_limit_bytes=4 * MIB),
        name="pack",
    )(plan, held(cells), *received, *after)


def swapped(block, axis):
    count = lax.axis_size(axis)
    return lax.ppermute(block, axis, [(i, i ^ (count // 2)) for i in range(count)])


WAVES = (
    ([(0, 0), (0, 1), (0, 2), (0, 3), (0, 4)], []),
    ([(1, 0)], []),
    ([(1, 1)], []),
    ([(1, 2), (2, 0)], []),
    ([(1, 3), (2, 1)], []),
    ([(1, 4), (2, 2)], [(2, 0)]),
    ([(2, 3)], [(2, 1)]),
    ([(2, 4)], [(2, 2)]),
)


def migrate(plan, cells):
    got, last = {}, []
    for sends, awaited in WAVES:
        received = [got[i, c] for r, c in sends for i in range(r)]
        after = list(last[-1:]) + [got[at] for at in awaited]
        last = pack(sends, plan, cells, received, after)
        for (r, c), block in zip(sends, last):
            got[r, c] = swapped(block, ("gx", "gy", "gz")[r])
    return got, last[-1]


def primitives(u):
    inv = 1.0 / u[0]
    v = [u[i] * inv for i in (1, 2, 3)]
    kinetic = u[1] * v[0] + u[2] * v[1] + u[3] * v[2]
    return [u[0]] + v + [(GAMMA - 1.0) * (u[4] - 0.5 * kinetic)]


def block_transpose(b):
    lane = lax.broadcasted_iota(jnp.int32, b[0].shape, 1)
    low = lane < 64
    even = (lane & 32) == 0

    def rolled(x, shift):
        return pltpu.roll(x, shift, 1)

    a0 = jnp.where(low, b[0], rolled(b[2], 64))
    a2 = jnp.where(low, rolled(b[0], 64), b[2])
    a1 = jnp.where(low, b[1], rolled(b[3], 64))
    a3 = jnp.where(low, rolled(b[1], 64), b[3])
    return [
        jnp.where(even, a0, rolled(a1, 32)),
        jnp.where(even, rolled(a0, 96), a1),
        jnp.where(even, a2, rolled(a3, 32)),
        jnp.where(even, rolled(a2, 96), a3),
    ]


def y_rows(i, g):
    return pl.ds(pl.multiple_of((i % 8) * PITCH + 8 * g, 8), 8)


def turned_rows(direction, i, g):
    if direction == 0:
        return g, pl.ds(i, 8, stride=PITCH)
    return i // 8, y_rows(i, g)


def flat(turned, f):
    rows = [turned[f, g, pl.ds(y * PITCH, EDGE), :] for g in range(4) for y in range(8)]
    return jnp.concatenate(rows, axis=0)


def pieces(f):
    out = []
    for c, start in enumerate(STARTS):
        low, high = max(start, f * LAYERS), min(start + CHUNKS[c], (f + 1) * LAYERS)
        if low < high:
            out.append((c, low - start, high - low, low - f * LAYERS))
    return out


def chunks_of(fields):
    return sorted({c for f in fields for c, _, _, _ in pieces(f)})


def faces_kernel(fields, plan, place, links, cells, *refs):
    count, first, last = len(fields), fields[0], fields[0] > 0
    chunks = chunks_of(fields)
    received = refs[: 3 * len(chunks)]
    refs = refs[3 * len(chunks) + 1 + 4 * last :]
    patches_out, turned_out, send, own_items = refs[:4]
    patches, turned, items, sems, item_sems, out_sems = refs[-6:]
    parts = []
    for n, f in enumerate(fields):
        for p, (c, start, size, layer) in enumerate(pieces(f)):
            got = received[3 * chunks.index(c) : 3 * chunks.index(c) + 3]
            for k in range(SLOTS):
                target, sem = patches.at[n, k, pl.ds(layer, size)], sems.at[n, k, p]
                start_copy(plan, k, 3, c, cells, got, target, sem, start, size)
                parts.append((n, size, target, sem))
    loads = []
    if last:
        z_first, z_last, ends, end_sems = refs[4:8]
        for end, c in ((0, 0), (1, LAYERS - 1)):
            source = patches_out.at[pl.ds(0, first), :, c]
            loads.append(pltpu.make_async_copy(source, ends.at[end], end_sems.at[end]))
    for load in loads:
        load.start()

    mine = pl.ds(first, count)
    outs = [
        pltpu.make_async_copy(patches, patches_out.at[mine], out_sems.at[0]),
        pltpu.make_async_copy(turned, turned_out.at[mine], out_sems.at[1]),
    ]
    for n, f in enumerate(fields):
        for at, size, target, sem in parts:
            if at == n:
                wait_copy(cells, size, target, sem)
        columns = [
            jnp.concatenate(
                [patches[n, k, c, pl.ds(8 * b, 8), :] for k in range(SLOTS) for c in range(LAYERS)],
                axis=0,
            )
            for b in range(8)
        ]
        rows = jnp.transpose(jnp.concatenate(columns, axis=1))
        for y in range(EDGE):
            turned[n, y // 8, pl.ds(y % 8 * PITCH, EDGE), :] = rows[y * EDGE : (y + 1) * EDGE]
    for copy in outs:
        copy.start()

    me = place[0]
    owners = [links[me * LINKS + i] // SLOTS for i in range(LINKS)]
    rows = pl.ds(first * GHOST * 8, count * GHOST * 8)
    for side in range(4):
        start = EDGE - GHOST if side % 2 else 0
        blocks = []
        for g in range(4):
            tiles = []
            for n in range(count):
                for layer in range(start, start + GHOST):
                    block, where = turned_rows(side // 2, layer, g)
                    tiles.append(turned[n, block, where, :])
            blocks.append(jnp.concatenate(tiles, axis=0))
        for k, block in enumerate(block_transpose(blocks)):
            items[k * 4 + side] = block
        for i in range(side, LINKS, 4):
            rank = jnp.int32(0)
            for j in range(i):
                rank = rank + (owners[j] == owners[i]).astype(jnp.int32)
            rank = jnp.minimum(rank, 1)

            @pl.when(owners[i] != me)
            def _(i=i, rank=rank):
                target = send.at[owners[i], rank, rows]
                pltpu.make_async_copy(items.at[i], target, item_sems.at[i]).start()

            @pl.when(owners[i] == me)
            def _(i=i):
                target = own_items.at[i, rows]
                pltpu.make_async_copy(items.at[i], target, item_sems.at[i]).start()

    for load in loads:
        load.wait()
    if last:
        for f in range(FIELDS):
            for k in range(SLOTS):
                if f < first:
                    head, tail = ends.at[0, f, k], ends.at[1, f, k]
                else:
                    head, tail = patches.at[f - first, k, 0], patches.at[f - first, k, LAYERS - 1]
                for layer in range(GHOST):
                    z_first[k, f, layer] = head[pl.ds(layer, 8, stride=8), :]
                    z_last[k, f, layer] = tail[pl.ds(8 - GHOST + layer, 8, stride=8), :]

    for i in range(LINKS):
        pltpu.make_async_copy(items.at[i], own_items.at[i, rows], item_sems.at[i]).wait()
    for copy in outs:
        copy.wait()


def faces(fields, plan, place, links, cells, received, after, carried):
    count, first, last = len(fields), fields[0], fields[0] > 0
    held_chunks = 3 * len(chunks_of(fields))
    z_shape = jax.ShapeDtypeStruct((SLOTS, FIELDS, GHOST, 8, 128), F32)
    scratch = [
        pltpu.VMEM((count,) + PATCH_SHAPE[1:], F32),
        pltpu.VMEM((count,) + TURNED_SHAPE[1:], F32),
        pltpu.VMEM((LINKS, count * GHOST * 8, 128), F32),
        pltpu.SemaphoreType.DMA((count, SLOTS, 2)),
        pltpu.SemaphoreType.DMA((LINKS,)),
        pltpu.SemaphoreType.DMA((2,)),
    ]
    if last:
        scratch = [
            pltpu.VMEM((2, first, SLOTS, 64, 128), F32),
            pltpu.SemaphoreType.DMA((2,)),
        ] + scratch
    inputs = [held(cells)] + list(received) + [after] + [held(x) for x in carried]
    return pl.pallas_call(
        functools.partial(faces_kernel, fields),
        out_shape=[
            pltpu.HBM(PATCH_SHAPE, F32),
            pltpu.HBM(TURNED_SHAPE, F32),
            pltpu.HBM((PLANE, 2, ITEM_ROWS, 128), F32),
            pltpu.HBM((LINKS, ITEM_ROWS, 128), F32),
        ]
        + [z_shape] * (2 * last),
        in_specs=[SMEM] * 3 + [HBM] + [ANY] * (held_chunks + 1) + [HBM] * len(carried),
        out_specs=[HBM] * 4 + [VMEM] * (2 * last),
        scratch_shapes=scratch,
        input_output_aliases={held_chunks + 5 + i: i for i in range(len(carried))},
        compiler_params=pltpu.CompilerParams(vmem_limit_bytes=16 * MIB),
        cost_estimate=LONG if last else None,
        name="faces",
    )(plan, place, links, *inputs)


def clamped(x, y):
    return jnp.minimum(jnp.maximum(x, jnp.minimum(y, 0.0)), jnp.maximum(y, 0.0))


def euler_terms(w, normal):
    density, velocity, pressure = w[0], w[1:4], w[4]
    speed = velocity[normal]
    momentum = [density * v for v in velocity]
    kinetic = momentum[0] * velocity[0] + momentum[1] * velocity[1] + momentum[2] * velocity[2]
    energy = 1.5 * pressure + 0.5 * kinetic
    flux = [momentum[normal]]
    for i in range(3):
        term = momentum[i] * speed
        flux.append(term + pressure if i == normal else term)
    flux.append((energy + pressure) * speed)
    stiff = GAMMA * pressure
    signal = jnp.abs(speed) + stiff * lax.rsqrt(stiff * density)
    return [density] + momentum + [energy], flux, signal


def sweep(get, put, normal, first, last):
    w, d, a, b = {}, {}, {}, {}
    prev, left = None, None
    start = first - 2
    for i in range(start, last + 4):
        w[i] = get(i)
        if i == start:
            continue
        d[i - 1] = [hi - lo for hi, lo in zip(w[i], w[i - 1])]
        m = i - 2
        if m <= start:
            continue
        a[m] = [
            clamped(0.5 * mid - (1.0 / 12.0) * (up - down), mid)
            for down, mid, up in zip(d[m - 1], d[m], d[m + 1])
        ]
        b[m + 1] = [mid - part for mid, part in zip(d[m], a[m])]
        if m < first:
            continue
        if m > first:
            lower = [v - clamped(y, 2.0 * x) for v, x, y in zip(w[m], a[m], b[m])]
            right = euler_terms(lower, normal)
            fastest = jnp.maximum(left[2], right[2])
            flux = [
                gl + gr - fastest * (ur - ul)
                for gl, gr, ul, ur in zip(left[1], right[1], left[0], right[0])
            ]
            if prev is not None:
                put(m - 1, [new - old for new, old in zip(flux, prev)])
            elif m > 0:
                put(m - 1, flux)
            prev = flux
        if m <= last:
            upper = [v + clamped(x, 2.0 * y) for v, x, y in zip(w[m], a[m], b[m])]
            left = euler_terms(upper, normal)
    if last + 1 < EDGE:
        put(last + 1, [-v for v in prev])


def inner_kernel(turned_in, patches_in, z_below, z_above, out, rim_out, *scratch):
    turned, patches, change, partial, rim, sems, out_sems = scratch
    loads = [
        pltpu.make_async_copy(patches_in.at[:, k], patches.at[:, k], sems.at[k])
        for k in range(SLOTS)
    ]
    loads.append(pltpu.make_async_copy(turned_in, turned, sems.at[SLOTS]))
    for load in loads:
        load.start()
    for load in loads[:SLOTS]:
        load.wait()

    def z_sweep(k, carry):
        def get(i):
            if i < 0:
                u = [z_below[k, f, i + GHOST] for f in range(FIELDS)]
            elif i >= EDGE:
                u = [z_above[k, f, i - EDGE] for f in range(FIELDS)]
            else:
                rows = pl.ds(i % 8, 8, stride=8)
                u = [patches[f, k, i // 8, rows, :] for f in range(FIELDS)]
            return primitives(u)

        def put(i, values):
            rows = pl.ds(i % 8, 8, stride=8)
            for f in range(FIELDS):
                partial[f, k, i // 8, rows, :] = (
                    patches[f, k, i // 8, rows, :] - (0.5 * DT_DX) * values[f]
                )

        sweep(get, put, 2, -1, EDGE - 1)
        return carry

    lax.fori_loop(0, SLOTS, z_sweep, 0)
    loads[SLOTS].wait()

    def plane_sweep(direction, g, put):
        def get(i):
            block, rows = turned_rows(direction, i, g)
            w = primitives([turned[f, block, rows, :] for f in range(FIELDS)])
            end, at = (0, i) if i < RIM else (1, i - EDGE + RIM)
            if 0 <= at < RIM:
                for f in range(FIELDS):
                    rim[direction, end, at, f, g] = w[f]
            return w

        sweep(get, put, direction, 2, EDGE - 4)

    def y_sweep(g, carry):
        def put(i, values):
            block, rows = turned_rows(1, i, g)
            for f in range(FIELDS):
                change[f, block, rows, :] = values[f]

        for i in (0, 1, EDGE - 2, EDGE - 1):
            put(i, [jnp.zeros((8, 128), F32)] * FIELDS)
        plane_sweep(1, g, put)
        return carry

    lax.fori_loop(0, 4, y_sweep, 0)

    def x_sweep(g, carry):
        def put(i, values):
            block, rows = turned_rows(0, i, g)
            for f in range(FIELDS):
                change[f, block, rows, :] = change[f, block, rows, :] + values[f]

        plane_sweep(0, g, put)
        return carry

    lax.fori_loop(0, 4, x_sweep, 0)
    rim_copy = pltpu.make_async_copy(rim, rim_out, out_sems.at[FIELDS])
    rim_copy.start()
    copies = []
    for f in range(FIELDS):
        add_turned(change, partial, f, partial.at[f])
        copies.append(pltpu.make_async_copy(partial.at[f], out.at[f], out_sems.at[f]))
        copies[f].start()
    for copy in copies + [rim_copy]:
        copy.wait()


def add_turned(change, partial, f, result):
    back = (0.5 * DT_DX) * jnp.transpose(flat(change, f))
    for k in range(SLOTS):
        for c in range(LAYERS):
            n = (k * LAYERS + c) * 8
            for b in range(8):
                rows = pl.ds(8 * b, 8)
                result[k, c, rows, :] = (
                    partial[f, k, c, rows, :] - back[n : n + 8, 128 * b : 128 * (b + 1)]
                )


def inner(turned, patches, z_below, z_above):
    return pl.pallas_call(
        inner_kernel,
        out_shape=[pltpu.HBM(PATCH_SHAPE, F32), pltpu.HBM(RIM_SHAPE, F32)],
        in_specs=[HBM, HBM, VMEM, VMEM],
        out_specs=[HBM, HBM],
        scratch_shapes=[
            pltpu.VMEM(TURNED_SHAPE, F32),
            pltpu.VMEM(PATCH_SHAPE, F32),
            pltpu.VMEM(TURNED_SHAPE, F32),
            pltpu.VMEM(PATCH_SHAPE, F32),
            pltpu.VMEM(RIM_SHAPE, F32),
            pltpu.SemaphoreType.DMA((SLOTS + 1,)),
            pltpu.SemaphoreType.DMA((FIELDS + 1,)),
        ],
        compiler_params=pltpu.CompilerParams(vmem_limit_bytes=24 * MIB),
        cost_estimate=LONG,
        name="inner",
    )(held(turned), held(patches), z_below, z_above)


def outer_kernel(place, links, rim_in, arrived, own_items, partial_in, out, *scratch):
    rim, items, ghosts, change, partial, result, item_sems, sems, out_sems = scratch
    me = place[0]
    for i in range(LINKS):
        entry = links[me * LINKS + i]
        owner = entry // SLOTS
        source = (entry % SLOTS) * 4 + (i % 4 ^ 1)
        rank = jnp.int32(0)
        for j in range(LINKS - 1):
            same = jnp.logical_and(links[owner * LINKS + j] // SLOTS == me, j < source)
            rank = rank + same.astype(jnp.int32)
        rank = jnp.minimum(rank, 1)

        @pl.when(owner != me)
        def _(i=i, owner=owner, rank=rank):
            pltpu.make_async_copy(arrived.at[owner, rank], items.at[i], item_sems.at[i]).start()

        @pl.when(owner == me)
        def _(i=i, source=source):
            pltpu.make_async_copy(own_items.at[source], items.at[i], item_sems.at[i]).start()

    loads = [
        pltpu.make_async_copy(rim_in, rim, sems.at[0]),
        pltpu.make_async_copy(partial_in, partial, sems.at[1]),
    ]
    for load in loads:
        load.start()
    change[...] = jnp.zeros(TURNED_SHAPE, F32)
    for i in range(LINKS):
        pltpu.make_async_copy(own_items.at[i], items.at[i], item_sems.at[i]).wait()
    for side in range(4):
        blocks = [items[k * 4 + side] for k in range(SLOTS)]
        for g, block in enumerate(block_transpose(blocks)):
            ghosts[side, g] = block
    loads[0].wait()

    def border(g, carry):
        for direction in (1, 0):

            def get(i):
                if 0 <= i < EDGE:
                    end, at = (0, i) if i < RIM else (1, i - EDGE + RIM)
                    return [rim[direction, end, at, f, g] for f in range(FIELDS)]
                side, layer = (0, i + GHOST) if i < 0 else (1, i - EDGE)
                rows = [pl.ds((f * GHOST + layer) * 8, 8) for f in range(FIELDS)]
                return primitives([ghosts[2 * direction + side, g, at, :] for at in rows])

            def put(i, values):
                block, rows = turned_rows(direction, i, g)
                for f in range(FIELDS):
                    change[f, block, rows, :] = change[f, block, rows, :] + values[f]

            sweep(get, put, direction, -1, 1)
            sweep(get, put, direction, EDGE - 3, EDGE - 1)
        return carry

    lax.fori_loop(0, 4, border, 0)
    loads[1].wait()
    copies = []
    for f in range(FIELDS):
        add_turned(change, partial, f, result.at[f])
        copies.append(pltpu.make_async_copy(result.at[f], out.at[:, f], out_sems.at[f]))
        copies[f].start()
    for copy in copies:
        copy.wait()


def outer(place, links, rim, arrived, own_items, partial):
    return pl.pallas_call(
        outer_kernel,
        out_shape=jax.ShapeDtypeStruct((SLOTS, FIELDS, LAYERS, 64, 128), F32),
        in_specs=[SMEM, SMEM] + [HBM] * 4,
        out_specs=HBM,
        scratch_shapes=[
            pltpu.VMEM(RIM_SHAPE, F32),
            pltpu.VMEM((LINKS, ITEM_ROWS, 128), F32),
            pltpu.VMEM((4, 4, ITEM_ROWS, 128), F32),
            pltpu.VMEM(TURNED_SHAPE, F32),
            pltpu.VMEM(PATCH_SHAPE, F32),
            pltpu.VMEM(PATCH_SHAPE, F32),
            pltpu.SemaphoreType.DMA((LINKS,)),
            pltpu.SemaphoreType.DMA((2,)),
            pltpu.SemaphoreType.DMA((FIELDS,)),
        ],
        compiler_params=pltpu.CompilerParams(vmem_limit_bytes=24 * MIB),
        name="outer",
    )(place, links, held(rim), held(arrived), held(own_items), held(partial))


def local(cells, moves, neighbours):
    tiled = cells.reshape(SLOTS, FIELDS, LAYERS, 8, 8, 128).transpose(0, 1, 2, 4, 3, 5)
    tiled = tiled.reshape(SLOTS, FIELDS * LAYERS, 64, 128)
    plan = moves[lax.axis_index(("gx", "gy", "gz"))].reshape(-1)
    place = lax.axis_index(("gx", "gy")).reshape(1)
    links = neighbours.reshape(-1)

    got, after = migrate(plan, tiled)
    made = ()
    for fields in GROUPS:
        received = [got[r, c] for c in chunks_of(fields) for r in range(3)]
        made = faces(fields, plan, place, links, tiled, received, after, made)
    patches, turned, send, own_items, z_first, z_last = made

    arrived = lax.all_to_all(send, ("gx", "gy"), 0, 0, tiled=True)
    layers = lax.axis_size("gz")
    up = [(i, (i + 1) % layers) for i in range(layers)]
    down = [(j, i) for i, j in up]
    z_below = lax.ppermute(z_last, "gz", up)
    z_above = lax.ppermute(z_first, "gz", down)
    partial, rim = inner(turned, patches, z_below, z_above)
    result = outer(place, links, rim, arrived, own_items, partial)
    result = result.reshape(SLOTS, FIELDS, LAYERS, 8, 8, 128).transpose(0, 1, 2, 4, 3, 5)
    return result.reshape(cells.shape)


def solution(mesh):
    return jax.shard_map(
        local,
        mesh=mesh,
        in_specs=(P(("gx", "gy", "gz"), None, None, None), P(), P()),
        out_specs=P(("gx", "gy", "gz"), None, None, None),
        check_vma=False,
    )
```

time: 128 us -> 117 us (0.914)
  Pallas kernels: 59.2 us -> 46.1 us
  local copies, waits for them, and re-layouts: 6.32 us -> 1.21 us
  waiting for transfers between devices: 19.5 us -> 23.8 us
  starting transfers between devices: 41.8 us -> 44.3 us
    unnamed x17 -> x13, local copies, waits for them, and re-layouts: 5.92 us -> 0.8 us
    pallas_call x3 -> x1, Pallas kernels: 19.8 us -> 14.8 us  [inner(): pl.pallas_call(inner_kernel, out_shape=[pltpu.HBM(PATCH_SHAPE, F32), pltp...]
    pallas_call x1, Pallas kernels: 13.1 us -> 8.73 us  [outer(): pl.pallas_call(outer_kernel, out_shape=jax.ShapeDtypeStruct((SLOTS, FIELD...]
    pallas_call x2, Pallas kernels: 12.7 us -> 10.1 us  [faces(): pl.pallas_call(functools.partial(faces_kernel, fields), out_shape=[pltpu....]
    ppermute x1, starting transfers between devices: 0.57 us -> 3.02 us  [local(): z_below = lax.ppermute(z_last, 'gz', up)]
    ppermute x15, starting transfers between devices: 33.7 us -> 35.4 us  [swapped(): lax.ppermute(block, axis, [(i, i ^ count // 2) for i in range(count)])]
    ppermute x1, waiting for transfers between devices: 0.01 us -> 1.77 us  [local(): z_above = lax.ppermute(z_first, 'gz', down)]
    ppermute x1, starting transfers between devices: 2.94 us -> 1.19 us  [local(): z_above = lax.ppermute(z_first, 'gz', down)]
  transfers between devices with their start and end apart: 18 -> 18, of which waited for: 4 -> 7; matrix products, arithmetic and copies ran while one was open for 0% -> 0% of each run, Pallas kernels for 33% -> 27%
where the time goes in v2:
time: 117 us; the launch traced here: 116 us
  Pallas kernels  46.1 us (39%)
  starting transfers between devices  44.3 us (38%)
  waiting for transfers between devices  23.8 us (20%)
  local copies, waits for them, and re-layouts  1.21 us (1%)
    ppermute x15, starting transfers between devices, swapped(): lax.ppermute(block, axis, [(i, i ^ count // 2) for i in range(count)])  35.4 us
    pallas_call x1, Pallas kernels, inner(): pl.pallas_call(inner_kernel, out_shape=[pltpu.HBM(PATCH_SHAPE, F32), pltp...  14.8 us
    pallas_call x8, Pallas kernels, pack(): pl.pallas_call(functools.partial(pack_kernel, sends, len(received)), out_...  12.5 us
    all_to_all x1, waiting for transfers between devices, local(): arrived = lax.all_to_all(send, ('gx', 'gy'), 0, 0, tiled=True)  12.1 us
    pallas_call x2, Pallas kernels, faces(): pl.pallas_call(functools.partial(faces_kernel, fields), out_shape=[pltpu....  10.1 us
    ppermute x15, waiting for transfers between devices, swapped(): lax.ppermute(block, axis, [(i, i ^ count // 2) for i in range(count)])  9.43 us
    pallas_call x1, Pallas kernels, outer(): pl.pallas_call(outer_kernel, out_shape=jax.ShapeDtypeStruct((SLOTS, FIELD...  8.73 us
    all_to_all x1, starting transfers between devices, local(): arrived = lax.all_to_all(send, ('gx', 'gy'), 0, 0, tiled=True)  4.64 us
  transfers between devices with their start and end apart: 18, of which 7 were waited for; matrix products, arithmetic and copies ran while one was open for 0% of the time, Pallas kernels for 27%

profile of v2, /device:TPU:0, one launch (start us, length us, event | category | flops | bytes accessed | tf_op | source)
XLA Modules:
  0.0 115.8 jit_solution(16860361842706058640)
XLA Ops:
  0.0 0.7 copy-done
  0.7 0.2 dynamic-slice_reduce_fusion
  0.9 0.1 reshape_squeeze.3.plan
  1.0 2.0 %pack.8 = (f32[2,4,64,128]{3,2,1,0:T(8,128)S(1)}, f32[2,4,64,128]{3,2,1,0:T(8,128)S(1)}, f32[2,4,64,128]{3,2,1,0:T(8,128)S(1)}, f32[2,4,64,128]{3,2,1,0:T(8,128)S(1)}, f32[2,4,64,128]{3,2,1,0:T(8,128)S(1)}) custom-call(s32[6]{0:T(128)S(1)} %reshape_squeeze.3.plan, f32[4,20,64,128]{3,2,1,0:T(8,128)} %bitcast.11), custom_call_target="tpu_custom_call" | custom-call | tf_op jit(solution)/shard_map/pack/pallas_call | solution.py:81
  3.0 4.0 %collective-permute-start.2 = (f32[2,4,64,128]{3,2,1,0:T(8,128)S(1)}, f32[2,4,64,128]{3,2,1,0:T(8,128)S(1)}, u32[]{:S(2)}, u32[]{:S(2)}) collective-permute-start(f32[2,4,64,128]{3,2,1,0:T(8,128)S(1)} %get-tuple-element.30), channel_id=1, source_target_pairs={{0,64},{32,96},{64,0},{96,32},{1,65},{33,97},{65,1},{97,33},{2,66}... | collective-permute-start | bytes 786440 | tf_op jit(solution)/shard_map/ppermute | solution.py:94
  7.0 0.1 collective-permute-start.1
  7.1 3.4 %collective-permute-start.4 = (f32[2,4,64,128]{3,2,1,0:T(8,128)S(1)}, f32[2,4,64,128]{3,2,1,0:T(8,128)S(1)}, u32[]{:S(2)}, u32[]{:S(2)}) collective-permute-start(f32[2,4,64,128]{3,2,1,0:T(8,128)S(1)} %get-tuple-element.32), channel_id=1, source_target_pairs={{0,64},{32,96},{64,0},{96,32},{1,65},{33,97},{65,1},{97,33},{2,66}... | collective-permute-start | bytes 786440 | tf_op jit(solution)/shard_map/ppermute | solution.py:94
  10.6 3.6 %collective-permute-done.2.refs_0_.refs_1_ = f32[2,4,64,128]{3,2,1,0:T(8,128)S(1)} collective-permute-done((f32[2,4,64,128]{3,2,1,0:T(8,128)S(1)}, f32[2,4,64,128]{3,2,1,0:T(8,128)S(1)}, u32[]{:S(2)}, u32[]{:S(2)}) %collective-permute-start.2) | collective-permute-done | bytes 262176 | tf_op jit(solution)/shard_map/ppermute | solution.py:94
  14.2 0.9 pack.9.refs_1_
  15.1 4.0 %collective-permute-start.5 = (f32[2,4,64,128]{3,2,1,0:T(8,128)S(1)}, f32[2,4,64,128]{3,2,1,0:T(8,128)S(1)}, u32[]{:S(2)}, u32[]{:S(2)}) collective-permute-start(f32[2,4,64,128]{3,2,1,0:T(8,128)S(1)} %pack.9.refs_1_), channel_id=1, source_target_pairs={{0,16},{8,24},{16,0},{24,8},{1,17},{9,25},{17,1},{25,9},{2,18},{10... | collective-permute-start | bytes 786440 | tf_op jit(solution)/shard_map/ppermute | solution.py:94
  19.1 3.4 %collective-permute-start = (f32[2,4,64,128]{3,2,1,0:T(8,128)S(1)}, f32[2,4,64,128]{3,2,1,0:T(8,128)S(1)}, u32[]{:S(2)}, u32[]{:S(2)}) collective-permute-start(f32[2,4,64,128]{3,2,1,0:T(8,128)S(1)} %get-tuple-element.28), channel_id=1, source_target_pairs={{0,64},{32,96},{64,0},{96,32},{1,65},{33,97},{65,1},{97,33},{2,66}... | collective-permute-start | bytes 786440 | tf_op jit(solution)/shard_map/ppermute | solution.py:94
  22.5 0.9 pack.10.refs_3_
  23.4 1.3 %collective-permute-start.3 = (f32[2,4,64,128]{3,2,1,0:T(8,128)S(1)}, f32[2,4,64,128]{3,2,1,0:T(8,128)S(1)}, u32[]{:S(2)}, u32[]{:S(2)}) collective-permute-start(f32[2,4,64,128]{3,2,1,0:T(8,128)S(1)} %pack.10.refs_3_), channel_id=1, source_target_pairs={{0,16},{8,24},{16,0},{24,8},{1,17},{9,25},{17,1},{25,9},{2,18},{10... | collective-permute-start | bytes 786440 | tf_op jit(solution)/shard_map/ppermute | solution.py:94
  24.7 3.4 %collective-permute-start.7 = (f32[2,4,64,128]{3,2,1,0:T(8,128)S(1)}, f32[2,4,64,128]{3,2,1,0:T(8,128)S(1)}, u32[]{:S(2)}, u32[]{:S(2)}) collective-permute-start(f32[2,4,64,128]{3,2,1,0:T(8,128)S(1)} %get-tuple-element.31.refs_1_), channel_id=1, source_target_pairs={{0,64},{32,96},{64,0},{96,32},{1,65},{33,97},{65,1},{97,33},{2,66}... | collective-permute-start | bytes 786440 | tf_op jit(solution)/shard_map/ppermute | solution.py:94
  28.1 0.0 collective-permute-done.4.refs_0_.refs_1_.refs_6_
  28.1 0.0 collective-permute-done.5.refs_2_.refs_1_
  28.1 1.9 %pack.11 = (f32[2,4,64,128]{3,2,1,0:T(8,128)S(1)}, f32[2,4,64,128]{3,2,1,0:T(8,128)S(1)}) custom-call(s32[6]{0:T(128)S(1)} %reshape_squeeze.3.plan, f32[4,20,64,128]{3,2,1,0:T(8,128)} %bitcast.14, f32[2,4,64,128]{3,2,1,0:T(8,128)S(1)} %collective-permute-done.4.refs_0_.refs_1_.refs_6_, f32[2,4,64,128]{3,2,1,0:T(8,128)S(1)} %collective-permute-done.2.refs_0_.refs_1_, ...), custom_call_target="tpu_custom_call" | custom-call | tf_op jit(solution)/shard_map/pack/pallas_call | solution.py:81
  30.0 0.6 collective-permute-start.8
  30.6 2.6 %collective-permute-start.9 = (f32[2,4,64,128]{3,2,1,0:T(8,128)S(1)}, f32[2,4,64,128]{3,2,1,0:T(8,128)S(1)}, u32[]{:S(2)}, u32[]{:S(2)}) collective-permute-start(f32[2,4,64,128]{3,2,1,0:T(8,128)S(1)} %get-tuple-element.33.refs_3_), channel_id=1, source_target_pairs={{0,4},{1,5},{2,6},{3,7},{4,0},{5,1},{6,2},{7,3},{8,12},{9,13},{10,... | collective-permute-start | bytes 786440 | tf_op jit(solution)/shard_map/ppermute | solution.py:94
  33.2 0.0 collective-permute-done.3.refs_2_.refs_4_
  33.2 1.9 %pack.12 = (f32[2,4,64,128]{3,2,1,0:T(8,128)S(1)}, f32[2,4,64,128]{3,2,1,0:T(8,128)S(1)}) custom-call(s32[6]{0:T(128)S(1)} %reshape_squeeze.3.plan, f32[4,20,64,128]{3,2,1,0:T(8,128)} %bitcast.15, f32[2,4,64,128]{3,2,1,0:T(8,128)S(1)} %collective-permute-done.refs_0_, f32[2,4,64,128]{3,2,1,0:T(8,128)S(1)} %collective-permute-done.1.refs_0_.refs_1_.refs_3_, ...), custom_call_target="tpu_custom_call" | custom-call | tf_op jit(solution)/shard_map/pack/pallas_call | solution.py:81
  35.1 3.2 %collective-permute-start.6 = (f32[2,4,64,128]{3,2,1,0:T(8,128)S(1)}, f32[2,4,64,128]{3,2,1,0:T(8,128)S(1)}, u32[]{:S(2)}, u32[]{:S(2)}) collective-permute-start(f32[2,4,64,128]{3,2,1,0:T(8,128)S(1)} %get-tuple-element.34), channel_id=1, source_target_pairs={{0,16},{8,24},{16,0},{24,8},{1,17},{9,25},{17,1},{25,9},{2,18},{10... | collective-permute-start | bytes 786440 | tf_op jit(solution)/shard_map/ppermute | solution.py:94
  38.4 0.5 collective-permute-start.10
  38.8 0.0 collective-permute-done.7.refs_0_.refs_3_
  38.8 0.0 collective-permute-done.8.refs_2_.refs_7_
  38.8 1.9 %pack.13 = (f32[2,4,64,128]{3,2,1,0:T(8,128)S(1)}, f32[2,4,64,128]{3,2,1,0:T(8,128)S(1)}) custom-call(s32[6]{0:T(128)S(1)} %reshape_squeeze.3.plan, f32[4,20,64,128]{3,2,1,0:T(8,128)} %bitcast.16, f32[2,4,64,128]{3,2,1,0:T(8,128)S(1)} %collective-permute-done.7.refs_0_.refs_3_, f32[2,4,64,128]{3,2,1,0:T(8,128)S(1)} %collective-permute-done.4.refs_0_.refs_1_.refs_6_, ...), custom_call_target="tpu_custom_call" | custom-call | tf_op jit(solution)/shard_map/pack/pallas_call | solution.py:81
  40.7 3.9 %collective-permute-start.12 = (f32[2,4,64,128]{3,2,1,0:T(8,128)S(1)}, f32[2,4,64,128]{3,2,1,0:T(8,128)S(1)}, u32[]{:S(2)}, u32[]{:S(2)}) collective-permute-start(f32[2,4,64,128]{3,2,1,0:T(8,128)S(1)} %get-tuple-element.38), channel_id=1, source_target_pairs={{0,16},{8,24},{16,0},{24,8},{1,17},{9,25},{17,1},{25,9},{2,18},{10... | collective-permute-start | bytes 786440 | tf_op jit(solution)/shard_map/ppermute | solution.py:94
  44.6 3.6 %collective-permute-start.13 = (f32[2,4,64,128]{3,2,1,0:T(8,128)S(1)}, f32[2,4,64,128]{3,2,1,0:T(8,128)S(1)}, u32[]{:S(2)}, u32[]{:S(2)}) collective-permute-start(f32[2,4,64,128]{3,2,1,0:T(8,128)S(1)} %get-tuple-element.37.refs_2_), channel_id=1, source_target_pairs={{0,4},{1,5},{2,6},{3,7},{4,0},{5,1},{6,2},{7,3},{8,12},{9,13},{10,... | collective-permute-start | bytes 786440 | tf_op jit(solution)/shard_map/ppermute | solution.py:94
  48.2 0.5 collective-permute-done.10.refs_3_.refs_5_
  48.6 1.5 %pack.14.refs_2_ = f32[2,4,64,128]{3,2,1,0:T(8,128)S(1)} custom-call(s32[6]{0:T(128)S(1)} %reshape_squeeze.3.plan, f32[4,20,64,128]{3,2,1,0:T(8,128)} %bitcast.17, f32[2,4,64,128]{3,2,1,0:T(8,128)S(1)} %collective-permute-done.refs_0_, f32[2,4,64,128]{3,2,1,0:T(8,128)S(1)} %collective-permute-done.6.refs_1_, ...), custom_call_target="tpu_custom_call" | custom-call | tf_op jit(solution)/shard_map/pack/pallas_call | solution.py:81
  50.1 0.0 copy-start.5
  50.2 0.1 collective-permute-start.11
  50.3 4.6 %collective-permute-done.13.refs_3_.refs_8_ = f32[2,4,64,128]{3,2,1,0:T(8,128)S(1)} collective-permute-done((f32[2,4,64,128]{3,2,1,0:T(8,128)S(1)}, f32[2,4,64,128]{3,2,1,0:T(8,128)S(1)}, u32[]{:S(2)}, u32[]{:S(2)}) %collective-permute-start.13) | collective-permute-done | bytes 262176 | tf_op jit(solution)/shard_map/ppermute | solution.py:94
  54.9 1.5 %pack.15.refs_9_.refs_6_ = f32[2,4,64,128]{3,2,1,0:T(8,128)S(1)} custom-call(s32[6]{0:T(128)S(1)} %reshape_squeeze.3.plan, f32[4,20,64,128]{3,2,1,0:T(8,128)} %bitcast.18, f32[2,4,64,128]{3,2,1,0:T(8,128)S(1)} %collective-permute-done.7.refs_0_.refs_3_, f32[2,4,64,128]{3,2,1,0:T(8,128)S(1)} %collective-permute-done.12.refs_1_.refs_4_, ...), custom_call_target="tpu_custom_call" | custom-call | tf_op jit(solution)/shard_map/pack/pallas_call | solution.py:81
  56.5 1.4 %collective-permute-start.14 = (f32[2,4,64,128]{3,2,1,0:T(8,128)S(1)}, f32[2,4,64,128]{3,2,1,0:T(8,128)}, u32[]{:S(2)}, u32[]{:S(2)}) collective-permute-start(f32[2,4,64,128]{3,2,1,0:T(8,128)S(1)} %pack.15.refs_9_.refs_6_), channel_id=1, source_target_pairs={{0,4},{1,5},{2,6},{3,7},{4,0},{5,1},{6,2},{7,3},{8,12},{9,13},{10,... | collective-permute-start | bytes 786440 | tf_op jit(solution)/shard_map/ppermute | solution.py:94
  57.8 0.1 copy.8
  57.9 0.1 reshape.19.links
  58.1 5.8 %faces.2 = (f32[5,4,4,64,128]{4,3,2,1,0:T(8,128)}, f32[5,4,320,128]{3,2,1,0:T(8,128)}, f32[16,2,120,128]{3,2,1,0:T(8,128)}, f32[16,120,128]{2,1,0:T(8,128)}) custom-call(s32[6]{0:T(128)S(1)} %reshape_squeeze.3.plan, s32[1]{0:T(128)} %bitcast.place, s32[256]{0:T(256)S(1)} %reshape.19.links, f32[4,20,64,128]{3,2,1,0:T(8,128)} %bitcast.19, ...), custom_call_target="tpu_custom_call" | custom-call | tf_op jit(solution)/shard_map/faces/pallas_call | solution.py:289
  63.8 0.7 collective-permute-done.14.refs_5_
  64.5 4.3 %faces.3 = (f32[5,4,4,64,128]{4,3,2,1,0:T(8,128)}, f32[5,4,320,128]{3,2,1,0:T(8,128)}, f32[16,2,120,128]{3,2,1,0:T(8,128)}, f32[16,120,128]{2,1,0:T(8,128)}, f32...) custom-call(s32[6]{0:T(128)S(1)} %reshape_squeeze.3.plan, ...), custom_call_target="tpu_custom_call", output_to_operand_aliasing={{0}: (11, {}), {1}: (12, {}), {2}: (13, {}), {3}: (14, {})} | custom-call | flops 999999995904 | bytes 10000000000 | tf_op jit(solution)/shard_map/faces/pallas_call | solution.py:289
  68.9 3.0 %collective-permute-start.15 = (f32[4,5,3,8,128]{4,3,2,1,0:T(8,128)S(1)}, f32[4,5,3,8,128]{4,3,2,1,0:T(8,128)S(1)}, u32[]{:S(2)}, u32[]{:S(2)}) collective-permute-start(f32[4,5,3,8,128]{4,3,2,1,0:T(8,128)S(1)} %get-tuple-element.45), channel_id=1, source_target_pairs={{0,1},{1,2},{2,3},{3,4},{4,5},{5,6},{6,7},{7,0},{8,9},{9,10},{10,1... | collective-permute-start | bytes 737288 | tf_op jit(solution)/shard_map/ppermute | solution.py:589
  71.9 1.2 %collective-permute-start.16 = (f32[4,5,3,8,128]{4,3,2,1,0:T(8,128)S(1)}, f32[4,5,3,8,128]{4,3,2,1,0:T(8,128)S(1)}, u32[]{:S(2)}, u32[]{:S(2)}) collective-permute-start(f32[4,5,3,8,128]{4,3,2,1,0:T(8,128)S(1)} %get-tuple-element.46), channel_id=1, source_target_pairs={{1,0},{2,1},{3,2},{4,3},{5,4},{6,5},{7,6},{0,7},{9,8},{10,9},{11,1... | collective-permute-start | bytes 737288 | tf_op jit(solution)/shard_map/ppermute | solution.py:590
  73.1 4.6 %all-to-all-start = ((f32[16,2,120,128]{3,2,1,0:T(8,128)}), f32[16,2,120,128]{3,2,1,0:T(8,128)}, u32[]{:S(2)}, u32[]{:S(2)}) async-start(f32[16,2,120,128]{3,2,1,0:T(8,128)} %get-tuple-element.48), calls=%async_computation | async-start | bytes 3932160 | tf_op jit(solution)/shard_map/all_to_all | solution.py:585
  77.7 0.5 collective-permute-done.15.z_below
  78.2 1.8 %collective-permute-done.16.z_above = f32[4,5,3,8,128]{4,3,2,1,0:T(8,128)S(1)} collective-permute-done((f32[4,5,3,8,128]{4,3,2,1,0:T(8,128)S(1)}, f32[4,5,3,8,128]{4,3,2,1,0:T(8,128)S(1)}, u32[]{:S(2)}, u32[]{:S(2)}) %collective-permute-start.16) | collective-permute-done | bytes 245792 | tf_op jit(solution)/shard_map/ppermute | solution.py:590
  80.0 14.8 %inner.1 = (f32[5,4,4,64,128]{4,3,2,1,0:T(8,128)}, f32[2,2,5,5,4,8,128]{6,5,4,3,2,1,0:T(8,128)}) custom-call(f32[5,4,320,128]{3,2,1,0:T(8,128)} %get-tuple-element.43.turned_in, f32[5,4,4,64,128]{4,3,2,1,0:T(8,128)} %get-tuple-element.44.patches_in, f32[4,5,3,8,128]{4,3,2,1,0:T(8,128)S(1)} %collective-permute-done.15.z_below, ...), custom_call_target="tpu_custom_call" | custom-call | flops 999999995904 | bytes 10000000000 | tf_op jit(solution)/shard_map/inner/pallas_call | solution.py:462
  94.8 12.1 %all-to-all-done.arrived = f32[16,2,120,128]{3,2,1,0:T(8,128)} async-done(((f32[16,2,120,128]{3,2,1,0:T(8,128)}), f32[16,2,120,128]{3,2,1,0:T(8,128)}, u32[]{:S(2)}, u32[]{:S(2)}) %all-to-all-start) | async-done | bytes 1966112 | tf_op jit(solution)/shard_map/all_to_all | solution.py:585
  106.9 8.7 %outer.1 = f32[4,5,4,64,128]{4,3,2,1,0:T(8,128)} custom-call(s32[1]{0:T(128)} %bitcast.place, s32[256]{0:T(256)S(1)} %reshape.19.links, f32[2,2,5,5,4,8,128]{6,5,4,3,2,1,0:T(8,128)} %get-tuple-element.47.rim_in, f32[16,2,120,128]{3,2,1,0:T(8,128)} %all-to-all-done.arrived, f32[16,120,128]{2,1,0:T(8,128)} %get-tuple-element.49.own_items, ...), custom_call_target="tpu_custom_call" | custom-call | tf_op jit(solution)/shard_map/outer/pallas_call | solution.py:550
  (16 shorter events, 0.0 us)
Async XLA Ops:
  0.0 0.7 copy-start
  3.0 11.2 %collective-permute-start.2 = (f32[2,4,64,128]{3,2,1,0:T(8,128)S(1)}, f32[2,4,64,128]{3,2,1,0:T(8,128)S(1)}, u32[]{:S(2)}, u32[]{:S(2)}) collective-permute-start(f32[2,4,64,128]{3,2,1,0:T(8,128)S(1)} %get-tuple-element.30), channel_id=1, source_target_pairs={{0,64},{32,96},{64,0},{96,32},{1,65},{33,97},{65,1},{97,33},{2,66}... | collective-permute-start | bytes 786440 | tf_op jit(solution)/shard_map/ppermute | solution.py:94
  7.0 15.5 %collective-permute-start.1 = (f32[2,4,64,128]{3,2,1,0:T(8,128)S(1)}, f32[2,4,64,128]{3,2,1,0:T(8,128)S(1)}, u32[]{:S(2)}, u32[]{:S(2)}) collective-permute-start(f32[2,4,64,128]{3,2,1,0:T(8,128)S(1)} %get-tuple-element.29), channel_id=1, source_target_pairs={{0,64},{32,96},{64,0},{96,32},{1,65},{33,97},{65,1},{97,33},{2,66}... | collective-permute-start | bytes 786440 | tf_op jit(solution)/shard_map/ppermute | solution.py:94
  7.1 21.0 %collective-permute-start.4 = (f32[2,4,64,128]{3,2,1,0:T(8,128)S(1)}, f32[2,4,64,128]{3,2,1,0:T(8,128)S(1)}, u32[]{:S(2)}, u32[]{:S(2)}) collective-permute-start(f32[2,4,64,128]{3,2,1,0:T(8,128)S(1)} %get-tuple-element.32), channel_id=1, source_target_pairs={{0,64},{32,96},{64,0},{96,32},{1,65},{33,97},{65,1},{97,33},{2,66}... | collective-permute-start | bytes 786440 | tf_op jit(solution)/shard_map/ppermute | solution.py:94
  15.1 13.0 %collective-permute-start.5 = (f32[2,4,64,128]{3,2,1,0:T(8,128)S(1)}, f32[2,4,64,128]{3,2,1,0:T(8,128)S(1)}, u32[]{:S(2)}, u32[]{:S(2)}) collective-permute-start(f32[2,4,64,128]{3,2,1,0:T(8,128)S(1)} %pack.9.refs_1_), channel_id=1, source_target_pairs={{0,16},{8,24},{16,0},{24,8},{1,17},{9,25},{17,1},{25,9},{2,18},{10... | collective-permute-start | bytes 786440 | tf_op jit(solution)/shard_map/ppermute | solution.py:94
  19.1 14.1 %collective-permute-start = (f32[2,4,64,128]{3,2,1,0:T(8,128)S(1)}, f32[2,4,64,128]{3,2,1,0:T(8,128)S(1)}, u32[]{:S(2)}, u32[]{:S(2)}) collective-permute-start(f32[2,4,64,128]{3,2,1,0:T(8,128)S(1)} %get-tuple-element.28), channel_id=1, source_target_pairs={{0,64},{32,96},{64,0},{96,32},{1,65},{33,97},{65,1},{97,33},{2,66}... | collective-permute-start | bytes 786440 | tf_op jit(solution)/shard_map/ppermute | solution.py:94
  23.4 9.8 %collective-permute-start.3 = (f32[2,4,64,128]{3,2,1,0:T(8,128)S(1)}, f32[2,4,64,128]{3,2,1,0:T(8,128)S(1)}, u32[]{:S(2)}, u32[]{:S(2)}) collective-permute-start(f32[2,4,64,128]{3,2,1,0:T(8,128)S(1)} %pack.10.refs_3_), channel_id=1, source_target_pairs={{0,16},{8,24},{16,0},{24,8},{1,17},{9,25},{17,1},{25,9},{2,18},{10... | collective-permute-start | bytes 786440 | tf_op jit(solution)/shard_map/ppermute | solution.py:94
  24.7 14.1 %collective-permute-start.7 = (f32[2,4,64,128]{3,2,1,0:T(8,128)S(1)}, f32[2,4,64,128]{3,2,1,0:T(8,128)S(1)}, u32[]{:S(2)}, u32[]{:S(2)}) collective-permute-start(f32[2,4,64,128]{3,2,1,0:T(8,128)S(1)} %get-tuple-element.31.refs_1_), channel_id=1, source_target_pairs={{0,64},{32,96},{64,0},{96,32},{1,65},{33,97},{65,1},{97,33},{2,66}... | collective-permute-start | bytes 786440 | tf_op jit(solution)/shard_map/ppermute | solution.py:94
  30.0 8.8 %collective-permute-start.8 = (f32[2,4,64,128]{3,2,1,0:T(8,128)S(1)}, f32[2,4,64,128]{3,2,1,0:T(8,128)S(1)}, u32[]{:S(2)}, u32[]{:S(2)}) collective-permute-start(f32[2,4,64,128]{3,2,1,0:T(8,128)S(1)} %get-tuple-element.35), channel_id=1, source_target_pairs={{0,16},{8,24},{16,0},{24,8},{1,17},{9,25},{17,1},{25,9},{2,18},{10... | collective-permute-start | bytes 786440 | tf_op jit(solution)/shard_map/ppermute | solution.py:94
  30.6 8.2 %collective-permute-start.9 = (f32[2,4,64,128]{3,2,1,0:T(8,128)S(1)}, f32[2,4,64,128]{3,2,1,0:T(8,128)S(1)}, u32[]{:S(2)}, u32[]{:S(2)}) collective-permute-start(f32[2,4,64,128]{3,2,1,0:T(8,128)S(1)} %get-tuple-element.33.refs_3_), channel_id=1, source_target_pairs={{0,4},{1,5},{2,6},{3,7},{4,0},{5,1},{6,2},{7,3},{8,12},{9,13},{10,... | collective-permute-start | bytes 786440 | tf_op jit(solution)/shard_map/ppermute | solution.py:94
  35.1 13.0 %collective-permute-start.6 = (f32[2,4,64,128]{3,2,1,0:T(8,128)S(1)}, f32[2,4,64,128]{3,2,1,0:T(8,128)S(1)}, u32[]{:S(2)}, u32[]{:S(2)}) collective-permute-start(f32[2,4,64,128]{3,2,1,0:T(8,128)S(1)} %get-tuple-element.34), channel_id=1, source_target_pairs={{0,16},{8,24},{16,0},{24,8},{1,17},{9,25},{17,1},{25,9},{2,18},{10... | collective-permute-start | bytes 786440 | tf_op jit(solution)/shard_map/ppermute | solution.py:94
  38.4 10.3 %collective-permute-start.10 = (f32[2,4,64,128]{3,2,1,0:T(8,128)S(1)}, f32[2,4,64,128]{3,2,1,0:T(8,128)S(1)}, u32[]{:S(2)}, u32[]{:S(2)}) collective-permute-start(f32[2,4,64,128]{3,2,1,0:T(8,128)S(1)} %get-tuple-element.36.refs_3_), channel_id=1, source_target_pairs={{0,4},{1,5},{2,6},{3,7},{4,0},{5,1},{6,2},{7,3},{8,12},{9,13},{10,... | collective-permute-start | bytes 786440 | tf_op jit(solution)/shard_map/ppermute | solution.py:94
  40.7 9.5 %collective-permute-start.12 = (f32[2,4,64,128]{3,2,1,0:T(8,128)S(1)}, f32[2,4,64,128]{3,2,1,0:T(8,128)S(1)}, u32[]{:S(2)}, u32[]{:S(2)}) collective-permute-start(f32[2,4,64,128]{3,2,1,0:T(8,128)S(1)} %get-tuple-element.38), channel_id=1, source_target_pairs={{0,16},{8,24},{16,0},{24,8},{1,17},{9,25},{17,1},{25,9},{2,18},{10... | collective-permute-start | bytes 786440 | tf_op jit(solution)/shard_map/ppermute | solution.py:94
  44.6 10.3 %collective-permute-start.13 = (f32[2,4,64,128]{3,2,1,0:T(8,128)S(1)}, f32[2,4,64,128]{3,2,1,0:T(8,128)S(1)}, u32[]{:S(2)}, u32[]{:S(2)}) collective-permute-start(f32[2,4,64,128]{3,2,1,0:T(8,128)S(1)} %get-tuple-element.37.refs_2_), channel_id=1, source_target_pairs={{0,4},{1,5},{2,6},{3,7},{4,0},{5,1},{6,2},{7,3},{8,12},{9,13},{10,... | collective-permute-start | bytes 786440 | tf_op jit(solution)/shard_map/ppermute | solution.py:94
  48.2 8.3 %copy-start.1 = (f32[2,4,64,128]{3,2,1,0:T(8,128)}, f32[2,4,64,128]{3,2,1,0:T(8,128)S(1)}, u32[]{:S(2)}) copy-start(f32[2,4,64,128]{3,2,1,0:T(8,128)S(1)} %collective-permute-done.6.refs_1_) | copy-start | bytes 786436
  50.1 7.7 %copy-start.5 = (s32[64,4]{0,1:T(4,128)S(1)}, s32[64,4]{0,1:T(4,128)}, u32[]{:S(2)}) copy-start(s32[64,4]{0,1:T(4,128)} %param.5) | copy-start | bytes 3076
  50.2 13.7 %collective-permute-start.11 = (f32[2,4,64,128]{3,2,1,0:T(8,128)S(1)}, f32[2,4,64,128]{3,2,1,0:T(8,128)}, u32[]{:S(2)}, u32[]{:S(2)}) collective-permute-start(f32[2,4,64,128]{3,2,1,0:T(8,128)S(1)} %pack.14.refs_2_), channel_id=1, source_target_pairs={{0,4},{1,5},{2,6},{3,7},{4,0},{5,1},{6,2},{7,3},{8,12},{9,13},{10,... | collective-permute-start | bytes 786440 | tf_op jit(solution)/shard_map/ppermute | solution.py:94
  50.3 6.2 %copy-start.3 = (f32[2,4,64,128]{3,2,1,0:T(8,128)}, f32[2,4,64,128]{3,2,1,0:T(8,128)S(1)}, u32[]{:S(2)}) copy-start(f32[2,4,64,128]{3,2,1,0:T(8,128)S(1)} %collective-permute-done.12.refs_1_.refs_4_) | copy-start | bytes 786436
  56.5 8.1 %collective-permute-start.14 = (f32[2,4,64,128]{3,2,1,0:T(8,128)S(1)}, f32[2,4,64,128]{3,2,1,0:T(8,128)}, u32[]{:S(2)}, u32[]{:S(2)}) collective-permute-start(f32[2,4,64,128]{3,2,1,0:T(8,128)S(1)} %pack.15.refs_9_.refs_6_), channel_id=1, source_target_pairs={{0,4},{1,5},{2,6},{3,7},{4,0},{5,1},{6,2},{7,3},{8,12},{9,13},{10,... | collective-permute-start | bytes 786440 | tf_op jit(solution)/shard_map/ppermute | solution.py:94
  58.0 6.5 %copy-start.2 = (f32[2,4,64,128]{3,2,1,0:T(8,128)S(1)}, f32[2,4,64,128]{3,2,1,0:T(8,128)}, u32[]{:S(2)}) copy-start(f32[2,4,64,128]{3,2,1,0:T(8,128)} %copy-done.1) | copy-start | bytes 786436
  58.0 6.5 %copy-start.4 = (f32[2,4,64,128]{3,2,1,0:T(8,128)S(1)}, f32[2,4,64,128]{3,2,1,0:T(8,128)}, u32[]{:S(2)}) copy-start(f32[2,4,64,128]{3,2,1,0:T(8,128)} %copy-done.3) | copy-start | bytes 786436
  68.9 9.4 %collective-permute-start.15 = (f32[4,5,3,8,128]{4,3,2,1,0:T(8,128)S(1)}, f32[4,5,3,8,128]{4,3,2,1,0:T(8,128)S(1)}, u32[]{:S(2)}, u32[]{:S(2)}) collective-permute-start(f32[4,5,3,8,128]{4,3,2,1,0:T(8,128)S(1)} %get-tuple-element.45), channel_id=1, source_target_pairs={{0,1},{1,2},{2,3},{3,4},{4,5},{5,6},{6,7},{7,0},{8,9},{9,10},{10,1... | collective-permute-start | bytes 737288 | tf_op jit(solution)/shard_map/ppermute | solution.py:589
  71.9 8.1 %collective-permute-start.16 = (f32[4,5,3,8,128]{4,3,2,1,0:T(8,128)S(1)}, f32[4,5,3,8,128]{4,3,2,1,0:T(8,128)S(1)}, u32[]{:S(2)}, u32[]{:S(2)}) collective-permute-start(f32[4,5,3,8,128]{4,3,2,1,0:T(8,128)S(1)} %get-tuple-element.46), channel_id=1, source_target_pairs={{1,0},{2,1},{3,2},{4,3},{5,4},{6,5},{7,6},{0,7},{9,8},{10,9},{11,1... | collective-permute-start | bytes 737288 | tf_op jit(solution)/shard_map/ppermute | solution.py:590
  73.1 33.9 %all-to-all-start = ((f32[16,2,120,128]{3,2,1,0:T(8,128)}), f32[16,2,120,128]{3,2,1,0:T(8,128)}, u32[]{:S(2)}, u32[]{:S(2)}) async-start(f32[16,2,120,128]{3,2,1,0:T(8,128)} %get-tuple-element.48), calls=%async_computation | async-start | bytes 3932160 | tf_op jit(solution)/shard_map/all_to_all | solution.py:585

commit v3 on v2

--- a/solution.py
+++ b/solution.py
@@ -39,8 +39,7 @@
     return pltpu.with_memory_space_constraint(x, pltpu.HBM)
 
 
-def start_copy(plan, slot, rounds, chunk, cells, received, target, sem, first=0, count=None):
-    count = count or CHUNKS[chunk]
+def start_copies(plan, slot, rounds, cells, jobs):
     taken = jnp.bool_(False)
     for r in reversed(range(rounds)):
         for j in range(2):
@@ -48,15 +47,17 @@
 
             @pl.when(hit)
             def _(r=r, j=j):
-                source = received[r].at[j, pl.ds(first, count)]
-                pltpu.make_async_copy(source, target, sem).start()
+                for _, received, first, count, target, sem in jobs:
+                    source = received[r].at[j, pl.ds(first, count)]
+                    pltpu.make_async_copy(source, target, sem).start()
 
             taken = jnp.logical_or(taken, hit)
 
     @pl.when(jnp.logical_not(taken))
     def _():
-        source = cells.at[slot, pl.ds(STARTS[chunk] + first, count)]
-        pltpu.make_async_copy(source, target, sem).start()
+        for chunk, _, first, count, target, sem in jobs:
+            source = cells.at[slot, pl.ds(STARTS[chunk] + first, count)]
+            pltpu.make_async_copy(source, target, sem).start()
 
 
 def wait_copy(cells, count, target, sem):
@@ -71,7 +72,8 @@
         got = received[at : at + r]
         at += r
         for j in range(2):
-            start_copy(plan, plan[2 * r + j], r, c, cells, got, outs[n].at[j], sems.at[n, j])
+            job = (c, got, 0, CHUNKS[c], outs[n].at[j], sems.at[n, j])
+            start_copies(plan, plan[2 * r + j], r, cells, [job])
     for n, (r, c) in enumerate(sends):
         for j in range(2):
             wait_copy(cells, CHUNKS[c], outs[n].at[j], sems.at[n, j])
@@ -159,6 +161,19 @@
     return jnp.concatenate(rows, axis=0)
 
 
+def turn(patches, turned, n):
+    columns = [
+        jnp.concatenate(
+            [patches[n, k, c, pl.ds(8 * b, 8), :] for k in range(SLOTS) for c in range(LAYERS)],
+            axis=0,
+        )
+        for b in range(8)
+    ]
+    rows = jnp.transpose(jnp.concatenate(columns, axis=1))
+    for y in range(EDGE):
+        turned[n, y // 8, pl.ds(y % 8 * PITCH, EDGE), :] = rows[y * EDGE : (y + 1) * EDGE]
+
+
 def pieces(f):
     out = []
     for c, start in enumerate(STARTS):
@@ -176,47 +191,35 @@
     count, first, last = len(fields), fields[0], fields[0] > 0
     chunks = chunks_of(fields)
     received = refs[: 3 * len(chunks)]
-    refs = refs[3 * len(chunks) + 1 + 4 * last :]
-    patches_out, turned_out, send, own_items = refs[:4]
-    patches, turned, items, sems, item_sems, out_sems = refs[-6:]
+    refs = refs[3 * len(chunks) + 1 + 3 * last :]
+    patches_out, send, own_items = refs[:3]
+    patches, turned, items, sems, item_sems, out_sem = refs[-6:]
     parts = []
-    for n, f in enumerate(fields):
-        for p, (c, start, size, layer) in enumerate(pieces(f)):
-            got = received[3 * chunks.index(c) : 3 * chunks.index(c) + 3]
-            for k in range(SLOTS):
+    for k in range(SLOTS):
+        jobs = []
+        for n, f in enumerate(fields):
+            for p, (c, start, size, layer) in enumerate(pieces(f)):
+                got = received[3 * chunks.index(c) : 3 * chunks.index(c) + 3]
                 target, sem = patches.at[n, k, pl.ds(layer, size)], sems.at[n, k, p]
-                start_copy(plan, k, 3, c, cells, got, target, sem, start, size)
+                jobs.append((c, got, start, size, target, sem))
                 parts.append((n, size, target, sem))
+        start_copies(plan, k, 3, cells, jobs)
     loads = []
     if last:
-        z_first, z_last, ends, end_sems = refs[4:8]
+        z_first, z_last, ends, end_sems = refs[3:7]
         for end, c in ((0, 0), (1, LAYERS - 1)):
             source = patches_out.at[pl.ds(0, first), :, c]
             loads.append(pltpu.make_async_copy(source, ends.at[end], end_sems.at[end]))
     for load in loads:
         load.start()
 
-    mine = pl.ds(first, count)
-    outs = [
-        pltpu.make_async_copy(patches, patches_out.at[mine], out_sems.at[0]),
-        pltpu.make_async_copy(turned, turned_out.at[mine], out_sems.at[1]),
-    ]
+    whole = pltpu.make_async_copy(patches, patches_out.at[pl.ds(first, count)], out_sem)
     for n, f in enumerate(fields):
         for at, size, target, sem in parts:
             if at == n:
                 wait_copy(cells, size, target, sem)
-        columns = [
-            jnp.concatenate(
-                [patches[n, k, c, pl.ds(8 * b, 8), :] for k in range(SLOTS) for c in range(LAYERS)],
-                axis=0,
-            )
-            for b in range(8)
-        ]
-        rows = jnp.transpose(jnp.concatenate(columns, axis=1))
-        for y in range(EDGE):
-            turned[n, y // 8, pl.ds(y % 8 * PITCH, EDGE), :] = rows[y * EDGE : (y + 1) * EDGE]
-    for copy in outs:
-        copy.start()
+        turn(patches, turned, n)
+    whole.start()
 
     me = place[0]
     owners = [links[me * LINKS + i] // SLOTS for i in range(LINKS)]
@@ -264,8 +267,7 @@
 
     for i in range(LINKS):
         pltpu.make_async_copy(items.at[i], own_items.at[i, rows], item_sems.at[i]).wait()
-    for copy in outs:
-        copy.wait()
+    whole.wait()
 
 
 def faces(fields, plan, place, links, cells, received, after, carried):
@@ -278,7 +280,7 @@
         pltpu.VMEM((LINKS, count * GHOST * 8, 128), F32),
         pltpu.SemaphoreType.DMA((count, SLOTS, 2)),
         pltpu.SemaphoreType.DMA((LINKS,)),
-        pltpu.SemaphoreType.DMA((2,)),
+        pltpu.SemaphoreType.DMA,
     ]
     if last:
         scratch = [
@@ -290,13 +292,12 @@
         functools.partial(faces_kernel, fields),
         out_shape=[
             pltpu.HBM(PATCH_SHAPE, F32),
-            pltpu.HBM(TURNED_SHAPE, F32),
             pltpu.HBM((PLANE, 2, ITEM_ROWS, 128), F32),
             pltpu.HBM((LINKS, ITEM_ROWS, 128), F32),
         ]
         + [z_shape] * (2 * last),
         in_specs=[SMEM] * 3 + [HBM] + [ANY] * (held_chunks + 1) + [HBM] * len(carried),
-        out_specs=[HBM] * 4 + [VMEM] * (2 * last),
+        out_specs=[HBM] * 3 + [VMEM] * (2 * last),
         scratch_shapes=scratch,
         input_output_aliases={held_chunks + 5 + i: i for i in range(len(carried))},
         compiler_params=pltpu.CompilerParams(vmem_limit_bytes=16 * MIB),
@@ -364,17 +365,30 @@
         put(last + 1, [-v for v in prev])
 
 
-def inner_kernel(turned_in, patches_in, z_below, z_above, out, rim_out, *scratch):
+def inner_kernel(place, links, patches_in, z_below, z_above, out, rim_out, table, *scratch):
     turned, patches, change, partial, rim, sems, out_sems = scratch
     loads = [
         pltpu.make_async_copy(patches_in.at[:, k], patches.at[:, k], sems.at[k])
         for k in range(SLOTS)
     ]
-    loads.append(pltpu.make_async_copy(turned_in, turned, sems.at[SLOTS]))
     for load in loads:
         load.start()
-    for load in loads[:SLOTS]:
+    me = place[0]
+    for i in range(LINKS):
+        entry = links[me * LINKS + i]
+        owner = entry // SLOTS
+        source = (entry % SLOTS) * 4 + (i % 4 ^ 1)
+        rank = jnp.int32(0)
+        for j in range(LINKS - 1):
+            same = jnp.logical_and(links[owner * LINKS + j] // SLOTS == me, j < source)
+            rank = rank + same.astype(jnp.int32)
+        table[i] = owner
+        table[LINKS + i] = jnp.minimum(rank, 1)
+        table[2 * LINKS + i] = source
+    for load in loads:
         load.wait()
+    for f in range(FIELDS):
+        turn(patches, turned, f)
 
     def z_sweep(k, carry):
         def get(i):
@@ -398,7 +412,6 @@
         return carry
 
     lax.fori_loop(0, SLOTS, z_sweep, 0)
-    loads[SLOTS].wait()
 
     def plane_sweep(direction, g, put):
         def get(i):
@@ -458,39 +471,36 @@
                 )
 
 
-def inner(turned, patches, z_below, z_above):
+def inner(place, links, patches, z_below, z_above):
     return pl.pallas_call(
         inner_kernel,
-        out_shape=[pltpu.HBM(PATCH_SHAPE, F32), pltpu.HBM(RIM_SHAPE, F32)],
-        in_specs=[HBM, HBM, VMEM, VMEM],
-        out_specs=[HBM, HBM],
+        out_shape=[
+            pltpu.HBM(PATCH_SHAPE, F32),
+            pltpu.HBM(RIM_SHAPE, F32),
+            jax.ShapeDtypeStruct((3 * LINKS,), jnp.int32),
+        ],
+        in_specs=[SMEM, SMEM, HBM, VMEM, VMEM],
+        out_specs=[HBM, HBM, SMEM],
         scratch_shapes=[
             pltpu.VMEM(TURNED_SHAPE, F32),
             pltpu.VMEM(PATCH_SHAPE, F32),
             pltpu.VMEM(TURNED_SHAPE, F32),
             pltpu.VMEM(PATCH_SHAPE, F32),
             pltpu.VMEM(RIM_SHAPE, F32),
-            pltpu.SemaphoreType.DMA((SLOTS + 1,)),
+            pltpu.SemaphoreType.DMA((SLOTS,)),
             pltpu.SemaphoreType.DMA((FIELDS + 1,)),
         ],
         compiler_params=pltpu.CompilerParams(vmem_limit_bytes=24 * MIB),
         cost_estimate=LONG,
         name="inner",
-    )(held(turned), held(patches), z_below, z_above)
-
-
-def outer_kernel(place, links, rim_in, arrived, own_items, partial_in, out, *scratch):
+    )(place, links, held(patches), z_below, z_above)
+
+
+def outer_kernel(place, table, rim_in, arrived, own_items, partial_in, out, *scratch):
     rim, items, ghosts, change, partial, result, item_sems, sems, out_sems = scratch
     me = place[0]
     for i in range(LINKS):
-        entry = links[me * LINKS + i]
-        owner = entry // SLOTS
-        source = (entry % SLOTS) * 4 + (i % 4 ^ 1)
-        rank = jnp.int32(0)
-        for j in range(LINKS - 1):
-            same = jnp.logical_and(links[owner * LINKS + j] // SLOTS == me, j < source)
-            rank = rank + same.astype(jnp.int32)
-        rank = jnp.minimum(rank, 1)
+        owner, rank, source = table[i], table[LINKS + i], table[2 * LINKS + i]
 
         @pl.when(owner != me)
         def _(i=i, owner=owner, rank=rank):
@@ -546,7 +556,7 @@
         copy.wait()
 
 
-def outer(place, links, rim, arrived, own_items, partial):
+def outer(place, table, rim, arrived, own_items, partial):
     return pl.pallas_call(
         outer_kernel,
         out_shape=jax.ShapeDtypeStruct((SLOTS, FIELDS, LAYERS, 64, 128), F32),
@@ -565,7 +575,7 @@
         ],
         compiler_params=pltpu.CompilerParams(vmem_limit_bytes=24 * MIB),
         name="outer",
-    )(place, links, held(rim), held(arrived), held(own_items), held(partial))
+    )(place, table, held(rim), held(arrived), held(own_items), held(partial))
 
 
 def local(cells, moves, neighbours):
@@ -580,7 +590,7 @@
     for fields in GROUPS:
         received = [got[r, c] for c in chunks_of(fields) for r in range(3)]
         made = faces(fields, plan, place, links, tiled, received, after, made)
-    patches, turned, send, own_items, z_first, z_last = made
+    patches, send, own_items, z_first, z_last = made
 
     arrived = lax.all_to_all(send, ("gx", "gy"), 0, 0, tiled=True)
     layers = lax.axis_size("gz")
@@ -588,8 +598,8 @@
     down = [(j, i) for i, j in up]
     z_below = lax.ppermute(z_last, "gz", up)
     z_above = lax.ppermute(z_first, "gz", down)
-    partial, rim = inner(turned, patches, z_below, z_above)
-    result = outer(place, links, rim, arrived, own_items, partial)
+    partial, rim, table = inner(place, links, patches, z_below, z_above)
+    result = outer(place, table, rim, arrived, own_items, partial)
     result = result.reshape(SLOTS, FIELDS, LAYERS, 8, 8, 128).transpose(0, 1, 2, 4, 3, 5)
     return result.reshape(cells.shape)
 

time: 117 us -> 114 us (0.974); the launches traced: 116 us -> 115 us
  starting transfers between devices: 44.3 us -> 49.2 us
  waiting for transfers between devices: 23.8 us -> 20.3 us
  Pallas kernels: 46.1 us -> 43.8 us
    ppermute x15, starting transfers between devices: 35.4 us -> 40.4 us  [swapped(): lax.ppermute(block, axis, [(i, i ^ count // 2) for i in range(count)])]
    all_to_all x1, waiting for transfers between devices: 12.1 us -> 10.1 us  [local(): arrived = lax.all_to_all(send, ('gx', 'gy'), 0, 0, tiled=True)]
    pallas_call x1, Pallas kernels: 14.8 us -> 16.7 us  [inner(): pl.pallas_call(inner_kernel, out_shape=[pltpu.HBM(PATCH_SHAPE, F32), pltp...]
    ppermute x15, waiting for transfers between devices: 9.43 us -> 7.55 us  [swapped(): lax.ppermute(block, axis, [(i, i ^ count // 2) for i in range(count)])]
    pallas_call x2, Pallas kernels: 10.1 us -> 8.36 us  [faces(): pl.pallas_call(functools.partial(faces_kernel, fields), out_shape=[pltpu....]
    pallas_call x1, Pallas kernels: 8.73 us -> 7.35 us  [outer(): pl.pallas_call(outer_kernel, out_shape=jax.ShapeDtypeStruct((SLOTS, FIELD...]
    ppermute x1, starting transfers between devices: 1.19 us -> 2.53 us  [local(): z_above = lax.ppermute(z_first, 'gz', down)]
    ppermute x1, starting transfers between devices: 3.02 us -> 1.67 us  [local(): z_below = lax.ppermute(z_last, 'gz', up)]
  transfers between devices with their start and end apart: 18 -> 18, of which waited for: 7 -> 4; matrix products, arithmetic and copies ran while one was open for 0% -> 0% of each run, Pallas kernels for 27% -> 27%
where the time goes in v3:
time: 114 us; the launch traced here: 115 us
  starting transfers between devices  49.2 us (43%)
  Pallas kernels  43.8 us (38%)
  waiting for transfers between devices  20.3 us (18%)
  local copies, waits for them, and re-layouts  1.2 us (1%)
    ppermute x15, starting transfers between devices, swapped(): lax.ppermute(block, axis, [(i, i ^ count // 2) for i in range(count)])  40.4 us
    pallas_call x1, Pallas kernels, inner(): pl.pallas_call(inner_kernel, out_shape=[pltpu.HBM(PATCH_SHAPE, F32), pltp...  16.7 us
    pallas_call x8, Pallas kernels, pack(): pl.pallas_call(functools.partial(pack_kernel, sends, len(received)), out_...  11.4 us
    all_to_all x1, waiting for transfers between devices, local(): arrived = lax.all_to_all(send, ('gx', 'gy'), 0, 0, tiled=True)  10.1 us
    pallas_call x2, Pallas kernels, faces(): pl.pallas_call(functools.partial(faces_kernel, fields), out_shape=[pltpu....  8.36 us
    ppermute x15, waiting for transfers between devices, swapped(): lax.ppermute(block, axis, [(i, i ^ count // 2) for i in range(count)])  7.55 us
    pallas_call x1, Pallas kernels, outer(): pl.pallas_call(outer_kernel, out_shape=jax.ShapeDtypeStruct((SLOTS, FIELD...  7.35 us
    all_to_all x1, starting transfers between devices, local(): arrived = lax.all_to_all(send, ('gx', 'gy'), 0, 0, tiled=True)  4.66 us
  transfers between devices with their start and end apart: 18, of which 4 were waited for; matrix products, arithmetic and copies ran while one was open for 0% of the time, Pallas kernels for 27%

profile of v3, /device:TPU:0, one launch (start us, length us, event | category | flops | bytes accessed | tf_op | source)
XLA Modules:
  0.0 114.9 jit_solution(14893212617743292809)
XLA Ops:
  0.0 0.7 copy-done
  0.7 0.2 dynamic-slice_reduce_fusion
  0.9 0.1 reshape_squeeze.3.plan
  1.0 2.0 %pack.8 = (f32[2,4,64,128]{3,2,1,0:T(8,128)S(1)}, f32[2,4,64,128]{3,2,1,0:T(8,128)S(1)}, f32[2,4,64,128]{3,2,1,0:T(8,128)S(1)}, f32[2,4,64,128]{3,2,1,0:T(8,128)S(1)}, f32[2,4,64,128]{3,2,1,0:T(8,128)S(1)}) custom-call(s32[6]{0:T(128)S(1)} %reshape_squeeze.3.plan, f32[4,20,64,128]{3,2,1,0:T(8,128)} %bitcast.11), custom_call_target="tpu_custom_call" | custom-call | tf_op jit(solution)/shard_map/pack/pallas_call | solution.py:83
  3.0 4.0 %collective-permute-start.2 = (f32[2,4,64,128]{3,2,1,0:T(8,128)S(1)}, f32[2,4,64,128]{3,2,1,0:T(8,128)S(1)}, u32[]{:S(2)}, u32[]{:S(2)}) collective-permute-start(f32[2,4,64,128]{3,2,1,0:T(8,128)S(1)} %get-tuple-element.29), channel_id=1, source_target_pairs={{0,64},{32,96},{64,0},{96,32},{1,65},{33,97},{65,1},{97,33},{2,66}... | collective-permute-start | bytes 786440 | tf_op jit(solution)/shard_map/ppermute | solution.py:96
  7.0 0.1 collective-permute-start.1
  7.1 3.4 %collective-permute-start.4 = (f32[2,4,64,128]{3,2,1,0:T(8,128)S(1)}, f32[2,4,64,128]{3,2,1,0:T(8,128)S(1)}, u32[]{:S(2)}, u32[]{:S(2)}) collective-permute-start(f32[2,4,64,128]{3,2,1,0:T(8,128)S(1)} %get-tuple-element.31), channel_id=1, source_target_pairs={{0,64},{32,96},{64,0},{96,32},{1,65},{33,97},{65,1},{97,33},{2,66}... | collective-permute-start | bytes 786440 | tf_op jit(solution)/shard_map/ppermute | solution.py:96
  10.6 3.6 %collective-permute-done.2.refs_0_.refs_1_ = f32[2,4,64,128]{3,2,1,0:T(8,128)S(1)} collective-permute-done((f32[2,4,64,128]{3,2,1,0:T(8,128)S(1)}, f32[2,4,64,128]{3,2,1,0:T(8,128)S(1)}, u32[]{:S(2)}, u32[]{:S(2)}) %collective-permute-start.2) | collective-permute-done | bytes 262176 | tf_op jit(solution)/shard_map/ppermute | solution.py:96
  14.2 1.5 %pack.9.refs_1_ = f32[2,4,64,128]{3,2,1,0:T(8,128)S(1)} custom-call(s32[6]{0:T(128)S(1)} %reshape_squeeze.3.plan, f32[4,20,64,128]{3,2,1,0:T(8,128)} %bitcast.12, f32[2,4,64,128]{3,2,1,0:T(8,128)S(1)} %collective-permute-done.2.refs_0_.refs_1_, f32[2,4,64,128]{3,2,1,0:T(8,128)S(1)} %get-tuple-element.30.refs_1_), custom_call_target="tpu_custom_call" | custom-call | tf_op jit(solution)/shard_map/pack/pallas_call | solution.py:83
  15.7 3.5 %collective-permute-start.5 = (f32[2,4,64,128]{3,2,1,0:T(8,128)S(1)}, f32[2,4,64,128]{3,2,1,0:T(8,128)S(1)}, u32[]{:S(2)}, u32[]{:S(2)}) collective-permute-start(f32[2,4,64,128]{3,2,1,0:T(8,128)S(1)} %pack.9.refs_1_), channel_id=1, source_target_pairs={{0,16},{8,24},{16,0},{24,8},{1,17},{9,25},{17,1},{25,9},{2,18},{10... | collective-permute-start | bytes 786440 | tf_op jit(solution)/shard_map/ppermute | solution.py:96
  19.1 3.4 %collective-permute-start = (f32[2,4,64,128]{3,2,1,0:T(8,128)S(1)}, f32[2,4,64,128]{3,2,1,0:T(8,128)S(1)}, u32[]{:S(2)}, u32[]{:S(2)}) collective-permute-start(f32[2,4,64,128]{3,2,1,0:T(8,128)S(1)} %get-tuple-element.27), channel_id=1, source_target_pairs={{0,64},{32,96},{64,0},{96,32},{1,65},{33,97},{65,1},{97,33},{2,66}... | collective-permute-start | bytes 786440 | tf_op jit(solution)/shard_map/ppermute | solution.py:96
  22.5 0.0 collective-permute-done.1.refs_0_.refs_1_.refs_3_
  22.5 1.5 %pack.10.refs_3_ = f32[2,4,64,128]{3,2,1,0:T(8,128)S(1)} custom-call(s32[6]{0:T(128)S(1)} %reshape_squeeze.3.plan, f32[4,20,64,128]{3,2,1,0:T(8,128)} %bitcast.13, f32[2,4,64,128]{3,2,1,0:T(8,128)S(1)} %collective-permute-done.1.refs_0_.refs_1_.refs_3_, f32[2,4,64,128]{3,2,1,0:T(8,128)S(1)} %pack.9.refs_1_), custom_call_target="tpu_custom_call" | custom-call | tf_op jit(solution)/shard_map/pack/pallas_call | solution.py:83
  24.0 0.8 collective-permute-start.3
  24.8 3.3 %collective-permute-start.7 = (f32[2,4,64,128]{3,2,1,0:T(8,128)S(1)}, f32[2,4,64,128]{3,2,1,0:T(8,128)S(1)}, u32[]{:S(2)}, u32[]{:S(2)}) collective-permute-start(f32[2,4,64,128]{3,2,1,0:T(8,128)S(1)} %get-tuple-element.30.refs_1_), channel_id=1, source_target_pairs={{0,64},{32,96},{64,0},{96,32},{1,65},{33,97},{65,1},{97,33},{2,66}... | collective-permute-start | bytes 786440 | tf_op jit(solution)/shard_map/ppermute | solution.py:96
  28.1 0.0 collective-permute-done.4.refs_0_.refs_1_.refs_6_
  28.1 0.0 collective-permute-done.5.refs_2_.refs_1_
  28.1 1.5 %pack.11 = (f32[2,4,64,128]{3,2,1,0:T(8,128)S(1)}, f32[2,4,64,128]{3,2,1,0:T(8,128)S(1)}) custom-call(s32[6]{0:T(128)S(1)} %reshape_squeeze.3.plan, f32[4,20,64,128]{3,2,1,0:T(8,128)} %bitcast.14, f32[2,4,64,128]{3,2,1,0:T(8,128)S(1)} %collective-permute-done.4.refs_0_.refs_1_.refs_6_, f32[2,4,64,128]{3,2,1,0:T(8,128)S(1)} %collective-permute-done.2.refs_0_.refs_1_, ...), custom_call_target="tpu_custom_call" | custom-call | tf_op jit(solution)/shard_map/pack/pallas_call | solution.py:83
  29.6 0.8 collective-permute-start.8
  30.4 3.2 %collective-permute-start.9 = (f32[2,4,64,128]{3,2,1,0:T(8,128)S(1)}, f32[2,4,64,128]{3,2,1,0:T(8,128)S(1)}, u32[]{:S(2)}, u32[]{:S(2)}) collective-permute-start(f32[2,4,64,128]{3,2,1,0:T(8,128)S(1)} %get-tuple-element.32.refs_3_), channel_id=1, source_target_pairs={{0,4},{1,5},{2,6},{3,7},{4,0},{5,1},{6,2},{7,3},{8,12},{9,13},{10,... | collective-permute-start | bytes 786440 | tf_op jit(solution)/shard_map/ppermute | solution.py:96
  33.6 0.0 collective-permute-done.3.refs_2_.refs_4_
  33.6 1.5 %pack.12 = (f32[2,4,64,128]{3,2,1,0:T(8,128)S(1)}, f32[2,4,64,128]{3,2,1,0:T(8,128)S(1)}) custom-call(s32[6]{0:T(128)S(1)} %reshape_squeeze.3.plan, f32[4,20,64,128]{3,2,1,0:T(8,128)} %bitcast.15, f32[2,4,64,128]{3,2,1,0:T(8,128)S(1)} %collective-permute-done.refs_0_, f32[2,4,64,128]{3,2,1,0:T(8,128)S(1)} %collective-permute-done.1.refs_0_.refs_1_.refs_3_, ...), custom_call_target="tpu_custom_call" | custom-call | tf_op jit(solution)/shard_map/pack/pallas_call | solution.py:83
  35.1 3.7 %collective-permute-start.6 = (f32[2,4,64,128]{3,2,1,0:T(8,128)S(1)}, f32[2,4,64,128]{3,2,1,0:T(8,128)S(1)}, u32[]{:S(2)}, u32[]{:S(2)}) collective-permute-start(f32[2,4,64,128]{3,2,1,0:T(8,128)S(1)} %get-tuple-element.33), channel_id=1, source_target_pairs={{0,16},{8,24},{16,0},{24,8},{1,17},{9,25},{17,1},{25,9},{2,18},{10... | collective-permute-start | bytes 786440 | tf_op jit(solution)/shard_map/ppermute | solution.py:96
  38.8 0.2 collective-permute-start.10
  39.0 0.0 collective-permute-done.8.refs_2_.refs_7_
  39.0 0.0 collective-permute-done.9.refs_4_.refs_2_
  39.0 1.5 %pack.13 = (f32[2,4,64,128]{3,2,1,0:T(8,128)S(1)}, f32[2,4,64,128]{3,2,1,0:T(8,128)S(1)}) custom-call(s32[6]{0:T(128)S(1)} %reshape_squeeze.3.plan, f32[4,20,64,128]{3,2,1,0:T(8,128)} %bitcast.16, f32[2,4,64,128]{3,2,1,0:T(8,128)S(1)} %collective-permute-done.7.refs_0_.refs_3_, f32[2,4,64,128]{3,2,1,0:T(8,128)S(1)} %collective-permute-done.4.refs_0_.refs_1_.refs_6_, ...), custom_call_target="tpu_custom_call" | custom-call | tf_op jit(solution)/shard_map/pack/pallas_call | solution.py:83
  40.5 4.7 %collective-permute-start.12 = (f32[2,4,64,128]{3,2,1,0:T(8,128)S(1)}, f32[2,4,64,128]{3,2,1,0:T(8,128)S(1)}, u32[]{:S(2)}, u32[]{:S(2)}) collective-permute-start(f32[2,4,64,128]{3,2,1,0:T(8,128)S(1)} %get-tuple-element.37), channel_id=1, source_target_pairs={{0,16},{8,24},{16,0},{24,8},{1,17},{9,25},{17,1},{25,9},{2,18},{10... | collective-permute-start | bytes 786440 | tf_op jit(solution)/shard_map/ppermute | solution.py:96
  45.3 4.0 %collective-permute-start.13 = (f32[2,4,64,128]{3,2,1,0:T(8,128)S(1)}, f32[2,4,64,128]{3,2,1,0:T(8,128)S(1)}, u32[]{:S(2)}, u32[]{:S(2)}) collective-permute-start(f32[2,4,64,128]{3,2,1,0:T(8,128)S(1)} %get-tuple-element.36.refs_2_), channel_id=1, source_target_pairs={{0,4},{1,5},{2,6},{3,7},{4,0},{5,1},{6,2},{7,3},{8,12},{9,13},{10,... | collective-permute-start | bytes 786440 | tf_op jit(solution)/shard_map/ppermute | solution.py:96
  49.3 1.0 pack.14.refs_2_
  50.3 0.0 copy-start.5
  50.3 0.9 collective-permute-start.11
  51.2 0.0 collective-permute-done.12.refs_1_.refs_4_
  51.2 3.9 %collective-permute-done.13.refs_3_.refs_8_ = f32[2,4,64,128]{3,2,1,0:T(8,128)S(1)} collective-permute-done((f32[2,4,64,128]{3,2,1,0:T(8,128)S(1)}, f32[2,4,64,128]{3,2,1,0:T(8,128)S(1)}, u32[]{:S(2)}, u32[]{:S(2)}) %collective-permute-start.13) | collective-permute-done | bytes 262176 | tf_op jit(solution)/shard_map/ppermute | solution.py:96
  55.1 1.0 pack.15.refs_9_.refs_6_
  56.1 4.3 %collective-permute-start.14 = (f32[2,4,64,128]{3,2,1,0:T(8,128)S(1)}, f32[2,4,64,128]{3,2,1,0:T(8,128)}, u32[]{:S(2)}, u32[]{:S(2)}) collective-permute-start(f32[2,4,64,128]{3,2,1,0:T(8,128)S(1)} %pack.15.refs_9_.refs_6_), channel_id=1, source_target_pairs={{0,4},{1,5},{2,6},{3,7},{4,0},{5,1},{6,2},{7,3},{8,12},{9,13},{10,... | collective-permute-start | bytes 786440 | tf_op jit(solution)/shard_map/ppermute | solution.py:96
  60.4 0.1 copy.7
  60.5 0.1 reshape.19.links
  60.7 4.5 %faces.2 = (f32[5,4,4,64,128]{4,3,2,1,0:T(8,128)}, f32[16,2,120,128]{3,2,1,0:T(8,128)}, f32[16,120,128]{2,1,0:T(8,128)}) custom-call(s32[6]{0:T(128)S(1)} %reshape_squeeze.3.plan, s32[1]{0:T(128)} %bitcast.place, s32[256]{0:T(256)S(1)} %reshape.19.links, f32[4,20,64,128]{3,2,1,0:T(8,128)} %bitcast.19, ...), custom_call_target="tpu_custom_call" | custom-call | tf_op jit(solution)/shard_map/faces/pallas_call | solution.py:291
  65.2 0.0 collective-permute-done.14.refs_5_
  65.2 3.9 %faces.3 = (f32[5,4,4,64,128]{4,3,2,1,0:T(8,128)}, f32[16,2,120,128]{3,2,1,0:T(8,128)}, f32[16,120,128]{2,1,0:T(8,128)}, f32[4,5,3,8,128]{4,3,2,1,0:T(8,128)S(1)}, f32[4,5,3,8,128]{4,3,2,1,0:T(8,128)S(1)}) custom-call(s32[6]{0:T(128)S(1)} %reshape_squeeze.3.plan, s32[1]{0:T(128)} %bitcast.place, ...), custom_call_target="tpu_custom_call", output_to_operand_aliasing={{0}: (11, {}), {1}: (12, {}), {2}: (13, {})} | custom-call | flops 999999995904 | bytes 10000000000 | tf_op jit(solution)/shard_map/faces/pallas_call | solution.py:291
  69.1 1.7 %collective-permute-start.15 = (f32[4,5,3,8,128]{4,3,2,1,0:T(8,128)S(1)}, f32[4,5,3,8,128]{4,3,2,1,0:T(8,128)S(1)}, u32[]{:S(2)}, u32[]{:S(2)}) collective-permute-start(f32[4,5,3,8,128]{4,3,2,1,0:T(8,128)S(1)} %get-tuple-element.42), channel_id=1, source_target_pairs={{0,1},{1,2},{2,3},{3,4},{4,5},{5,6},{6,7},{7,0},{8,9},{9,10},{10,1... | collective-permute-start | bytes 737288 | tf_op jit(solution)/shard_map/ppermute | solution.py:599
  70.7 2.5 %collective-permute-start.16 = (f32[4,5,3,8,128]{4,3,2,1,0:T(8,128)S(1)}, f32[4,5,3,8,128]{4,3,2,1,0:T(8,128)S(1)}, u32[]{:S(2)}, u32[]{:S(2)}) collective-permute-start(f32[4,5,3,8,128]{4,3,2,1,0:T(8,128)S(1)} %get-tuple-element.43), channel_id=1, source_target_pairs={{1,0},{2,1},{3,2},{4,3},{5,4},{6,5},{7,6},{0,7},{9,8},{10,9},{11,1... | collective-permute-start | bytes 737288 | tf_op jit(solution)/shard_map/ppermute | solution.py:600
  73.3 4.7 %all-to-all-start = ((f32[16,2,120,128]{3,2,1,0:T(8,128)}), f32[16,2,120,128]{3,2,1,0:T(8,128)}, u32[]{:S(2)}, u32[]{:S(2)}) async-start(f32[16,2,120,128]{3,2,1,0:T(8,128)} %get-tuple-element.46), calls=%async_computation | async-start | bytes 3932160 | tf_op jit(solution)/shard_map/all_to_all | solution.py:595
  77.9 2.6 %collective-permute-done.16.z_above = f32[4,5,3,8,128]{4,3,2,1,0:T(8,128)S(1)} collective-permute-done((f32[4,5,3,8,128]{4,3,2,1,0:T(8,128)S(1)}, f32[4,5,3,8,128]{4,3,2,1,0:T(8,128)S(1)}, u32[]{:S(2)}, u32[]{:S(2)}) %collective-permute-start.16) | collective-permute-done | bytes 245792 | tf_op jit(solution)/shard_map/ppermute | solution.py:600
  80.6 16.7 %inner.1 = (f32[5,4,4,64,128]{4,3,2,1,0:T(8,128)}, f32[2,2,5,5,4,8,128]{6,5,4,3,2,1,0:T(8,128)}, s32[48]{0:T(128)S(1)}) custom-call(s32[1]{0:T(128)} %bitcast.place, s32[256]{0:T(256)S(1)} %reshape.19.links, f32[5,4,4,64,128]{4,3,2,1,0:T(8,128)} %get-tuple-element.41.patches_in, f32[4,5,3,8,128]{4,3,2,1,0:T(8,128)S(1)} %collective-permute-done.15.z_below, ...), custom_call_target="tpu_custom_call" | custom-call | flops 999999995904 | bytes 10000000000 | tf_op jit(solution)/shard_map/inner/pallas_call | solution.py:475
  97.2 10.1 %all-to-all-done.arrived = f32[16,2,120,128]{3,2,1,0:T(8,128)} async-done(((f32[16,2,120,128]{3,2,1,0:T(8,128)}), f32[16,2,120,128]{3,2,1,0:T(8,128)}, u32[]{:S(2)}, u32[]{:S(2)}) %all-to-all-start) | async-done | bytes 1966112 | tf_op jit(solution)/shard_map/all_to_all | solution.py:595
  107.3 7.4 %outer.1 = f32[4,5,4,64,128]{4,3,2,1,0:T(8,128)} custom-call(s32[1]{0:T(128)} %bitcast.place, s32[48]{0:T(128)S(1)} %get-tuple-element.44.table, f32[2,2,5,5,4,8,128]{6,5,4,3,2,1,0:T(8,128)} %get-tuple-element.45.rim_in, f32[16,2,120,128]{3,2,1,0:T(8,128)} %all-to-all-done.arrived, f32[16,120,128]{2,1,0:T(8,128)} %get-tuple-element.47.own_items, ...), custom_call_target="tpu_custom_call" | custom-call | tf_op jit(solution)/shard_map/outer/pallas_call | solution.py:560
  (16 shorter events, 0.0 us)
Async XLA Ops:
  0.0 0.7 copy-start
  3.0 11.2 %collective-permute-start.2 = (f32[2,4,64,128]{3,2,1,0:T(8,128)S(1)}, f32[2,4,64,128]{3,2,1,0:T(8,128)S(1)}, u32[]{:S(2)}, u32[]{:S(2)}) collective-permute-start(f32[2,4,64,128]{3,2,1,0:T(8,128)S(1)} %get-tuple-element.29), channel_id=1, source_target_pairs={{0,64},{32,96},{64,0},{96,32},{1,65},{33,97},{65,1},{97,33},{2,66}... | collective-permute-start | bytes 786440 | tf_op jit(solution)/shard_map/ppermute | solution.py:96
  7.0 15.5 %collective-permute-start.1 = (f32[2,4,64,128]{3,2,1,0:T(8,128)S(1)}, f32[2,4,64,128]{3,2,1,0:T(8,128)S(1)}, u32[]{:S(2)}, u32[]{:S(2)}) collective-permute-start(f32[2,4,64,128]{3,2,1,0:T(8,128)S(1)} %get-tuple-element.28), channel_id=1, source_target_pairs={{0,64},{32,96},{64,0},{96,32},{1,65},{33,97},{65,1},{97,33},{2,66}... | collective-permute-start | bytes 786440 | tf_op jit(solution)/shard_map/ppermute | solution.py:96
  7.1 21.0 %collective-permute-start.4 = (f32[2,4,64,128]{3,2,1,0:T(8,128)S(1)}, f32[2,4,64,128]{3,2,1,0:T(8,128)S(1)}, u32[]{:S(2)}, u32[]{:S(2)}) collective-permute-start(f32[2,4,64,128]{3,2,1,0:T(8,128)S(1)} %get-tuple-element.31), channel_id=1, source_target_pairs={{0,64},{32,96},{64,0},{96,32},{1,65},{33,97},{65,1},{97,33},{2,66}... | collective-permute-start | bytes 786440 | tf_op jit(solution)/shard_map/ppermute | solution.py:96
  15.7 12.5 %collective-permute-start.5 = (f32[2,4,64,128]{3,2,1,0:T(8,128)S(1)}, f32[2,4,64,128]{3,2,1,0:T(8,128)S(1)}, u32[]{:S(2)}, u32[]{:S(2)}) collective-permute-start(f32[2,4,64,128]{3,2,1,0:T(8,128)S(1)} %pack.9.refs_1_), channel_id=1, source_target_pairs={{0,16},{8,24},{16,0},{24,8},{1,17},{9,25},{17,1},{25,9},{2,18},{10... | collective-permute-start | bytes 786440 | tf_op jit(solution)/shard_map/ppermute | solution.py:96
  19.1 14.5 %collective-permute-start = (f32[2,4,64,128]{3,2,1,0:T(8,128)S(1)}, f32[2,4,64,128]{3,2,1,0:T(8,128)S(1)}, u32[]{:S(2)}, u32[]{:S(2)}) collective-permute-start(f32[2,4,64,128]{3,2,1,0:T(8,128)S(1)} %get-tuple-element.27), channel_id=1, source_target_pairs={{0,64},{32,96},{64,0},{96,32},{1,65},{33,97},{65,1},{97,33},{2,66}... | collective-permute-start | bytes 786440 | tf_op jit(solution)/shard_map/ppermute | solution.py:96
  24.0 9.6 %collective-permute-start.3 = (f32[2,4,64,128]{3,2,1,0:T(8,128)S(1)}, f32[2,4,64,128]{3,2,1,0:T(8,128)S(1)}, u32[]{:S(2)}, u32[]{:S(2)}) collective-permute-start(f32[2,4,64,128]{3,2,1,0:T(8,128)S(1)} %pack.10.refs_3_), channel_id=1, source_target_pairs={{0,16},{8,24},{16,0},{24,8},{1,17},{9,25},{17,1},{25,9},{2,18},{10... | collective-permute-start | bytes 786440 | tf_op jit(solution)/shard_map/ppermute | solution.py:96
  24.8 14.3 %collective-permute-start.7 = (f32[2,4,64,128]{3,2,1,0:T(8,128)S(1)}, f32[2,4,64,128]{3,2,1,0:T(8,128)S(1)}, u32[]{:S(2)}, u32[]{:S(2)}) collective-permute-start(f32[2,4,64,128]{3,2,1,0:T(8,128)S(1)} %get-tuple-element.30.refs_1_), channel_id=1, source_target_pairs={{0,64},{32,96},{64,0},{96,32},{1,65},{33,97},{65,1},{97,33},{2,66}... | collective-permute-start | bytes 786440 | tf_op jit(solution)/shard_map/ppermute | solution.py:96
  29.6 9.4 %collective-permute-start.8 = (f32[2,4,64,128]{3,2,1,0:T(8,128)S(1)}, f32[2,4,64,128]{3,2,1,0:T(8,128)S(1)}, u32[]{:S(2)}, u32[]{:S(2)}) collective-permute-start(f32[2,4,64,128]{3,2,1,0:T(8,128)S(1)} %get-tuple-element.34), channel_id=1, source_target_pairs={{0,16},{8,24},{16,0},{24,8},{1,17},{9,25},{17,1},{25,9},{2,18},{10... | collective-permute-start | bytes 786440 | tf_op jit(solution)/shard_map/ppermute | solution.py:96
  30.4 8.6 %collective-permute-start.9 = (f32[2,4,64,128]{3,2,1,0:T(8,128)S(1)}, f32[2,4,64,128]{3,2,1,0:T(8,128)S(1)}, u32[]{:S(2)}, u32[]{:S(2)}) collective-permute-start(f32[2,4,64,128]{3,2,1,0:T(8,128)S(1)} %get-tuple-element.32.refs_3_), channel_id=1, source_target_pairs={{0,4},{1,5},{2,6},{3,7},{4,0},{5,1},{6,2},{7,3},{8,12},{9,13},{10,... | collective-permute-start | bytes 786440 | tf_op jit(solution)/shard_map/ppermute | solution.py:96
  35.1 14.2 %collective-permute-start.6 = (f32[2,4,64,128]{3,2,1,0:T(8,128)S(1)}, f32[2,4,64,128]{3,2,1,0:T(8,128)S(1)}, u32[]{:S(2)}, u32[]{:S(2)}) collective-permute-start(f32[2,4,64,128]{3,2,1,0:T(8,128)S(1)} %get-tuple-element.33), channel_id=1, source_target_pairs={{0,16},{8,24},{16,0},{24,8},{1,17},{9,25},{17,1},{25,9},{2,18},{10... | collective-permute-start | bytes 786440 | tf_op jit(solution)/shard_map/ppermute | solution.py:96
  38.8 10.5 %collective-permute-start.10 = (f32[2,4,64,128]{3,2,1,0:T(8,128)S(1)}, f32[2,4,64,128]{3,2,1,0:T(8,128)S(1)}, u32[]{:S(2)}, u32[]{:S(2)}) collective-permute-start(f32[2,4,64,128]{3,2,1,0:T(8,128)S(1)} %get-tuple-element.35.refs_3_), channel_id=1, source_target_pairs={{0,4},{1,5},{2,6},{3,7},{4,0},{5,1},{6,2},{7,3},{8,12},{9,13},{10,... | collective-permute-start | bytes 786440 | tf_op jit(solution)/shard_map/ppermute | solution.py:96
  40.5 10.7 %collective-permute-start.12 = (f32[2,4,64,128]{3,2,1,0:T(8,128)S(1)}, f32[2,4,64,128]{3,2,1,0:T(8,128)S(1)}, u32[]{:S(2)}, u32[]{:S(2)}) collective-permute-start(f32[2,4,64,128]{3,2,1,0:T(8,128)S(1)} %get-tuple-element.37), channel_id=1, source_target_pairs={{0,16},{8,24},{16,0},{24,8},{1,17},{9,25},{17,1},{25,9},{2,18},{10... | collective-permute-start | bytes 786440 | tf_op jit(solution)/shard_map/ppermute | solution.py:96
  45.3 9.8 %collective-permute-start.13 = (f32[2,4,64,128]{3,2,1,0:T(8,128)S(1)}, f32[2,4,64,128]{3,2,1,0:T(8,128)S(1)}, u32[]{:S(2)}, u32[]{:S(2)}) collective-permute-start(f32[2,4,64,128]{3,2,1,0:T(8,128)S(1)} %get-tuple-element.36.refs_2_), channel_id=1, source_target_pairs={{0,4},{1,5},{2,6},{3,7},{4,0},{5,1},{6,2},{7,3},{8,12},{9,13},{10,... | collective-permute-start | bytes 786440 | tf_op jit(solution)/shard_map/ppermute | solution.py:96
  49.3 6.8 %copy-start.1 = (f32[2,4,64,128]{3,2,1,0:T(8,128)}, f32[2,4,64,128]{3,2,1,0:T(8,128)S(1)}, u32[]{:S(2)}) copy-start(f32[2,4,64,128]{3,2,1,0:T(8,128)S(1)} %collective-permute-done.6.refs_1_) | copy-start | bytes 786436
  50.3 10.2 %copy-start.5 = (s32[64,4]{0,1:T(4,128)S(1)}, s32[64,4]{0,1:T(4,128)}, u32[]{:S(2)}) copy-start(s32[64,4]{0,1:T(4,128)} %param.5) | copy-start | bytes 3076
  50.3 14.9 %collective-permute-start.11 = (f32[2,4,64,128]{3,2,1,0:T(8,128)S(1)}, f32[2,4,64,128]{3,2,1,0:T(8,128)}, u32[]{:S(2)}, u32[]{:S(2)}) collective-permute-start(f32[2,4,64,128]{3,2,1,0:T(8,128)S(1)} %pack.14.refs_2_), channel_id=1, source_target_pairs={{0,4},{1,5},{2,6},{3,7},{4,0},{5,1},{6,2},{7,3},{8,12},{9,13},{10,... | collective-permute-start | bytes 786440 | tf_op jit(solution)/shard_map/ppermute | solution.py:96
  51.2 4.9 %copy-start.3 = (f32[2,4,64,128]{3,2,1,0:T(8,128)}, f32[2,4,64,128]{3,2,1,0:T(8,128)S(1)}, u32[]{:S(2)}) copy-start(f32[2,4,64,128]{3,2,1,0:T(8,128)S(1)} %collective-permute-done.12.refs_1_.refs_4_) | copy-start | bytes 786436
  56.1 9.0 %collective-permute-start.14 = (f32[2,4,64,128]{3,2,1,0:T(8,128)S(1)}, f32[2,4,64,128]{3,2,1,0:T(8,128)}, u32[]{:S(2)}, u32[]{:S(2)}) collective-permute-start(f32[2,4,64,128]{3,2,1,0:T(8,128)S(1)} %pack.15.refs_9_.refs_6_), channel_id=1, source_target_pairs={{0,4},{1,5},{2,6},{3,7},{4,0},{5,1},{6,2},{7,3},{8,12},{9,13},{10,... | collective-permute-start | bytes 786440 | tf_op jit(solution)/shard_map/ppermute | solution.py:96
  60.6 4.5 %copy-start.2 = (f32[2,4,64,128]{3,2,1,0:T(8,128)S(1)}, f32[2,4,64,128]{3,2,1,0:T(8,128)}, u32[]{:S(2)}) copy-start(f32[2,4,64,128]{3,2,1,0:T(8,128)} %copy-done.1) | copy-start | bytes 786436
  60.6 4.5 %copy-start.4 = (f32[2,4,64,128]{3,2,1,0:T(8,128)S(1)}, f32[2,4,64,128]{3,2,1,0:T(8,128)}, u32[]{:S(2)}) copy-start(f32[2,4,64,128]{3,2,1,0:T(8,128)} %copy-done.3) | copy-start | bytes 786436
  69.1 8.9 %collective-permute-start.15 = (f32[4,5,3,8,128]{4,3,2,1,0:T(8,128)S(1)}, f32[4,5,3,8,128]{4,3,2,1,0:T(8,128)S(1)}, u32[]{:S(2)}, u32[]{:S(2)}) collective-permute-start(f32[4,5,3,8,128]{4,3,2,1,0:T(8,128)S(1)} %get-tuple-element.42), channel_id=1, source_target_pairs={{0,1},{1,2},{2,3},{3,4},{4,5},{5,6},{6,7},{7,0},{8,9},{9,10},{10,1... | collective-permute-start | bytes 737288 | tf_op jit(solution)/shard_map/ppermute | solution.py:599
  70.7 9.8 %collective-permute-start.16 = (f32[4,5,3,8,128]{4,3,2,1,0:T(8,128)S(1)}, f32[4,5,3,8,128]{4,3,2,1,0:T(8,128)S(1)}, u32[]{:S(2)}, u32[]{:S(2)}) collective-permute-start(f32[4,5,3,8,128]{4,3,2,1,0:T(8,128)S(1)} %get-tuple-element.43), channel_id=1, source_target_pairs={{1,0},{2,1},{3,2},{4,3},{5,4},{6,5},{7,6},{0,7},{9,8},{10,9},{11,1... | collective-permute-start | bytes 737288 | tf_op jit(solution)/shard_map/ppermute | solution.py:600
  73.3 34.1 %all-to-all-start = ((f32[16,2,120,128]{3,2,1,0:T(8,128)}), f32[16,2,120,128]{3,2,1,0:T(8,128)}, u32[]{:S(2)}, u32[]{:S(2)}) async-start(f32[16,2,120,128]{3,2,1,0:T(8,128)} %get-tuple-element.46), calls=%async_computation | async-start | bytes 3932160 | tf_op jit(solution)/shard_map/all_to_all | solution.py:595

commit v4 on v3

--- a/solution.py
+++ b/solution.py
@@ -97,14 +97,16 @@
 
 
 WAVES = (
-    ([(0, 0), (0, 1), (0, 2), (0, 3), (0, 4)], []),
+    ([(0, 0)], []),
+    ([(0, 1), (0, 2)], []),
+    ([(0, 3), (0, 4)], []),
     ([(1, 0)], []),
     ([(1, 1)], []),
     ([(1, 2), (2, 0)], []),
     ([(1, 3), (2, 1)], []),
     ([(1, 4), (2, 2)], [(2, 0)]),
     ([(2, 3)], [(2, 1)]),
-    ([(2, 4)], [(2, 2)]),
+    ([(2, 4)], [(2, 1)]),
 )
 
 
@@ -213,13 +215,16 @@
     for load in loads:
         load.start()
 
-    whole = pltpu.make_async_copy(patches, patches_out.at[pl.ds(first, count)], out_sem)
+    whole = [
+        pltpu.make_async_copy(patches.at[n], patches_out.at[f], out_sem.at[n])
+        for n, f in enumerate(fields)
+    ]
     for n, f in enumerate(fields):
         for at, size, target, sem in parts:
             if at == n:
                 wait_copy(cells, size, target, sem)
+        whole[n].start()
         turn(patches, turned, n)
-    whole.start()
 
     me = place[0]
     owners = [links[me * LINKS + i] // SLOTS for i in range(LINKS)]
@@ -267,7 +272,8 @@
 
     for i in range(LINKS):
         pltpu.make_async_copy(items.at[i], own_items.at[i, rows], item_sems.at[i]).wait()
-    whole.wait()
+    for copy in whole:
+        copy.wait()
 
 
 def faces(fields, plan, place, links, cells, received, after, carried):
@@ -280,7 +286,7 @@
         pltpu.VMEM((LINKS, count * GHOST * 8, 128), F32),
         pltpu.SemaphoreType.DMA((count, SLOTS, 2)),
         pltpu.SemaphoreType.DMA((LINKS,)),
-        pltpu.SemaphoreType.DMA,
+        pltpu.SemaphoreType.DMA((count,)),
     ]
     if last:
         scratch = [

time: 114 us -> 114 us (level); the launches traced: 115 us -> 113 us
  Pallas kernels: 43.8 us -> 48.9 us
  waiting for transfers between devices: 20.3 us -> 15.8 us
  starting transfers between devices: 49.2 us -> 47 us
    ppermute x15, waiting for transfers between devices: 7.55 us -> 3.04 us  [swapped(): lax.ppermute(block, axis, [(i, i ^ count // 2) for i in range(count)])]
    pallas_call x8 -> x10, Pallas kernels: 11.4 us -> 15.3 us  [pack(): pl.pallas_call(functools.partial(pack_kernel, sends, len(received)), out_...]
    ppermute x15, starting transfers between devices: 40.4 us -> 37.9 us  [swapped(): lax.ppermute(block, axis, [(i, i ^ count // 2) for i in range(count)])]
    all_to_all x1, waiting for transfers between devices: 10.1 us -> 11.6 us  [local(): arrived = lax.all_to_all(send, ('gx', 'gy'), 0, 0, tiled=True)]
    ppermute x1, waiting for transfers between devices: 2.62 us -> 1.11 us  [local(): z_above = lax.ppermute(z_first, 'gz', down)]
    pallas_call x2, Pallas kernels: 8.36 us -> 9.51 us  [faces(): pl.pallas_call(functools.partial(faces_kernel, fields), out_shape=[pltpu....]
  transfers between devices with their start and end apart: 18 -> 18, of which waited for: 4 -> 5; matrix products, arithmetic and copies ran while one was open for 0% -> 0% of each run, Pallas kernels for 27% -> 32%
where the time goes in v4:
time: 114 us; the launch traced here: 113 us
  Pallas kernels  48.9 us (43%)
  starting transfers between devices  47 us (41%)
  waiting for transfers between devices  15.8 us (14%)
  local copies, waits for them, and re-layouts  1.2 us (1%)
    ppermute x15, starting transfers between devices, swapped(): lax.ppermute(block, axis, [(i, i ^ count // 2) for i in range(count)])  37.9 us
    pallas_call x1, Pallas kernels, inner(): pl.pallas_call(inner_kernel, out_shape=[pltpu.HBM(PATCH_SHAPE, F32), pltp...  16.7 us
    pallas_call x10, Pallas kernels, pack(): pl.pallas_call(functools.partial(pack_kernel, sends, len(received)), out_...  15.3 us
    all_to_all x1, waiting for transfers between devices, local(): arrived = lax.all_to_all(send, ('gx', 'gy'), 0, 0, tiled=True)  11.6 us
    pallas_call x2, Pallas kernels, faces(): pl.pallas_call(functools.partial(faces_kernel, fields), out_shape=[pltpu....  9.51 us
    pallas_call x1, Pallas kernels, outer(): pl.pallas_call(outer_kernel, out_shape=jax.ShapeDtypeStruct((SLOTS, FIELD...  7.35 us
    all_to_all x1, starting transfers between devices, local(): arrived = lax.all_to_all(send, ('gx', 'gy'), 0, 0, tiled=True)  4.83 us
    ppermute x1, starting transfers between devices, local(): z_above = lax.ppermute(z_first, 'gz', down)  3.4 us
  transfers between devices with their start and end apart: 18, of which 5 were waited for; matrix products, arithmetic and copies ran while one was open for 0% of the time, Pallas kernels for 32%

profile of v4, /device:TPU:0, one launch (start us, length us, event | category | flops | bytes accessed | tf_op | source)
XLA Modules:
  0.0 113.2 jit_solution(18195580343137045672)
XLA Ops:
  0.0 0.7 copy-done
  0.7 0.2 dynamic-slice_reduce_fusion
  0.9 0.1 reshape_squeeze.3.plan
  1.0 1.5 %pack.10.refs_0_ = f32[2,4,64,128]{3,2,1,0:T(8,128)S(1)} custom-call(s32[6]{0:T(128)S(1)} %reshape_squeeze.3.plan, f32[4,20,64,128]{3,2,1,0:T(8,128)} %bitcast.11), custom_call_target="tpu_custom_call" | custom-call | tf_op jit(solution)/shard_map/pack/pallas_call | solution.py:83
  2.5 4.0 %collective-permute-start.2 = (f32[2,4,64,128]{3,2,1,0:T(8,128)S(1)}, f32[2,4,64,128]{3,2,1,0:T(8,128)S(1)}, u32[]{:S(2)}, u32[]{:S(2)}) collective-permute-start(f32[2,4,64,128]{3,2,1,0:T(8,128)S(1)} %pack.10.refs_0_), channel_id=1, source_target_pairs={{0,64},{32,96},{64,0},{96,32},{1,65},{33,97},{65,1},{97,33},{2,66}... | collective-permute-start | bytes 786440 | tf_op jit(solution)/shard_map/ppermute | solution.py:96
  6.6 1.7 %pack.11 = (f32[2,4,64,128]{3,2,1,0:T(8,128)S(1)}, f32[2,4,64,128]{3,2,1,0:T(8,128)S(1)}) custom-call(s32[6]{0:T(128)S(1)} %reshape_squeeze.3.plan, f32[4,20,64,128]{3,2,1,0:T(8,128)} %bitcast.12, f32[2,4,64,128]{3,2,1,0:T(8,128)S(1)} %pack.10.refs_0_), custom_call_target="tpu_custom_call" | custom-call | tf_op jit(solution)/shard_map/pack/pallas_call | solution.py:83
  8.2 0.1 collective-permute-start.1
  8.3 3.5 %collective-permute-start.4 = (f32[2,4,64,128]{3,2,1,0:T(8,128)S(1)}, f32[2,4,64,128]{3,2,1,0:T(8,128)S(1)}, u32[]{:S(2)}, u32[]{:S(2)}) collective-permute-start(f32[2,4,64,128]{3,2,1,0:T(8,128)S(1)} %get-tuple-element.26.refs_0_), channel_id=1, source_target_pairs={{0,64},{32,96},{64,0},{96,32},{1,65},{33,97},{65,1},{97,33},{2,66}... | collective-permute-start | bytes 786440 | tf_op jit(solution)/shard_map/ppermute | solution.py:96
  11.9 1.7 %pack.12 = (f32[2,4,64,128]{3,2,1,0:T(8,128)S(1)}, f32[2,4,64,128]{3,2,1,0:T(8,128)S(1)}) custom-call(s32[6]{0:T(128)S(1)} %reshape_squeeze.3.plan, f32[4,20,64,128]{3,2,1,0:T(8,128)} %bitcast.13, f32[2,4,64,128]{3,2,1,0:T(8,128)S(1)} %get-tuple-element.26.refs_0_), custom_call_target="tpu_custom_call" | custom-call | tf_op jit(solution)/shard_map/pack/pallas_call | solution.py:83
  13.5 0.2 collective-permute-done.2.refs_0_.refs_1_
  13.7 1.5 %pack.13.refs_1_ = f32[2,4,64,128]{3,2,1,0:T(8,128)S(1)} custom-call(s32[6]{0:T(128)S(1)} %reshape_squeeze.3.plan, f32[4,20,64,128]{3,2,1,0:T(8,128)} %bitcast.14, f32[2,4,64,128]{3,2,1,0:T(8,128)S(1)} %collective-permute-done.2.refs_0_.refs_1_, f32[2,4,64,128]{3,2,1,0:T(8,128)S(1)} %get-tuple-element.29.refs_1_), custom_call_target="tpu_custom_call" | custom-call | tf_op jit(solution)/shard_map/pack/pallas_call | solution.py:83
  15.3 2.7 %collective-permute-start.5 = (f32[2,4,64,128]{3,2,1,0:T(8,128)S(1)}, f32[2,4,64,128]{3,2,1,0:T(8,128)S(1)}, u32[]{:S(2)}, u32[]{:S(2)}) collective-permute-start(f32[2,4,64,128]{3,2,1,0:T(8,128)S(1)} %pack.13.refs_1_), channel_id=1, source_target_pairs={{0,16},{8,24},{16,0},{24,8},{1,17},{9,25},{17,1},{25,9},{2,18},{10... | collective-permute-start | bytes 786440 | tf_op jit(solution)/shard_map/ppermute | solution.py:96
  17.9 4.1 %collective-permute-start = (f32[2,4,64,128]{3,2,1,0:T(8,128)S(1)}, f32[2,4,64,128]{3,2,1,0:T(8,128)S(1)}, u32[]{:S(2)}, u32[]{:S(2)}) collective-permute-start(f32[2,4,64,128]{3,2,1,0:T(8,128)S(1)} %get-tuple-element.27), channel_id=1, source_target_pairs={{0,64},{32,96},{64,0},{96,32},{1,65},{33,97},{65,1},{97,33},{2,66}... | collective-permute-start | bytes 786440 | tf_op jit(solution)/shard_map/ppermute | solution.py:96
  22.0 0.0 collective-permute-done.1.refs_0_.refs_1_.refs_3_
  22.0 1.5 %pack.14.refs_3_ = f32[2,4,64,128]{3,2,1,0:T(8,128)S(1)} custom-call(s32[6]{0:T(128)S(1)} %reshape_squeeze.3.plan, f32[4,20,64,128]{3,2,1,0:T(8,128)} %bitcast.15, f32[2,4,64,128]{3,2,1,0:T(8,128)S(1)} %collective-permute-done.1.refs_0_.refs_1_.refs_3_, f32[2,4,64,128]{3,2,1,0:T(8,128)S(1)} %pack.13.refs_1_), custom_call_target="tpu_custom_call" | custom-call | tf_op jit(solution)/shard_map/pack/pallas_call | solution.py:83
  23.6 0.1 collective-permute-start.3
  23.7 4.0 %collective-permute-start.7 = (f32[2,4,64,128]{3,2,1,0:T(8,128)S(1)}, f32[2,4,64,128]{3,2,1,0:T(8,128)S(1)}, u32[]{:S(2)}, u32[]{:S(2)}) collective-permute-start(f32[2,4,64,128]{3,2,1,0:T(8,128)S(1)} %get-tuple-element.29.refs_1_), channel_id=1, source_target_pairs={{0,64},{32,96},{64,0},{96,32},{1,65},{33,97},{65,1},{97,33},{2,66}... | collective-permute-start | bytes 786440 | tf_op jit(solution)/shard_map/ppermute | solution.py:96
  27.6 0.0 collective-permute-done.4.refs_0_.refs_1_.refs_6_
  27.7 0.0 collective-permute-done.5.refs_2_.refs_1_
  27.7 1.6 %pack.15 = (f32[2,4,64,128]{3,2,1,0:T(8,128)S(1)}, f32[2,4,64,128]{3,2,1,0:T(8,128)S(1)}) custom-call(s32[6]{0:T(128)S(1)} %reshape_squeeze.3.plan, f32[4,20,64,128]{3,2,1,0:T(8,128)} %bitcast.16, f32[2,4,64,128]{3,2,1,0:T(8,128)S(1)} %collective-permute-done.4.refs_0_.refs_1_.refs_6_, f32[2,4,64,128]{3,2,1,0:T(8,128)S(1)} %collective-permute-done.2.refs_0_.refs_1_, ...), custom_call_target="tpu_custom_call" | custom-call | tf_op jit(solution)/shard_map/pack/pallas_call | solution.py:83
  29.2 0.9 collective-permute-start.8
  30.1 2.8 %collective-permute-start.9 = (f32[2,4,64,128]{3,2,1,0:T(8,128)S(1)}, f32[2,4,64,128]{3,2,1,0:T(8,128)S(1)}, u32[]{:S(2)}, u32[]{:S(2)}) collective-permute-start(f32[2,4,64,128]{3,2,1,0:T(8,128)S(1)} %get-tuple-element.30.refs_3_), channel_id=1, source_target_pairs={{0,4},{1,5},{2,6},{3,7},{4,0},{5,1},{6,2},{7,3},{8,12},{9,13},{10,... | collective-permute-start | bytes 786440 | tf_op jit(solution)/shard_map/ppermute | solution.py:96
  32.9 0.0 collective-permute-done.3.refs_2_.refs_4_
  32.9 1.6 %pack.16 = (f32[2,4,64,128]{3,2,1,0:T(8,128)S(1)}, f32[2,4,64,128]{3,2,1,0:T(8,128)S(1)}) custom-call(s32[6]{0:T(128)S(1)} %reshape_squeeze.3.plan, f32[4,20,64,128]{3,2,1,0:T(8,128)} %bitcast.17, f32[2,4,64,128]{3,2,1,0:T(8,128)S(1)} %collective-permute-done.refs_0_, f32[2,4,64,128]{3,2,1,0:T(8,128)S(1)} %collective-permute-done.1.refs_0_.refs_1_.refs_3_, ...), custom_call_target="tpu_custom_call" | custom-call | tf_op jit(solution)/shard_map/pack/pallas_call | solution.py:83
  34.5 3.5 %collective-permute-start.6 = (f32[2,4,64,128]{3,2,1,0:T(8,128)S(1)}, f32[2,4,64,128]{3,2,1,0:T(8,128)S(1)}, u32[]{:S(2)}, u32[]{:S(2)}) collective-permute-start(f32[2,4,64,128]{3,2,1,0:T(8,128)S(1)} %get-tuple-element.31), channel_id=1, source_target_pairs={{0,16},{8,24},{16,0},{24,8},{1,17},{9,25},{17,1},{25,9},{2,18},{10... | collective-permute-start | bytes 786440 | tf_op jit(solution)/shard_map/ppermute | solution.py:96
  38.0 0.5 collective-permute-start.10
  38.6 0.0 collective-permute-done.7.refs_0_.refs_3_
  38.6 2.3 %pack.17 = (f32[2,4,64,128]{3,2,1,0:T(8,128)S(1)}, f32[2,4,64,128]{3,2,1,0:T(8,128)}) custom-call(s32[6]{0:T(128)S(1)} %reshape_squeeze.3.plan, f32[4,20,64,128]{3,2,1,0:T(8,128)} %bitcast.18, f32[2,4,64,128]{3,2,1,0:T(8,128)S(1)} %collective-permute-done.7.refs_0_.refs_3_, f32[2,4,64,128]{3,2,1,0:T(8,128)S(1)} %collective-permute-done.4.refs_0_.refs_1_.refs_6_, ...), custom_call_target="tpu_custom_call" | custom-call | tf_op jit(solution)/shard_map/pack/pallas_call | solution.py:83
  40.8 4.3 %collective-permute-start.12 = (f32[2,4,64,128]{3,2,1,0:T(8,128)S(1)}, f32[2,4,64,128]{3,2,1,0:T(8,128)S(1)}, u32[]{:S(2)}, u32[]{:S(2)}) collective-permute-start(f32[2,4,64,128]{3,2,1,0:T(8,128)S(1)} %get-tuple-element.35), channel_id=1, source_target_pairs={{0,16},{8,24},{16,0},{24,8},{1,17},{9,25},{17,1},{25,9},{2,18},{10... | collective-permute-start | bytes 786440 | tf_op jit(solution)/shard_map/ppermute | solution.py:96
  45.1 3.8 %collective-permute-start.14 = (f32[2,4,64,128]{3,2,1,0:T(8,128)}, f32[2,4,64,128]{3,2,1,0:T(8,128)}, u32[]{:S(2)}, u32[]{:S(2)}) collective-permute-start(f32[2,4,64,128]{3,2,1,0:T(8,128)} %get-tuple-element.34.refs_2_), channel_id=1, source_target_pairs={{0,4},{1,5},{2,6},{3,7},{4,0},{5,1},{6,2},{7,3},{8,12},{9,13},{10,... | collective-permute-start | bytes 786440 | tf_op jit(solution)/shard_map/ppermute | solution.py:96
  48.9 1.0 pack.18.refs_2_
  49.9 0.0 copy-start.3
  49.9 0.1 collective-permute-start.11
  50.0 1.0 pack.19.refs_9_.refs_6_
  51.0 3.6 %collective-permute-start.13 = (f32[2,4,64,128]{3,2,1,0:T(8,128)S(1)}, f32[2,4,64,128]{3,2,1,0:T(8,128)}, u32[]{:S(2)}, u32[]{:S(2)}) collective-permute-start(f32[2,4,64,128]{3,2,1,0:T(8,128)S(1)} %pack.19.refs_9_.refs_6_), channel_id=1, source_target_pairs={{0,4},{1,5},{2,6},{3,7},{4,0},{5,1},{6,2},{7,3},{8,12},{9,13},{10,... | collective-permute-start | bytes 786440 | tf_op jit(solution)/shard_map/ppermute | solution.py:96
  54.6 0.1 copy.7
  54.7 0.1 reshape.19.links
  54.8 1.7 %collective-permute-done.14.refs_8_ = f32[2,4,64,128]{3,2,1,0:T(8,128)} collective-permute-done((f32[2,4,64,128]{3,2,1,0:T(8,128)}, f32[2,4,64,128]{3,2,1,0:T(8,128)}, u32[]{:S(2)}, u32[]{:S(2)}) %collective-permute-start.14) | collective-permute-done | bytes 262176 | tf_op jit(solution)/shard_map/ppermute | solution.py:96
  56.5 5.2 %faces.2 = (f32[5,4,4,64,128]{4,3,2,1,0:T(8,128)}, f32[16,2,120,128]{3,2,1,0:T(8,128)}, f32[16,120,128]{2,1,0:T(8,128)}) custom-call(s32[6]{0:T(128)S(1)} %reshape_squeeze.3.plan, s32[1]{0:T(128)} %bitcast.place, s32[256]{0:T(256)S(1)} %reshape.19.links, f32[4,20,64,128]{3,2,1,0:T(8,128)} %bitcast.21, ...), custom_call_target="tpu_custom_call" | custom-call | tf_op jit(solution)/shard_map/faces/pallas_call | solution.py:297
  61.7 1.2 %collective-permute-done.13.refs_5_ = f32[2,4,64,128]{3,2,1,0:T(8,128)} collective-permute-done((f32[2,4,64,128]{3,2,1,0:T(8,128)S(1)}, f32[2,4,64,128]{3,2,1,0:T(8,128)}, u32[]{:S(2)}, u32[]{:S(2)}) %collective-permute-start.13) | collective-permute-done | bytes 262176 | tf_op jit(solution)/shard_map/ppermute | solution.py:96
  62.9 4.3 %faces.3 = (f32[5,4,4,64,128]{4,3,2,1,0:T(8,128)}, f32[16,2,120,128]{3,2,1,0:T(8,128)}, f32[16,120,128]{2,1,0:T(8,128)}, f32[4,5,3,8,128]{4,3,2,1,0:T(8,128)S(1)}, f32[4,5,3,8,128]{4,3,2,1,0:T(8,128)S(1)}) custom-call(s32[6]{0:T(128)S(1)} %reshape_squeeze.3.plan, s32[1]{0:T(128)} %bitcast.place, ...), custom_call_target="tpu_custom_call", output_to_operand_aliasing={{0}: (11, {}), {1}: (12, {}), {2}: (13, {})} | custom-call | flops 999999995904 | bytes 10000000000 | tf_op jit(solution)/shard_map/faces/pallas_call | solution.py:297
  67.2 0.8 collective-permute-start.15
  68.0 3.4 %collective-permute-start.16 = (f32[4,5,3,8,128]{4,3,2,1,0:T(8,128)S(1)}, f32[4,5,3,8,128]{4,3,2,1,0:T(8,128)S(1)}, u32[]{:S(2)}, u32[]{:S(2)}) collective-permute-start(f32[4,5,3,8,128]{4,3,2,1,0:T(8,128)S(1)} %get-tuple-element.41), channel_id=1, source_target_pairs={{1,0},{2,1},{3,2},{4,3},{5,4},{6,5},{7,6},{0,7},{9,8},{10,9},{11,1... | collective-permute-start | bytes 737288 | tf_op jit(solution)/shard_map/ppermute | solution.py:606
  71.4 4.8 %all-to-all-start = ((f32[16,2,120,128]{3,2,1,0:T(8,128)}), f32[16,2,120,128]{3,2,1,0:T(8,128)}, u32[]{:S(2)}, u32[]{:S(2)}) async-start(f32[16,2,120,128]{3,2,1,0:T(8,128)} %get-tuple-element.44), calls=%async_computation | async-start | bytes 3932160 | tf_op jit(solution)/shard_map/all_to_all | solution.py:601
  76.2 1.1 collective-permute-done.16.z_above
  77.3 16.7 %inner.1 = (f32[5,4,4,64,128]{4,3,2,1,0:T(8,128)}, f32[2,2,5,5,4,8,128]{6,5,4,3,2,1,0:T(8,128)}, s32[48]{0:T(128)S(1)}) custom-call(s32[1]{0:T(128)} %bitcast.place, s32[256]{0:T(256)S(1)} %reshape.19.links, f32[5,4,4,64,128]{4,3,2,1,0:T(8,128)} %get-tuple-element.39.patches_in, f32[4,5,3,8,128]{4,3,2,1,0:T(8,128)S(1)} %collective-permute-done.15.z_below, ...), custom_call_target="tpu_custom_call" | custom-call | flops 999999995904 | bytes 10000000000 | tf_op jit(solution)/shard_map/inner/pallas_call | solution.py:481
  94.0 11.6 %all-to-all-done.arrived = f32[16,2,120,128]{3,2,1,0:T(8,128)} async-done(((f32[16,2,120,128]{3,2,1,0:T(8,128)}), f32[16,2,120,128]{3,2,1,0:T(8,128)}, u32[]{:S(2)}, u32[]{:S(2)}) %all-to-all-start) | async-done | bytes 1966112 | tf_op jit(solution)/shard_map/all_to_all | solution.py:601
  105.6 7.4 %outer.1 = f32[4,5,4,64,128]{4,3,2,1,0:T(8,128)} custom-call(s32[1]{0:T(128)} %bitcast.place, s32[48]{0:T(128)S(1)} %get-tuple-element.42.table, f32[2,2,5,5,4,8,128]{6,5,4,3,2,1,0:T(8,128)} %get-tuple-element.43.rim_in, f32[16,2,120,128]{3,2,1,0:T(8,128)} %all-to-all-done.arrived, f32[16,120,128]{2,1,0:T(8,128)} %get-tuple-element.45.own_items, ...), custom_call_target="tpu_custom_call" | custom-call | tf_op jit(solution)/shard_map/outer/pallas_call | solution.py:566
  (14 shorter events, 0.0 us)
Async XLA Ops:
  0.0 0.7 copy-start
  2.5 11.2 %collective-permute-start.2 = (f32[2,4,64,128]{3,2,1,0:T(8,128)S(1)}, f32[2,4,64,128]{3,2,1,0:T(8,128)S(1)}, u32[]{:S(2)}, u32[]{:S(2)}) collective-permute-start(f32[2,4,64,128]{3,2,1,0:T(8,128)S(1)} %pack.10.refs_0_), channel_id=1, source_target_pairs={{0,64},{32,96},{64,0},{96,32},{1,65},{33,97},{65,1},{97,33},{2,66}... | collective-permute-start | bytes 786440 | tf_op jit(solution)/shard_map/ppermute | solution.py:96
  8.2 13.8 %collective-permute-start.1 = (f32[2,4,64,128]{3,2,1,0:T(8,128)S(1)}, f32[2,4,64,128]{3,2,1,0:T(8,128)S(1)}, u32[]{:S(2)}, u32[]{:S(2)}) collective-permute-start(f32[2,4,64,128]{3,2,1,0:T(8,128)S(1)} %get-tuple-element.28), channel_id=1, source_target_pairs={{0,64},{32,96},{64,0},{96,32},{1,65},{33,97},{65,1},{97,33},{2,66}... | collective-permute-start | bytes 786440 | tf_op jit(solution)/shard_map/ppermute | solution.py:96
  8.3 19.3 %collective-permute-start.4 = (f32[2,4,64,128]{3,2,1,0:T(8,128)S(1)}, f32[2,4,64,128]{3,2,1,0:T(8,128)S(1)}, u32[]{:S(2)}, u32[]{:S(2)}) collective-permute-start(f32[2,4,64,128]{3,2,1,0:T(8,128)S(1)} %get-tuple-element.26.refs_0_), channel_id=1, source_target_pairs={{0,64},{32,96},{64,0},{96,32},{1,65},{33,97},{65,1},{97,33},{2,66}... | collective-permute-start | bytes 786440 | tf_op jit(solution)/shard_map/ppermute | solution.py:96
  15.3 12.4 %collective-permute-start.5 = (f32[2,4,64,128]{3,2,1,0:T(8,128)S(1)}, f32[2,4,64,128]{3,2,1,0:T(8,128)S(1)}, u32[]{:S(2)}, u32[]{:S(2)}) collective-permute-start(f32[2,4,64,128]{3,2,1,0:T(8,128)S(1)} %pack.13.refs_1_), channel_id=1, source_target_pairs={{0,16},{8,24},{16,0},{24,8},{1,17},{9,25},{17,1},{25,9},{2,18},{10... | collective-permute-start | bytes 786440 | tf_op jit(solution)/shard_map/ppermute | solution.py:96
  17.9 15.0 %collective-permute-start = (f32[2,4,64,128]{3,2,1,0:T(8,128)S(1)}, f32[2,4,64,128]{3,2,1,0:T(8,128)S(1)}, u32[]{:S(2)}, u32[]{:S(2)}) collective-permute-start(f32[2,4,64,128]{3,2,1,0:T(8,128)S(1)} %get-tuple-element.27), channel_id=1, source_target_pairs={{0,64},{32,96},{64,0},{96,32},{1,65},{33,97},{65,1},{97,33},{2,66}... | collective-permute-start | bytes 786440 | tf_op jit(solution)/shard_map/ppermute | solution.py:96
  23.6 9.4 %collective-permute-start.3 = (f32[2,4,64,128]{3,2,1,0:T(8,128)S(1)}, f32[2,4,64,128]{3,2,1,0:T(8,128)S(1)}, u32[]{:S(2)}, u32[]{:S(2)}) collective-permute-start(f32[2,4,64,128]{3,2,1,0:T(8,128)S(1)} %pack.14.refs_3_), channel_id=1, source_target_pairs={{0,16},{8,24},{16,0},{24,8},{1,17},{9,25},{17,1},{25,9},{2,18},{10... | collective-permute-start | bytes 786440 | tf_op jit(solution)/shard_map/ppermute | solution.py:96
  23.7 14.9 %collective-permute-start.7 = (f32[2,4,64,128]{3,2,1,0:T(8,128)S(1)}, f32[2,4,64,128]{3,2,1,0:T(8,128)S(1)}, u32[]{:S(2)}, u32[]{:S(2)}) collective-permute-start(f32[2,4,64,128]{3,2,1,0:T(8,128)S(1)} %get-tuple-element.29.refs_1_), channel_id=1, source_target_pairs={{0,64},{32,96},{64,0},{96,32},{1,65},{33,97},{65,1},{97,33},{2,66}... | collective-permute-start | bytes 786440 | tf_op jit(solution)/shard_map/ppermute | solution.py:96
  29.2 9.3 %collective-permute-start.8 = (f32[2,4,64,128]{3,2,1,0:T(8,128)S(1)}, f32[2,4,64,128]{3,2,1,0:T(8,128)S(1)}, u32[]{:S(2)}, u32[]{:S(2)}) collective-permute-start(f32[2,4,64,128]{3,2,1,0:T(8,128)S(1)} %get-tuple-element.32), channel_id=1, source_target_pairs={{0,16},{8,24},{16,0},{24,8},{1,17},{9,25},{17,1},{25,9},{2,18},{10... | collective-permute-start | bytes 786440 | tf_op jit(solution)/shard_map/ppermute | solution.py:96
  30.1 8.4 %collective-permute-start.9 = (f32[2,4,64,128]{3,2,1,0:T(8,128)S(1)}, f32[2,4,64,128]{3,2,1,0:T(8,128)S(1)}, u32[]{:S(2)}, u32[]{:S(2)}) collective-permute-start(f32[2,4,64,128]{3,2,1,0:T(8,128)S(1)} %get-tuple-element.30.refs_3_), channel_id=1, source_target_pairs={{0,4},{1,5},{2,6},{3,7},{4,0},{5,1},{6,2},{7,3},{8,12},{9,13},{10,... | collective-permute-start | bytes 786440 | tf_op jit(solution)/shard_map/ppermute | solution.py:96
  34.5 14.4 %collective-permute-start.6 = (f32[2,4,64,128]{3,2,1,0:T(8,128)S(1)}, f32[2,4,64,128]{3,2,1,0:T(8,128)S(1)}, u32[]{:S(2)}, u32[]{:S(2)}) collective-permute-start(f32[2,4,64,128]{3,2,1,0:T(8,128)S(1)} %get-tuple-element.31), channel_id=1, source_target_pairs={{0,16},{8,24},{16,0},{24,8},{1,17},{9,25},{17,1},{25,9},{2,18},{10... | collective-permute-start | bytes 786440 | tf_op jit(solution)/shard_map/ppermute | solution.py:96
  38.0 10.9 %collective-permute-start.10 = (f32[2,4,64,128]{3,2,1,0:T(8,128)S(1)}, f32[2,4,64,128]{3,2,1,0:T(8,128)S(1)}, u32[]{:S(2)}, u32[]{:S(2)}) collective-permute-start(f32[2,4,64,128]{3,2,1,0:T(8,128)S(1)} %get-tuple-element.33.refs_3_), channel_id=1, source_target_pairs={{0,4},{1,5},{2,6},{3,7},{4,0},{5,1},{6,2},{7,3},{8,12},{9,13},{10,... | collective-permute-start | bytes 786440 | tf_op jit(solution)/shard_map/ppermute | solution.py:96
  40.8 9.2 %collective-permute-start.12 = (f32[2,4,64,128]{3,2,1,0:T(8,128)S(1)}, f32[2,4,64,128]{3,2,1,0:T(8,128)S(1)}, u32[]{:S(2)}, u32[]{:S(2)}) collective-permute-start(f32[2,4,64,128]{3,2,1,0:T(8,128)S(1)} %get-tuple-element.35), channel_id=1, source_target_pairs={{0,16},{8,24},{16,0},{24,8},{1,17},{9,25},{17,1},{25,9},{2,18},{10... | collective-permute-start | bytes 786440 | tf_op jit(solution)/shard_map/ppermute | solution.py:96
  45.1 11.3 %collective-permute-start.14 = (f32[2,4,64,128]{3,2,1,0:T(8,128)}, f32[2,4,64,128]{3,2,1,0:T(8,128)}, u32[]{:S(2)}, u32[]{:S(2)}) collective-permute-start(f32[2,4,64,128]{3,2,1,0:T(8,128)} %get-tuple-element.34.refs_2_), channel_id=1, source_target_pairs={{0,4},{1,5},{2,6},{3,7},{4,0},{5,1},{6,2},{7,3},{8,12},{9,13},{10,... | collective-permute-start | bytes 786440 | tf_op jit(solution)/shard_map/ppermute | solution.py:96
  49.9 4.7 %copy-start.3 = (s32[64,4]{0,1:T(4,128)S(1)}, s32[64,4]{0,1:T(4,128)}, u32[]{:S(2)}) copy-start(s32[64,4]{0,1:T(4,128)} %param.5) | copy-start | bytes 3076
  49.9 11.8 %collective-permute-start.11 = (f32[2,4,64,128]{3,2,1,0:T(8,128)S(1)}, f32[2,4,64,128]{3,2,1,0:T(8,128)}, u32[]{:S(2)}, u32[]{:S(2)}) collective-permute-start(f32[2,4,64,128]{3,2,1,0:T(8,128)S(1)} %pack.18.refs_2_), channel_id=1, source_target_pairs={{0,4},{1,5},{2,6},{3,7},{4,0},{5,1},{6,2},{7,3},{8,12},{9,13},{10,... | collective-permute-start | bytes 786440 | tf_op jit(solution)/shard_map/ppermute | solution.py:96
  50.0 1.0 copy-start.1
  51.0 11.9 %collective-permute-start.13 = (f32[2,4,64,128]{3,2,1,0:T(8,128)S(1)}, f32[2,4,64,128]{3,2,1,0:T(8,128)}, u32[]{:S(2)}, u32[]{:S(2)}) collective-permute-start(f32[2,4,64,128]{3,2,1,0:T(8,128)S(1)} %pack.19.refs_9_.refs_6_), channel_id=1, source_target_pairs={{0,4},{1,5},{2,6},{3,7},{4,0},{5,1},{6,2},{7,3},{8,12},{9,13},{10,... | collective-permute-start | bytes 786440 | tf_op jit(solution)/shard_map/ppermute | solution.py:96
  56.5 6.4 %copy-start.2 = (f32[2,4,64,128]{3,2,1,0:T(8,128)S(1)}, f32[2,4,64,128]{3,2,1,0:T(8,128)}, u32[]{:S(2)}) copy-start(f32[2,4,64,128]{3,2,1,0:T(8,128)} %copy-done.1) | copy-start | bytes 786436
  67.2 9.0 %collective-permute-start.15 = (f32[4,5,3,8,128]{4,3,2,1,0:T(8,128)S(1)}, f32[4,5,3,8,128]{4,3,2,1,0:T(8,128)S(1)}, u32[]{:S(2)}, u32[]{:S(2)}) collective-permute-start(f32[4,5,3,8,128]{4,3,2,1,0:T(8,128)S(1)} %get-tuple-element.40), channel_id=1, source_target_pairs={{0,1},{1,2},{2,3},{3,4},{4,5},{5,6},{6,7},{7,0},{8,9},{9,10},{10,1... | collective-permute-start | bytes 737288 | tf_op jit(solution)/shard_map/ppermute | solution.py:605
  68.0 9.4 %collective-permute-start.16 = (f32[4,5,3,8,128]{4,3,2,1,0:T(8,128)S(1)}, f32[4,5,3,8,128]{4,3,2,1,0:T(8,128)S(1)}, u32[]{:S(2)}, u32[]{:S(2)}) collective-permute-start(f32[4,5,3,8,128]{4,3,2,1,0:T(8,128)S(1)} %get-tuple-element.41), channel_id=1, source_target_pairs={{1,0},{2,1},{3,2},{4,3},{5,4},{6,5},{7,6},{0,7},{9,8},{10,9},{11,1... | collective-permute-start | bytes 737288 | tf_op jit(solution)/shard_map/ppermute | solution.py:606
  71.4 34.3 %all-to-all-start = ((f32[16,2,120,128]{3,2,1,0:T(8,128)}), f32[16,2,120,128]{3,2,1,0:T(8,128)}, u32[]{:S(2)}, u32[]{:S(2)}) async-start(f32[16,2,120,128]{3,2,1,0:T(8,128)} %get-tuple-element.44), calls=%async_computation | async-start | bytes 3932160 | tf_op jit(solution)/shard_map/all_to_all | solution.py:601

commit v5 on v4

--- a/solution.py
+++ b/solution.py
@@ -104,8 +104,8 @@
     ([(1, 1)], []),
     ([(1, 2), (2, 0)], []),
     ([(1, 3), (2, 1)], []),
-    ([(1, 4), (2, 2)], [(2, 0)]),
-    ([(2, 3)], [(2, 1)]),
+    ([(1, 4), (2, 2)], []),
+    ([(2, 3)], [(2, 0)]),
     ([(2, 4)], [(2, 1)]),
 )
 

time: 114 us -> 114 us (level)
  starting transfers between devices: 47 us -> 43.4 us
  Pallas kernels: 48.9 us -> 51.7 us
    ppermute x1, waiting for transfers between devices: 1.11 us -> 6.96 us  [local(): z_above = lax.ppermute(z_first, 'gz', down)]
    all_to_all x1, waiting for transfers between devices: 11.6 us -> 5.76 us  [local(): arrived = lax.all_to_all(send, ('gx', 'gy'), 0, 0, tiled=True)]
    ppermute x15, starting transfers between devices: 37.9 us -> 34.3 us  [swapped(): lax.ppermute(block, axis, [(i, i ^ count // 2) for i in range(count)])]
    pallas_call x10, Pallas kernels: 15.3 us -> 18.1 us  [pack(): pl.pallas_call(functools.partial(pack_kernel, sends, len(received)), out_...]
  transfers between devices with their start and end apart: 18 -> 18, of which waited for: 5 -> 6; matrix products, arithmetic and copies ran while one was open for 0% -> 0% of each run, Pallas kernels for 32% -> 34%
where the time goes in v5:
time: 114 us; the launch traced here: 113 us
  Pallas kernels  51.7 us (45%)
  starting transfers between devices  43.4 us (38%)
  waiting for transfers between devices  16.7 us (15%)
  local copies, waits for them, and re-layouts  1.2 us (1%)
    ppermute x15, starting transfers between devices, swapped(): lax.ppermute(block, axis, [(i, i ^ count // 2) for i in range(count)])  34.3 us
    pallas_call x10, Pallas kernels, pack(): pl.pallas_call(functools.partial(pack_kernel, sends, len(received)), out_...  18.1 us
    pallas_call x1, Pallas kernels, inner(): pl.pallas_call(inner_kernel, out_shape=[pltpu.HBM(PATCH_SHAPE, F32), pltp...  16.7 us
    pallas_call x2, Pallas kernels, faces(): pl.pallas_call(functools.partial(faces_kernel, fields), out_shape=[pltpu....  9.5 us
    pallas_call x1, Pallas kernels, outer(): pl.pallas_call(outer_kernel, out_shape=jax.ShapeDtypeStruct((SLOTS, FIELD...  7.35 us
    ppermute x1, waiting for transfers between devices, local(): z_above = lax.ppermute(z_first, 'gz', down)  6.96 us
    all_to_all x1, waiting for transfers between devices, local(): arrived = lax.all_to_all(send, ('gx', 'gy'), 0, 0, tiled=True)  5.76 us
    all_to_all x1, starting transfers between devices, local(): arrived = lax.all_to_all(send, ('gx', 'gy'), 0, 0, tiled=True)  4.86 us
  transfers between devices with their start and end apart: 18, of which 6 were waited for; matrix products, arithmetic and copies ran while one was open for 0% of the time, Pallas kernels for 34%

profile of v5, /device:TPU:0, one launch (start us, length us, event | category | flops | bytes accessed | tf_op | source)
XLA Modules:
  0.0 113.2 jit_solution(10269042700130294994)
XLA Ops:
  0.0 0.7 copy-done
  0.7 0.2 dynamic-slice_reduce_fusion
  0.9 0.1 reshape_squeeze.3.plan
  1.0 1.5 %pack.10.refs_0_ = f32[2,4,64,128]{3,2,1,0:T(8,128)S(1)} custom-call(s32[6]{0:T(128)S(1)} %reshape_squeeze.3.plan, f32[4,20,64,128]{3,2,1,0:T(8,128)} %bitcast.11), custom_call_target="tpu_custom_call" | custom-call | tf_op jit(solution)/shard_map/pack/pallas_call | solution.py:83
  2.5 4.0 %collective-permute-start.2 = (f32[2,4,64,128]{3,2,1,0:T(8,128)S(1)}, f32[2,4,64,128]{3,2,1,0:T(8,128)S(1)}, u32[]{:S(2)}, u32[]{:S(2)}) collective-permute-start(f32[2,4,64,128]{3,2,1,0:T(8,128)S(1)} %pack.10.refs_0_), channel_id=1, source_target_pairs={{0,64},{32,96},{64,0},{96,32},{1,65},{33,97},{65,1},{97,33},{2,66}... | collective-permute-start | bytes 786440 | tf_op jit(solution)/shard_map/ppermute | solution.py:96
  6.6 1.7 %pack.11 = (f32[2,4,64,128]{3,2,1,0:T(8,128)S(1)}, f32[2,4,64,128]{3,2,1,0:T(8,128)S(1)}) custom-call(s32[6]{0:T(128)S(1)} %reshape_squeeze.3.plan, f32[4,20,64,128]{3,2,1,0:T(8,128)} %bitcast.12, f32[2,4,64,128]{3,2,1,0:T(8,128)S(1)} %pack.10.refs_0_), custom_call_target="tpu_custom_call" | custom-call | tf_op jit(solution)/shard_map/pack/pallas_call | solution.py:83
  8.2 0.1 collective-permute-start.1
  8.3 3.5 %collective-permute-start.4 = (f32[2,4,64,128]{3,2,1,0:T(8,128)S(1)}, f32[2,4,64,128]{3,2,1,0:T(8,128)S(1)}, u32[]{:S(2)}, u32[]{:S(2)}) collective-permute-start(f32[2,4,64,128]{3,2,1,0:T(8,128)S(1)} %get-tuple-element.26.refs_0_), channel_id=1, source_target_pairs={{0,64},{32,96},{64,0},{96,32},{1,65},{33,97},{65,1},{97,33},{2,66}... | collective-permute-start | bytes 786440 | tf_op jit(solution)/shard_map/ppermute | solution.py:96
  11.9 1.7 %pack.12 = (f32[2,4,64,128]{3,2,1,0:T(8,128)S(1)}, f32[2,4,64,128]{3,2,1,0:T(8,128)S(1)}) custom-call(s32[6]{0:T(128)S(1)} %reshape_squeeze.3.plan, f32[4,20,64,128]{3,2,1,0:T(8,128)} %bitcast.13, f32[2,4,64,128]{3,2,1,0:T(8,128)S(1)} %get-tuple-element.26.refs_0_), custom_call_target="tpu_custom_call" | custom-call | tf_op jit(solution)/shard_map/pack/pallas_call | solution.py:83
  13.5 0.2 collective-permute-done.2.refs_0_.refs_1_
  13.7 1.7 %pack.13.refs_1_ = f32[2,4,64,128]{3,2,1,0:T(8,128)S(1)} custom-call(s32[6]{0:T(128)S(1)} %reshape_squeeze.3.plan, f32[4,20,64,128]{3,2,1,0:T(8,128)} %bitcast.14, f32[2,4,64,128]{3,2,1,0:T(8,128)S(1)} %collective-permute-done.2.refs_0_.refs_1_, f32[2,4,64,128]{3,2,1,0:T(8,128)S(1)} %get-tuple-element.29.refs_1_), custom_call_target="tpu_custom_call" | custom-call | tf_op jit(solution)/shard_map/pack/pallas_call | solution.py:83
  15.4 3.3 %collective-permute-start.5 = (f32[2,4,64,128]{3,2,1,0:T(8,128)S(1)}, f32[2,4,64,128]{3,2,1,0:T(8,128)S(1)}, u32[]{:S(2)}, u32[]{:S(2)}) collective-permute-start(f32[2,4,64,128]{3,2,1,0:T(8,128)S(1)} %pack.13.refs_1_), channel_id=1, source_target_pairs={{0,16},{8,24},{16,0},{24,8},{1,17},{9,25},{17,1},{25,9},{2,18},{10... | collective-permute-start | bytes 786440 | tf_op jit(solution)/shard_map/ppermute | solution.py:96
  18.7 3.4 %collective-permute-start = (f32[2,4,64,128]{3,2,1,0:T(8,128)S(1)}, f32[2,4,64,128]{3,2,1,0:T(8,128)S(1)}, u32[]{:S(2)}, u32[]{:S(2)}) collective-permute-start(f32[2,4,64,128]{3,2,1,0:T(8,128)S(1)} %get-tuple-element.27), channel_id=1, source_target_pairs={{0,64},{32,96},{64,0},{96,32},{1,65},{33,97},{65,1},{97,33},{2,66}... | collective-permute-start | bytes 786440 | tf_op jit(solution)/shard_map/ppermute | solution.py:96
  22.1 0.0 collective-permute-done.1.refs_0_.refs_1_.refs_3_
  22.1 1.7 %pack.14.refs_3_ = f32[2,4,64,128]{3,2,1,0:T(8,128)S(1)} custom-call(s32[6]{0:T(128)S(1)} %reshape_squeeze.3.plan, f32[4,20,64,128]{3,2,1,0:T(8,128)} %bitcast.15, f32[2,4,64,128]{3,2,1,0:T(8,128)S(1)} %collective-permute-done.1.refs_0_.refs_1_.refs_3_, f32[2,4,64,128]{3,2,1,0:T(8,128)S(1)} %pack.13.refs_1_), custom_call_target="tpu_custom_call" | custom-call | tf_op jit(solution)/shard_map/pack/pallas_call | solution.py:83
  23.8 0.5 collective-permute-start.3
  24.3 3.4 %collective-permute-start.7 = (f32[2,4,64,128]{3,2,1,0:T(8,128)S(1)}, f32[2,4,64,128]{3,2,1,0:T(8,128)S(1)}, u32[]{:S(2)}, u32[]{:S(2)}) collective-permute-start(f32[2,4,64,128]{3,2,1,0:T(8,128)S(1)} %get-tuple-element.29.refs_1_), channel_id=1, source_target_pairs={{0,64},{32,96},{64,0},{96,32},{1,65},{33,97},{65,1},{97,33},{2,66}... | collective-permute-start | bytes 786440 | tf_op jit(solution)/shard_map/ppermute | solution.py:96
  27.7 0.0 collective-permute-done.4.refs_0_.refs_1_.refs_6_
  27.7 0.0 collective-permute-done.5.refs_2_.refs_1_
  27.7 1.9 %pack.15 = (f32[2,4,64,128]{3,2,1,0:T(8,128)S(1)}, f32[2,4,64,128]{3,2,1,0:T(8,128)S(1)}) custom-call(s32[6]{0:T(128)S(1)} %reshape_squeeze.3.plan, f32[4,20,64,128]{3,2,1,0:T(8,128)} %bitcast.16, f32[2,4,64,128]{3,2,1,0:T(8,128)S(1)} %collective-permute-done.4.refs_0_.refs_1_.refs_6_, f32[2,4,64,128]{3,2,1,0:T(8,128)S(1)} %collective-permute-done.2.refs_0_.refs_1_, ...), custom_call_target="tpu_custom_call" | custom-call | tf_op jit(solution)/shard_map/pack/pallas_call | solution.py:83
  29.7 0.5 collective-permute-start.8
  30.2 2.9 %collective-permute-start.9 = (f32[2,4,64,128]{3,2,1,0:T(8,128)S(1)}, f32[2,4,64,128]{3,2,1,0:T(8,128)S(1)}, u32[]{:S(2)}, u32[]{:S(2)}) collective-permute-start(f32[2,4,64,128]{3,2,1,0:T(8,128)S(1)} %get-tuple-element.30.refs_3_), channel_id=1, source_target_pairs={{0,4},{1,5},{2,6},{3,7},{4,0},{5,1},{6,2},{7,3},{8,12},{9,13},{10,... | collective-permute-start | bytes 786440 | tf_op jit(solution)/shard_map/ppermute | solution.py:96
  33.0 1.9 %pack.16 = (f32[2,4,64,128]{3,2,1,0:T(8,128)S(1)}, f32[2,4,64,128]{3,2,1,0:T(8,128)S(1)}) custom-call(s32[6]{0:T(128)S(1)} %reshape_squeeze.3.plan, f32[4,20,64,128]{3,2,1,0:T(8,128)} %bitcast.17, f32[2,4,64,128]{3,2,1,0:T(8,128)S(1)} %collective-permute-done.refs_0_, f32[2,4,64,128]{3,2,1,0:T(8,128)S(1)} %collective-permute-done.1.refs_0_.refs_1_.refs_3_, ...), custom_call_target="tpu_custom_call" | custom-call | tf_op jit(solution)/shard_map/pack/pallas_call | solution.py:83
  35.0 3.1 %collective-permute-start.6 = (f32[2,4,64,128]{3,2,1,0:T(8,128)S(1)}, f32[2,4,64,128]{3,2,1,0:T(8,128)S(1)}, u32[]{:S(2)}, u32[]{:S(2)}) collective-permute-start(f32[2,4,64,128]{3,2,1,0:T(8,128)S(1)} %get-tuple-element.31), channel_id=1, source_target_pairs={{0,16},{8,24},{16,0},{24,8},{1,17},{9,25},{17,1},{25,9},{2,18},{10... | collective-permute-start | bytes 786440 | tf_op jit(solution)/shard_map/ppermute | solution.py:96
  38.1 0.6 collective-permute-start.12
  38.6 2.6 %pack.17 = (f32[2,4,64,128]{3,2,1,0:T(8,128)S(1)}, f32[2,4,64,128]{3,2,1,0:T(8,128)}) custom-call(s32[6]{0:T(128)S(1)} %reshape_squeeze.3.plan, f32[4,20,64,128]{3,2,1,0:T(8,128)} %bitcast.18, f32[2,4,64,128]{3,2,1,0:T(8,128)S(1)} %collective-permute-done.7.refs_0_.refs_3_, f32[2,4,64,128]{3,2,1,0:T(8,128)S(1)} %collective-permute-done.4.refs_0_.refs_1_.refs_6_, ...), custom_call_target="tpu_custom_call" | custom-call | tf_op jit(solution)/shard_map/pack/pallas_call | solution.py:83
  41.3 2.1 %collective-permute-start.11 = (f32[2,4,64,128]{3,2,1,0:T(8,128)S(1)}, f32[2,4,64,128]{3,2,1,0:T(8,128)S(1)}, u32[]{:S(2)}, u32[]{:S(2)}) collective-permute-start(f32[2,4,64,128]{3,2,1,0:T(8,128)S(1)} %get-tuple-element.35), channel_id=1, source_target_pairs={{0,16},{8,24},{16,0},{24,8},{1,17},{9,25},{17,1},{25,9},{2,18},{10... | collective-permute-start | bytes 786440 | tf_op jit(solution)/shard_map/ppermute | solution.py:96
  43.4 2.0 %collective-permute-start.14 = (f32[2,4,64,128]{3,2,1,0:T(8,128)}, f32[2,4,64,128]{3,2,1,0:T(8,128)}, u32[]{:S(2)}, u32[]{:S(2)}) collective-permute-start(f32[2,4,64,128]{3,2,1,0:T(8,128)} %get-tuple-element.34.refs_2_), channel_id=1, source_target_pairs={{0,4},{1,5},{2,6},{3,7},{4,0},{5,1},{6,2},{7,3},{8,12},{9,13},{10,... | collective-permute-start | bytes 786440 | tf_op jit(solution)/shard_map/ppermute | solution.py:96
  45.3 1.7 %pack.18.refs_2_ = f32[2,4,64,128]{3,2,1,0:T(8,128)S(1)} custom-call(s32[6]{0:T(128)S(1)} %reshape_squeeze.3.plan, f32[4,20,64,128]{3,2,1,0:T(8,128)} %bitcast.19, f32[2,4,64,128]{3,2,1,0:T(8,128)S(1)} %collective-permute-done.refs_0_, f32[2,4,64,128]{3,2,1,0:T(8,128)S(1)} %collective-permute-done.6.refs_1_, f32[2,4,64,128]{3,2,1,0:T(8,128)} %get-tuple-element.34.refs_2_, ...), custom_call_target="tpu_custom_call" | custom-call | tf_op jit(solution)/shard_map/pack/pallas_call | solution.py:83
  47.1 0.0 copy-start.3
  47.1 1.7 %collective-permute-start.10 = (f32[2,4,64,128]{3,2,1,0:T(8,128)S(1)}, f32[2,4,64,128]{3,2,1,0:T(8,128)}, u32[]{:S(2)}, u32[]{:S(2)}) collective-permute-start(f32[2,4,64,128]{3,2,1,0:T(8,128)S(1)} %pack.18.refs_2_), channel_id=1, source_target_pairs={{0,4},{1,5},{2,6},{3,7},{4,0},{5,1},{6,2},{7,3},{8,12},{9,13},{10,... | collective-permute-start | bytes 786440 | tf_op jit(solution)/shard_map/ppermute | solution.py:96
  48.8 0.5 collective-permute-done.11.refs_1_.refs_4_
  49.3 1.7 %pack.19.refs_9_.refs_6_ = f32[2,4,64,128]{3,2,1,0:T(8,128)S(1)} custom-call(s32[6]{0:T(128)S(1)} %reshape_squeeze.3.plan, f32[4,20,64,128]{3,2,1,0:T(8,128)} %bitcast.20, f32[2,4,64,128]{3,2,1,0:T(8,128)S(1)} %collective-permute-done.7.refs_0_.refs_3_, f32[2,4,64,128]{3,2,1,0:T(8,128)S(1)} %collective-permute-done.11.refs_1_.refs_4_, ...), custom_call_target="tpu_custom_call" | custom-call | tf_op jit(solution)/shard_map/pack/pallas_call | solution.py:83
  51.0 3.2 %collective-permute-start.13 = (f32[2,4,64,128]{3,2,1,0:T(8,128)S(1)}, f32[2,4,64,128]{3,2,1,0:T(8,128)}, u32[]{:S(2)}, u32[]{:S(2)}) collective-permute-start(f32[2,4,64,128]{3,2,1,0:T(8,128)S(1)} %pack.19.refs_9_.refs_6_), channel_id=1, source_target_pairs={{0,4},{1,5},{2,6},{3,7},{4,0},{5,1},{6,2},{7,3},{8,12},{9,13},{10,... | collective-permute-start | bytes 786440 | tf_op jit(solution)/shard_map/ppermute | solution.py:96
  54.2 0.1 copy.7
  54.3 0.1 reshape.19.links
  54.4 0.0 collective-permute-done.14.refs_8_
  54.4 5.2 %faces.2 = (f32[5,4,4,64,128]{4,3,2,1,0:T(8,128)}, f32[16,2,120,128]{3,2,1,0:T(8,128)}, f32[16,120,128]{2,1,0:T(8,128)}) custom-call(s32[6]{0:T(128)S(1)} %reshape_squeeze.3.plan, s32[1]{0:T(128)} %bitcast.place, s32[256]{0:T(256)S(1)} %reshape.19.links, f32[4,20,64,128]{3,2,1,0:T(8,128)} %bitcast.21, ...), custom_call_target="tpu_custom_call" | custom-call | tf_op jit(solution)/shard_map/faces/pallas_call | solution.py:297
  59.6 0.4 collective-permute-done.10.refs_2_
  60.0 2.9 %collective-permute-done.13.refs_5_ = f32[2,4,64,128]{3,2,1,0:T(8,128)} collective-permute-done((f32[2,4,64,128]{3,2,1,0:T(8,128)S(1)}, f32[2,4,64,128]{3,2,1,0:T(8,128)}, u32[]{:S(2)}, u32[]{:S(2)}) %collective-permute-start.13) | collective-permute-done | bytes 262176 | tf_op jit(solution)/shard_map/ppermute | solution.py:96
  62.9 4.3 %faces.3 = (f32[5,4,4,64,128]{4,3,2,1,0:T(8,128)}, f32[16,2,120,128]{3,2,1,0:T(8,128)}, f32[16,120,128]{2,1,0:T(8,128)}, f32[4,5,3,8,128]{4,3,2,1,0:T(8,128)S(1)}, f32[4,5,3,8,128]{4,3,2,1,0:T(8,128)S(1)}) custom-call(s32[6]{0:T(128)S(1)} %reshape_squeeze.3.plan, s32[1]{0:T(128)} %bitcast.place, ...), custom_call_target="tpu_custom_call", output_to_operand_aliasing={{0}: (11, {}), {1}: (12, {}), {2}: (13, {})} | custom-call | flops 999999995904 | bytes 10000000000 | tf_op jit(solution)/shard_map/faces/pallas_call | solution.py:297
  67.2 0.4 collective-permute-start.15
  67.6 3.8 %collective-permute-start.16 = (f32[4,5,3,8,128]{4,3,2,1,0:T(8,128)S(1)}, f32[4,5,3,8,128]{4,3,2,1,0:T(8,128)S(1)}, u32[]{:S(2)}, u32[]{:S(2)}) collective-permute-start(f32[4,5,3,8,128]{4,3,2,1,0:T(8,128)S(1)} %get-tuple-element.41), channel_id=1, source_target_pairs={{1,0},{2,1},{3,2},{4,3},{5,4},{6,5},{7,6},{0,7},{9,8},{10,9},{11,1... | collective-permute-start | bytes 737288 | tf_op jit(solution)/shard_map/ppermute | solution.py:606
  71.4 4.9 %all-to-all-start = ((f32[16,2,120,128]{3,2,1,0:T(8,128)}), f32[16,2,120,128]{3,2,1,0:T(8,128)}, u32[]{:S(2)}, u32[]{:S(2)}) async-start(f32[16,2,120,128]{3,2,1,0:T(8,128)} %get-tuple-element.44), calls=%async_computation | async-start | bytes 3932160 | tf_op jit(solution)/shard_map/all_to_all | solution.py:601
  76.3 7.0 %collective-permute-done.16.z_above = f32[4,5,3,8,128]{4,3,2,1,0:T(8,128)S(1)} collective-permute-done((f32[4,5,3,8,128]{4,3,2,1,0:T(8,128)S(1)}, f32[4,5,3,8,128]{4,3,2,1,0:T(8,128)S(1)}, u32[]{:S(2)}, u32[]{:S(2)}) %collective-permute-start.16) | collective-permute-done | bytes 245792 | tf_op jit(solution)/shard_map/ppermute | solution.py:606
  83.3 16.7 %inner.1 = (f32[5,4,4,64,128]{4,3,2,1,0:T(8,128)}, f32[2,2,5,5,4,8,128]{6,5,4,3,2,1,0:T(8,128)}, s32[48]{0:T(128)S(1)}) custom-call(s32[1]{0:T(128)} %bitcast.place, s32[256]{0:T(256)S(1)} %reshape.19.links, f32[5,4,4,64,128]{4,3,2,1,0:T(8,128)} %get-tuple-element.39.patches_in, f32[4,5,3,8,128]{4,3,2,1,0:T(8,128)S(1)} %collective-permute-done.15.z_below, ...), custom_call_target="tpu_custom_call" | custom-call | flops 999999995904 | bytes 10000000000 | tf_op jit(solution)/shard_map/inner/pallas_call | solution.py:481
  100.0 5.8 %all-to-all-done.arrived = f32[16,2,120,128]{3,2,1,0:T(8,128)} async-done(((f32[16,2,120,128]{3,2,1,0:T(8,128)}), f32[16,2,120,128]{3,2,1,0:T(8,128)}, u32[]{:S(2)}, u32[]{:S(2)}) %all-to-all-start) | async-done | bytes 1966112 | tf_op jit(solution)/shard_map/all_to_all | solution.py:601
  105.7 7.4 %outer.1 = f32[4,5,4,64,128]{4,3,2,1,0:T(8,128)} custom-call(s32[1]{0:T(128)} %bitcast.place, s32[48]{0:T(128)S(1)} %get-tuple-element.42.table, f32[2,2,5,5,4,8,128]{6,5,4,3,2,1,0:T(8,128)} %get-tuple-element.43.rim_in, f32[16,2,120,128]{3,2,1,0:T(8,128)} %all-to-all-done.arrived, f32[16,120,128]{2,1,0:T(8,128)} %get-tuple-element.45.own_items, ...), custom_call_target="tpu_custom_call" | custom-call | tf_op jit(solution)/shard_map/outer/pallas_call | solution.py:566
  (14 shorter events, 0.0 us)
Async XLA Ops:
  0.0 0.7 copy-start
  2.5 11.2 %collective-permute-start.2 = (f32[2,4,64,128]{3,2,1,0:T(8,128)S(1)}, f32[2,4,64,128]{3,2,1,0:T(8,128)S(1)}, u32[]{:S(2)}, u32[]{:S(2)}) collective-permute-start(f32[2,4,64,128]{3,2,1,0:T(8,128)S(1)} %pack.10.refs_0_), channel_id=1, source_target_pairs={{0,64},{32,96},{64,0},{96,32},{1,65},{33,97},{65,1},{97,33},{2,66}... | collective-permute-start | bytes 786440 | tf_op jit(solution)/shard_map/ppermute | solution.py:96
  8.2 13.8 %collective-permute-start.1 = (f32[2,4,64,128]{3,2,1,0:T(8,128)S(1)}, f32[2,4,64,128]{3,2,1,0:T(8,128)S(1)}, u32[]{:S(2)}, u32[]{:S(2)}) collective-permute-start(f32[2,4,64,128]{3,2,1,0:T(8,128)S(1)} %get-tuple-element.28), channel_id=1, source_target_pairs={{0,64},{32,96},{64,0},{96,32},{1,65},{33,97},{65,1},{97,33},{2,66}... | collective-permute-start | bytes 786440 | tf_op jit(solution)/shard_map/ppermute | solution.py:96
  8.3 19.4 %collective-permute-start.4 = (f32[2,4,64,128]{3,2,1,0:T(8,128)S(1)}, f32[2,4,64,128]{3,2,1,0:T(8,128)S(1)}, u32[]{:S(2)}, u32[]{:S(2)}) collective-permute-start(f32[2,4,64,128]{3,2,1,0:T(8,128)S(1)} %get-tuple-element.26.refs_0_), channel_id=1, source_target_pairs={{0,64},{32,96},{64,0},{96,32},{1,65},{33,97},{65,1},{97,33},{2,66}... | collective-permute-start | bytes 786440 | tf_op jit(solution)/shard_map/ppermute | solution.py:96
  15.4 12.3 %collective-permute-start.5 = (f32[2,4,64,128]{3,2,1,0:T(8,128)S(1)}, f32[2,4,64,128]{3,2,1,0:T(8,128)S(1)}, u32[]{:S(2)}, u32[]{:S(2)}) collective-permute-start(f32[2,4,64,128]{3,2,1,0:T(8,128)S(1)} %pack.13.refs_1_), channel_id=1, source_target_pairs={{0,16},{8,24},{16,0},{24,8},{1,17},{9,25},{17,1},{25,9},{2,18},{10... | collective-permute-start | bytes 786440 | tf_op jit(solution)/shard_map/ppermute | solution.py:96
  18.7 14.4 %collective-permute-start = (f32[2,4,64,128]{3,2,1,0:T(8,128)S(1)}, f32[2,4,64,128]{3,2,1,0:T(8,128)S(1)}, u32[]{:S(2)}, u32[]{:S(2)}) collective-permute-start(f32[2,4,64,128]{3,2,1,0:T(8,128)S(1)} %get-tuple-element.27), channel_id=1, source_target_pairs={{0,64},{32,96},{64,0},{96,32},{1,65},{33,97},{65,1},{97,33},{2,66}... | collective-permute-start | bytes 786440 | tf_op jit(solution)/shard_map/ppermute | solution.py:96
  23.8 9.3 %collective-permute-start.3 = (f32[2,4,64,128]{3,2,1,0:T(8,128)S(1)}, f32[2,4,64,128]{3,2,1,0:T(8,128)S(1)}, u32[]{:S(2)}, u32[]{:S(2)}) collective-permute-start(f32[2,4,64,128]{3,2,1,0:T(8,128)S(1)} %pack.14.refs_3_), channel_id=1, source_target_pairs={{0,16},{8,24},{16,0},{24,8},{1,17},{9,25},{17,1},{25,9},{2,18},{10... | collective-permute-start | bytes 786440 | tf_op jit(solution)/shard_map/ppermute | solution.py:96
  24.3 14.4 %collective-permute-start.7 = (f32[2,4,64,128]{3,2,1,0:T(8,128)S(1)}, f32[2,4,64,128]{3,2,1,0:T(8,128)S(1)}, u32[]{:S(2)}, u32[]{:S(2)}) collective-permute-start(f32[2,4,64,128]{3,2,1,0:T(8,128)S(1)} %get-tuple-element.29.refs_1_), channel_id=1, source_target_pairs={{0,64},{32,96},{64,0},{96,32},{1,65},{33,97},{65,1},{97,33},{2,66}... | collective-permute-start | bytes 786440 | tf_op jit(solution)/shard_map/ppermute | solution.py:96
  29.7 9.0 %collective-permute-start.8 = (f32[2,4,64,128]{3,2,1,0:T(8,128)S(1)}, f32[2,4,64,128]{3,2,1,0:T(8,128)S(1)}, u32[]{:S(2)}, u32[]{:S(2)}) collective-permute-start(f32[2,4,64,128]{3,2,1,0:T(8,128)S(1)} %get-tuple-element.32), channel_id=1, source_target_pairs={{0,16},{8,24},{16,0},{24,8},{1,17},{9,25},{17,1},{25,9},{2,18},{10... | collective-permute-start | bytes 786440 | tf_op jit(solution)/shard_map/ppermute | solution.py:96
  30.2 15.2 %collective-permute-start.9 = (f32[2,4,64,128]{3,2,1,0:T(8,128)S(1)}, f32[2,4,64,128]{3,2,1,0:T(8,128)S(1)}, u32[]{:S(2)}, u32[]{:S(2)}) collective-permute-start(f32[2,4,64,128]{3,2,1,0:T(8,128)S(1)} %get-tuple-element.30.refs_3_), channel_id=1, source_target_pairs={{0,4},{1,5},{2,6},{3,7},{4,0},{5,1},{6,2},{7,3},{8,12},{9,13},{10,... | collective-permute-start | bytes 786440 | tf_op jit(solution)/shard_map/ppermute | solution.py:96
  35.0 10.4 %collective-permute-start.6 = (f32[2,4,64,128]{3,2,1,0:T(8,128)S(1)}, f32[2,4,64,128]{3,2,1,0:T(8,128)S(1)}, u32[]{:S(2)}, u32[]{:S(2)}) collective-permute-start(f32[2,4,64,128]{3,2,1,0:T(8,128)S(1)} %get-tuple-element.31), channel_id=1, source_target_pairs={{0,16},{8,24},{16,0},{24,8},{1,17},{9,25},{17,1},{25,9},{2,18},{10... | collective-permute-start | bytes 786440 | tf_op jit(solution)/shard_map/ppermute | solution.py:96
  38.1 10.7 %collective-permute-start.12 = (f32[2,4,64,128]{3,2,1,0:T(8,128)S(1)}, f32[2,4,64,128]{3,2,1,0:T(8,128)S(1)}, u32[]{:S(2)}, u32[]{:S(2)}) collective-permute-start(f32[2,4,64,128]{3,2,1,0:T(8,128)S(1)} %get-tuple-element.33.refs_3_), channel_id=1, source_target_pairs={{0,4},{1,5},{2,6},{3,7},{4,0},{5,1},{6,2},{7,3},{8,12},{9,13},{10,... | collective-permute-start | bytes 786440 | tf_op jit(solution)/shard_map/ppermute | solution.py:96
  41.3 8.0 %collective-permute-start.11 = (f32[2,4,64,128]{3,2,1,0:T(8,128)S(1)}, f32[2,4,64,128]{3,2,1,0:T(8,128)S(1)}, u32[]{:S(2)}, u32[]{:S(2)}) collective-permute-start(f32[2,4,64,128]{3,2,1,0:T(8,128)S(1)} %get-tuple-element.35), channel_id=1, source_target_pairs={{0,16},{8,24},{16,0},{24,8},{1,17},{9,25},{17,1},{25,9},{2,18},{10... | collective-permute-start | bytes 786440 | tf_op jit(solution)/shard_map/ppermute | solution.py:96
  43.4 11.1 %collective-permute-start.14 = (f32[2,4,64,128]{3,2,1,0:T(8,128)}, f32[2,4,64,128]{3,2,1,0:T(8,128)}, u32[]{:S(2)}, u32[]{:S(2)}) collective-permute-start(f32[2,4,64,128]{3,2,1,0:T(8,128)} %get-tuple-element.34.refs_2_), channel_id=1, source_target_pairs={{0,4},{1,5},{2,6},{3,7},{4,0},{5,1},{6,2},{7,3},{8,12},{9,13},{10,... | collective-permute-start | bytes 786440 | tf_op jit(solution)/shard_map/ppermute | solution.py:96
  47.1 7.1 %copy-start.3 = (s32[64,4]{0,1:T(4,128)S(1)}, s32[64,4]{0,1:T(4,128)}, u32[]{:S(2)}) copy-start(s32[64,4]{0,1:T(4,128)} %param.5) | copy-start | bytes 3076
  47.1 13.0 %collective-permute-start.10 = (f32[2,4,64,128]{3,2,1,0:T(8,128)S(1)}, f32[2,4,64,128]{3,2,1,0:T(8,128)}, u32[]{:S(2)}, u32[]{:S(2)}) collective-permute-start(f32[2,4,64,128]{3,2,1,0:T(8,128)S(1)} %pack.18.refs_2_), channel_id=1, source_target_pairs={{0,4},{1,5},{2,6},{3,7},{4,0},{5,1},{6,2},{7,3},{8,12},{9,13},{10,... | collective-permute-start | bytes 786440 | tf_op jit(solution)/shard_map/ppermute | solution.py:96
  49.2 1.7 %copy-start.1 = (f32[2,4,64,128]{3,2,1,0:T(8,128)}, f32[2,4,64,128]{3,2,1,0:T(8,128)S(1)}, u32[]{:S(2)}) copy-start(f32[2,4,64,128]{3,2,1,0:T(8,128)S(1)} %collective-permute-done.11.refs_1_.refs_4_) | copy-start | bytes 786436
  51.0 11.9 %collective-permute-start.13 = (f32[2,4,64,128]{3,2,1,0:T(8,128)S(1)}, f32[2,4,64,128]{3,2,1,0:T(8,128)}, u32[]{:S(2)}, u32[]{:S(2)}) collective-permute-start(f32[2,4,64,128]{3,2,1,0:T(8,128)S(1)} %pack.19.refs_9_.refs_6_), channel_id=1, source_target_pairs={{0,4},{1,5},{2,6},{3,7},{4,0},{5,1},{6,2},{7,3},{8,12},{9,13},{10,... | collective-permute-start | bytes 786440 | tf_op jit(solution)/shard_map/ppermute | solution.py:96
  54.4 8.5 %copy-start.2 = (f32[2,4,64,128]{3,2,1,0:T(8,128)S(1)}, f32[2,4,64,128]{3,2,1,0:T(8,128)}, u32[]{:S(2)}) copy-start(f32[2,4,64,128]{3,2,1,0:T(8,128)} %copy-done.1) | copy-start | bytes 786436
  67.2 9.1 %collective-permute-start.15 = (f32[4,5,3,8,128]{4,3,2,1,0:T(8,128)S(1)}, f32[4,5,3,8,128]{4,3,2,1,0:T(8,128)S(1)}, u32[]{:S(2)}, u32[]{:S(2)}) collective-permute-start(f32[4,5,3,8,128]{4,3,2,1,0:T(8,128)S(1)} %get-tuple-element.40), channel_id=1, source_target_pairs={{0,1},{1,2},{2,3},{3,4},{4,5},{5,6},{6,7},{7,0},{8,9},{9,10},{10,1... | collective-permute-start | bytes 737288 | tf_op jit(solution)/shard_map/ppermute | solution.py:605
  67.6 15.6 %collective-permute-start.16 = (f32[4,5,3,8,128]{4,3,2,1,0:T(8,128)S(1)}, f32[4,5,3,8,128]{4,3,2,1,0:T(8,128)S(1)}, u32[]{:S(2)}, u32[]{:S(2)}) collective-permute-start(f32[4,5,3,8,128]{4,3,2,1,0:T(8,128)S(1)} %get-tuple-element.41), channel_id=1, source_target_pairs={{1,0},{2,1},{3,2},{4,3},{5,4},{6,5},{7,6},{0,7},{9,8},{10,9},{11,1... | collective-permute-start | bytes 737288 | tf_op jit(solution)/shard_map/ppermute | solution.py:606
  71.4 34.3 %all-to-all-start = ((f32[16,2,120,128]{3,2,1,0:T(8,128)}), f32[16,2,120,128]{3,2,1,0:T(8,128)}, u32[]{:S(2)}, u32[]{:S(2)}) async-start(f32[16,2,120,128]{3,2,1,0:T(8,128)} %get-tuple-element.44), calls=%async_computation | async-start | bytes 3932160 | tf_op jit(solution)/shard_map/all_to_all | solution.py:601
